TPU v7x, 32 devices: a whole 2x2x4 slice. The times are simulated.
32 devices in a mesh: dp: 16 (over z, x, core), mp: 2 (over y).
Axes of the slice: x: 2, y: 2, z: 4, core: 2. Of those that a mesh axis runs over, the one named last changes fastest.
Arguments:
- hidden_in: bfloat16 [128, 64, 768], P('dp'), may hold values from -6 to 6
- image_feats: bfloat16 [128, 257, 1408], P('dp'), may hold values from -6 to 6
- caption_lengths: int32 [128, 3], P('dp'), may hold values from 1 to 16, 32 in all within a row
- pair_image: int32 [384], P('dp'), may hold values from 0 to 127, as said below
- out_grad: bfloat16 [128, 64, 768], P('dp'), may hold values from -6 to 6
- self_qkv: bfloat16 [3, 768, 768], P(None, 'dp', 'mp'), may hold values from -0.21875 to 0.21875
- self_out: bfloat16 [768, 768], P('mp', 'dp'), may hold values from -0.625 to 0.625
- cross_query: bfloat16 [768, 768], P('dp', 'mp'), may hold values from -0.21875 to 0.21875
- cross_kv: bfloat16 [2, 1408, 768], P(None, 'dp', 'mp'), may hold values from -0.15625 to 0.15625
- cross_out: bfloat16 [768, 768], P('mp', 'dp'), may hold values from -0.875 to 0.875
- up_weight: bfloat16 [768, 3072], P('dp', 'mp'), may hold values from -0.21875 to 0.21875
- down_weight: bfloat16 [3072, 768], P('mp', 'dp'), may hold values from -0.15625 to 0.15625
- vision_proj: bfloat16 [768, 256], P('dp'), may hold values from -0.21875 to 0.21875
- text_proj: bfloat16 [768, 256], P('dp'), may hold values from -0.21875 to 0.21875
- norm_gain: bfloat16 [3, 768], P(None, 'dp'), may hold values from 0.5 to 1.5
- norm_bias: bfloat16 [3, 768], P(None, 'dp'), may hold values from -2.5 to 2.5
Outputs:
- contrast_loss: float32 [], replicated
- block_out: bfloat16 [128, 64, 768], P('dp')
- grad_hidden: bfloat16 [128, 64, 768], P('dp')
- grad_feats: bfloat16 [128, 257, 1408], P('dp')
- grad_self_qkv: float32 [3, 768, 768], P(None, 'dp', 'mp')
- grad_self_out: float32 [768, 768], P('mp', 'dp')
- grad_cross_query: float32 [768, 768], P('dp', 'mp')
- grad_cross_kv: float32 [2, 1408, 768], P(None, 'dp', 'mp')
- grad_cross_out: float32 [768, 768], P('mp', 'dp')
- grad_up_weight: float32 [768, 3072], P('dp', 'mp')
- grad_down_weight: float32 [3072, 768], P('mp', 'dp')
- grad_vision_proj: float32 [768, 256], P('dp')
- grad_text_proj: float32 [768, 256], P('dp')
- grad_norm_gain: float32 [3, 768], P(None, 'dp')
- grad_norm_bias: float32 [3, 768], P(None, 'dp')
Inputs may be any that keep to these rules, and one draw needn't show every extreme that they name: `caption_lengths`: in each item the 3 lengths sum to 32, and the largest is half of 32. `pair_image`: items 0 to 63 are each named by exactly one caption, the other items by exactly five.
All inputs are finite; a program needn't handle non-finite values.
Results may differ from a plain program's by a relative error of at most 0.02.
Values may be sent and summed in bfloat16 or wider, within the bound.
No kernel may reach another device: no remote copies, remote signals or barrier semaphores. Data moves between devices by JAX's collectives and lax.ppermute only.
A program may use at most 192 MiB of HBM per device.

v0:
```python
import jax
import jax.numpy as jnp
from jax import lax
from jax.sharding import PartitionSpec as P

HEAD_DIM = 64
NQ = 32


EPS_NORM = 1e-06
EPS_UNIT = 1e-06
SIM_SCALE = 16.0
MASKED = -1000000000.0
NEG_START = -1e30


def layer_norm(value, gain, shift):
    row_mean = jnp.mean(value, -1, keepdims=True)
    centered = value - row_mean
    row_var = jnp.mean(centered * centered, -1, keepdims=True)
    return centered * lax.rsqrt(row_var + EPS_NORM) * gain + shift


def unit_rows(value):
    return value * lax.rsqrt(jnp.sum(value * value, -1, keepdims=True) + EPS_UNIT)


def gelu_exact(value):
    return jax.nn.gelu(value, approximate=False)


def matmul(left, right):
    return jnp.dot(left, right, preferred_element_type=jnp.float32)


def times_rows(left, right):
    return lax.dot_general(
        left, right, (((1,), (1,)), ((), ())), preferred_element_type=jnp.float32
    )


def times_cols(left, right):
    return lax.dot_general(
        left, right, (((0,), (0,)), ((), ())), preferred_element_type=jnp.float32
    )


def half_sum(value):
    return lax.psum(value, "mp")


def segments(lengths, seq_len):
    bounds = NQ + jnp.cumsum(lengths, axis=1, dtype=jnp.int32)
    places = jnp.arange(seq_len, dtype=jnp.int32)
    labels = (places >= NQ).astype(jnp.int32)[None, :] + jnp.sum(
        (places[None, None, :] >= bounds[:, :-1, None]).astype(jnp.int32), axis=1
    )
    return (labels, bounds - lengths)


def attend_scores(queries_b, keys_b, allowed):
    scores = jnp.einsum(
        "gqhe,gkhe->ghqk", queries_b, keys_b, preferred_element_type=jnp.float32
    ) * HEAD_DIM ** (-0.5)
    if allowed is not None:
        scores = jnp.where(allowed[:, None], scores, MASKED)
    return scores


def attend_forward(queries_b, keys_b, values_b, allowed):
    scores = attend_scores(queries_b, keys_b, allowed)
    row_peak = jnp.max(scores, -1, keepdims=True)
    expo = jnp.exp(scores - row_peak)
    row_total = jnp.sum(expo, -1, keepdims=True)
    attn_probs = expo / row_total
    mixed_out = jnp.einsum(
        "ghqk,gkhe->gqhe",
        attn_probs.astype(jnp.bfloat16),
        values_b,
        preferred_element_type=jnp.float32,
    )
    return (mixed_out.astype(jnp.bfloat16), row_peak + jnp.log(row_total))


def attend_backward(queries_b, keys_b, values_b, allowed, row_lse, grad_mixed):
    scores = attend_scores(queries_b, keys_b, allowed)
    attn_probs = jnp.exp(scores - row_lse)
    grad_probs = jnp.einsum(
        "gqhe,gkhe->ghqk", grad_mixed, values_b, preferred_element_type=jnp.float32
    )
    grad_scores = attn_probs * (grad_probs - jnp.sum(grad_probs * attn_probs, -1, keepdims=True))
    grad_scores_b = grad_scores.astype(jnp.bfloat16)
    grad_queries = jnp.einsum(
        "ghqk,gkhe->gqhe", grad_scores_b, keys_b, preferred_element_type=jnp.float32
    ) * HEAD_DIM ** (-0.5)
    grad_keys = jnp.einsum(
        "ghqk,gqhe->gkhe", grad_scores_b, queries_b, preferred_element_type=jnp.float32
    ) * HEAD_DIM ** (-0.5)
    grad_values = jnp.einsum(
        "ghqk,gqhe->gkhe",
        attn_probs.astype(jnp.bfloat16),
        grad_mixed,
        preferred_element_type=jnp.float32,
    )
    return (
        grad_queries.astype(jnp.bfloat16),
        grad_keys.astype(jnp.bfloat16),
        grad_values.astype(jnp.bfloat16),
    )


def shards(
    hidden_in,
    image_feats,
    caption_lengths,
    pair_image,
    out_grad,
    self_qkv,
    self_out,
    cross_query,
    cross_kv,
    cross_out,
    up_weight,
    down_weight,
    vision_proj,
    text_proj,
    norm_gain,
    norm_bias,
):
    item_count, seq_len, model_width = hidden_in.shape
    vis_len = image_feats.shape[1]
    vis_width = image_feats.shape[2]
    captions = caption_lengths.shape[1]
    token_rows = item_count * seq_len
    query_rows = item_count * NQ
    feature_rows = item_count * vis_len
    text_rows = item_count * captions
    full_weights = (
        lax.all_gather(self_qkv, "dp", axis=1, tiled=True),
        lax.all_gather(self_out, "dp", axis=1, tiled=True),
        lax.all_gather(cross_query, "dp", axis=0, tiled=True),
        lax.all_gather(cross_kv, "dp", axis=1, tiled=True),
        lax.all_gather(cross_out, "dp", axis=1, tiled=True),
        lax.all_gather(up_weight, "dp", axis=0, tiled=True),
        lax.all_gather(down_weight, "dp", axis=1, tiled=True),
        lax.all_gather(vision_proj, "dp", axis=0, tiled=True),
        lax.all_gather(text_proj, "dp", axis=0, tiled=True),
        lax.all_gather(norm_gain, "dp", axis=1, tiled=True),
        lax.all_gather(norm_bias, "dp", axis=1, tiled=True),
    )
    (
        qkv_full,
        out_full,
        query_full,
        kv_full,
        cross_out_full,
        up_full,
        down_full,
        vision_full,
        text_full,
        gain_full,
        shift_full,
    ) = full_weights
    local_width = qkv_full.shape[2]
    local_heads = local_width // HEAD_DIM
    emb_width = vision_full.shape[1]
    gain_rows = gain_full.astype(jnp.float32)
    shift_rows = shift_full.astype(jnp.float32)
    labels, starts = segments(caption_lengths, seq_len)
    allowed = labels[:, :, None] == labels[:, None, :]
    tokens = hidden_in.reshape(token_rows, model_width)
    heads_shape = (item_count, seq_len, local_heads, HEAD_DIM)
    projected = jnp.einsum(
        "nd,jdc->jnc", tokens, qkv_full, preferred_element_type=jnp.float32
    ).astype(jnp.bfloat16)
    self_queries = projected[0].reshape(heads_shape)
    self_keys = projected[1].reshape(heads_shape)
    self_values = projected[2].reshape(heads_shape)
    self_mixed, self_lse = attend_forward(self_queries, self_keys, self_values, allowed)
    mixed_flat = self_mixed.reshape(token_rows, local_width)
    resid_one = tokens.astype(jnp.float32) + half_sum(matmul(mixed_flat, out_full))
    normed_one = layer_norm(resid_one, gain_rows[0], shift_rows[0])
    normed_items = normed_one.reshape(item_count, seq_len, model_width)
    first_query = normed_items[:, :NQ].reshape(query_rows, model_width)
    first_query_b = first_query.astype(jnp.bfloat16)
    cross_queries = (
        matmul(first_query_b, query_full)
        .astype(jnp.bfloat16)
        .reshape(item_count, NQ, local_heads, HEAD_DIM)
    )
    feature_flat = image_feats.reshape(feature_rows, vis_width)
    cross_proj = jnp.einsum(
        "nd,jdc->jnc", feature_flat, kv_full, preferred_element_type=jnp.float32
    ).astype(jnp.bfloat16)
    vis_shape = (item_count, vis_len, local_heads, HEAD_DIM)
    cross_keys = cross_proj[0].reshape(vis_shape)
    cross_values = cross_proj[1].reshape(vis_shape)
    cross_mixed, cross_lse = attend_forward(cross_queries, cross_keys, cross_values, None)
    cross_flat = cross_mixed.reshape(query_rows, local_width)
    resid_two = first_query + half_sum(matmul(cross_flat, cross_out_full))
    normed_query = layer_norm(resid_two, gain_rows[1], shift_rows[1])
    normed_two = jnp.concatenate(
        [normed_query.reshape(item_count, NQ, model_width), normed_items[:, NQ:]], axis=1
    ).reshape(token_rows, model_width)
    normed_two_b = normed_two.astype(jnp.bfloat16)
    up_value = matmul(normed_two_b, up_full)
    activation = gelu_exact(up_value).astype(jnp.bfloat16)
    resid_three = normed_two + half_sum(matmul(activation, down_full))
    block_b = layer_norm(resid_three, gain_rows[2], shift_rows[2]).astype(jnp.bfloat16)
    block_items = block_b.reshape(item_count, seq_len, model_width)
    query_out = block_items[:, :NQ].reshape(query_rows, model_width)
    image_all = matmul(query_out, vision_full)
    image_raw = jnp.mean(image_all.reshape(item_count, NQ, emb_width), axis=1)
    image_b = unit_rows(image_raw).astype(jnp.bfloat16)
    picker = (starts[:, :, None] == jnp.arange(seq_len, dtype=jnp.int32)[None, None, :]).astype(
        jnp.bfloat16
    )
    cls_rows = (
        jnp.einsum("ics,isd->icd", picker, block_items, preferred_element_type=jnp.float32)
        .astype(jnp.bfloat16)
        .reshape(text_rows, model_width)
    )
    text_raw = matmul(cls_rows, text_full)
    text_b = unit_rows(text_raw).astype(jnp.bfloat16)
    all_pairs = lax.all_gather(pair_image, "dp", axis=0, tiled=True)
    image_ids = lax.axis_index("dp") * item_count + jnp.arange(item_count, dtype=jnp.int32)
    text_f = text_b.astype(jnp.float32)
    image_f = image_b.astype(jnp.float32)
    start_image = jnp.full((item_count,), NEG_START, jnp.float32)
    pair_piece = all_pairs
    sim_block = (
        times_rows(image_b, lax.all_gather(text_f, "dp", axis=0, tiled=True).astype(jnp.bfloat16))
        * SIM_SCALE
    )
    new_peak = jnp.maximum(start_image, jnp.max(sim_block, axis=1))
    expo = jnp.exp(sim_block - new_peak[:, None])
    is_pair = pair_piece[None, :] == image_ids[:, None]
    image_peak = new_peak
    image_total = jnp.sum(expo, axis=1)
    image_positive = jnp.sum(jnp.where(is_pair, expo, 0.0), axis=1)
    image_lse = image_peak + jnp.log(image_total)
    image_pos = image_peak + jnp.log(image_positive)
    start_text = jnp.full((text_rows,), NEG_START, jnp.float32)
    shard_rows = lax.all_gather(image_f, "dp", axis=0, tiled=True)
    sim_block = times_rows(text_b, shard_rows.astype(jnp.bfloat16)) * SIM_SCALE
    piece_ids = jnp.arange(shard_rows.shape[0], dtype=jnp.int32)
    new_peak = jnp.maximum(start_text, jnp.max(sim_block, axis=1))
    expo = jnp.exp(sim_block - new_peak[:, None])
    is_pair = pair_image[:, None] == piece_ids[None, :]
    text_total = jnp.sum(expo, axis=1)
    text_pos = jnp.sum(jnp.where(is_pair, sim_block, 0.0), axis=1)
    text_lse = new_peak + jnp.log(text_total)
    loss_parts = lax.psum((jnp.sum(image_lse - image_pos), jnp.sum(text_lse - text_pos)), "dp")
    image_count = item_count * lax.axis_size("dp")
    text_count = image_count * captions
    contrast_loss = 0.5 * loss_parts[0] / image_count + 0.5 * loss_parts[1] / text_count
    half_image = 0.5 / image_count
    half_text = 0.5 / text_count
    back_weights = (
        lax.all_gather(self_qkv, "dp", axis=1, tiled=True),
        lax.all_gather(self_out, "dp", axis=1, tiled=True),
        lax.all_gather(cross_query, "dp", axis=0, tiled=True),
        lax.all_gather(cross_kv, "dp", axis=1, tiled=True),
        lax.all_gather(cross_out, "dp", axis=1, tiled=True),
        lax.all_gather(up_weight, "dp", axis=0, tiled=True),
        lax.all_gather(down_weight, "dp", axis=1, tiled=True),
        lax.all_gather(vision_proj, "dp", axis=0, tiled=True),
        lax.all_gather(text_proj, "dp", axis=0, tiled=True),
        lax.all_gather(norm_gain, "dp", axis=1, tiled=True),
        lax.all_gather(norm_bias, "dp", axis=1, tiled=True),
    )
    (
        qkv_back,
        out_back,
        query_back,
        kv_back,
        cross_out_back,
        up_back,
        down_back,
        vision_back,
        text_back,
        gain_back,
        shift_back,
    ) = back_weights
    gain_again = gain_back.astype(jnp.float32)
    shift_again = shift_back.astype(jnp.float32)

    def sim_grad(sim_block, is_pair, row_lse, row_pos, col_lse):
        pair_hit = is_pair.astype(jnp.float32)
        return half_text * (jnp.exp(sim_block - col_lse) - pair_hit) + half_image * (
            jnp.exp(sim_block - row_lse) - pair_hit * jnp.exp(sim_block - row_pos)
        )

    text_piece = lax.all_gather(text_f, "dp", axis=0, tiled=True)
    lse_piece = lax.all_gather(text_lse, "dp", axis=0, tiled=True)
    pair_piece = all_pairs
    text_piece_b = text_piece.astype(jnp.bfloat16)
    sim_block = times_rows(image_b, text_piece_b) * SIM_SCALE
    is_pair = pair_piece[None, :] == image_ids[:, None]
    grad_block = sim_grad(
        sim_block, is_pair, image_lse[:, None], image_pos[:, None], lse_piece[None, :]
    )
    grad_image_unit = matmul(grad_block.astype(jnp.bfloat16), text_piece_b) * SIM_SCALE
    image_piece = lax.all_gather(image_f, "dp", axis=0, tiled=True)
    lse_piece = lax.all_gather(image_lse, "dp", axis=0, tiled=True)
    pos_piece = lax.all_gather(image_pos, "dp", axis=0, tiled=True)
    image_piece_b = image_piece.astype(jnp.bfloat16)
    piece_ids = jnp.arange(image_piece.shape[0], dtype=jnp.int32)
    sim_block = times_rows(image_piece_b, text_b) * SIM_SCALE
    is_pair = pair_image[None, :] == piece_ids[:, None]
    grad_block = sim_grad(
        sim_block, is_pair, lse_piece[:, None], pos_piece[:, None], text_lse[None, :]
    )
    grad_text_unit = times_cols(grad_block.astype(jnp.bfloat16), image_piece_b) * SIM_SCALE
    unit_value, image_unit_back = jax.vjp(unit_rows, image_raw)
    grad_image_raw = image_unit_back(grad_image_unit)[0]
    grad_image_all = (
        jnp.broadcast_to((grad_image_raw / NQ)[:, None, :], (item_count, NQ, emb_width))
        .reshape(query_rows, emb_width)
        .astype(jnp.bfloat16)
    )
    grad_vision = times_cols(query_out, grad_image_all)
    unit_text_value, text_unit_back = jax.vjp(unit_rows, text_raw)
    grad_text_raw = text_unit_back(grad_text_unit)[0].astype(jnp.bfloat16)
    grad_text = times_cols(cls_rows, grad_text_raw)
    query_grad = times_rows(grad_image_all, vision_back).reshape(item_count, NQ, model_width)
    cls_grad = times_rows(grad_text_raw, text_back).reshape(item_count, captions, model_width)
    spread = jnp.einsum(
        "ics,icd->isd", picker.astype(jnp.float32), cls_grad, precision=lax.Precision.HIGHEST
    )
    query_pad = jnp.concatenate(
        [query_grad, jnp.zeros((item_count, seq_len - NQ, model_width), jnp.float32)], axis=1
    )
    grad_items = (out_grad.astype(jnp.float32) + spread + query_pad).reshape(
        token_rows, model_width
    )
    norm_value, norm_three_back = jax.vjp(layer_norm, resid_three, gain_again[2], shift_again[2])
    grad_resid_three, grad_gain_three, grad_shift_three = norm_three_back(grad_items)
    grad_branch_three = grad_resid_three.astype(jnp.bfloat16)
    grad_down = times_cols(activation, grad_branch_three)
    grad_activation = times_rows(grad_branch_three, down_back)
    gelu_value, gelu_back = jax.vjp(gelu_exact, up_value)
    grad_up_value = gelu_back(grad_activation)[0].astype(jnp.bfloat16)
    grad_up = times_cols(normed_two_b, grad_up_value)
    grad_normed_two = grad_resid_three + half_sum(times_rows(grad_up_value, up_back))
    grad_two_items = grad_normed_two.reshape(item_count, seq_len, model_width)
    grad_two_query = grad_two_items[:, :NQ].reshape(query_rows, model_width)
    norm_two_value, norm_two_back = jax.vjp(layer_norm, resid_two, gain_again[1], shift_again[1])
    grad_resid_two, grad_gain_two, grad_shift_two = norm_two_back(grad_two_query)
    grad_branch_two = grad_resid_two.astype(jnp.bfloat16)
    grad_cross_out = times_cols(cross_flat, grad_branch_two)
    grad_cross_mixed = (
        times_rows(grad_branch_two, cross_out_back)
        .astype(jnp.bfloat16)
        .reshape(item_count, NQ, local_heads, HEAD_DIM)
    )
    grad_cross_q, grad_cross_k, grad_cross_v = attend_backward(
        cross_queries, cross_keys, cross_values, None, cross_lse, grad_cross_mixed
    )
    grad_cross_q_flat = grad_cross_q.reshape(query_rows, local_width)
    grad_cross_query = times_cols(first_query_b, grad_cross_q_flat)
    grad_first_query = grad_resid_two + half_sum(times_rows(grad_cross_q_flat, query_back))
    grad_kv_rows = jnp.stack(
        [
            grad_cross_k.reshape(feature_rows, local_width),
            grad_cross_v.reshape(feature_rows, local_width),
        ]
    )
    grad_cross_kv = jnp.einsum(
        "nd,jnc->jdc", feature_flat, grad_kv_rows, preferred_element_type=jnp.float32
    )
    feature_part = jnp.einsum(
        "jnc,jdc->nd", grad_kv_rows, kv_back, preferred_element_type=jnp.float32
    )
    grad_feats = lax.psum(feature_part.astype(jnp.bfloat16), "mp").reshape(image_feats.shape)
    grad_one = jnp.concatenate(
        [grad_first_query.reshape(item_count, NQ, model_width), grad_two_items[:, NQ:]], axis=1
    ).reshape(token_rows, model_width)
    norm_one_value, norm_one_back = jax.vjp(layer_norm, resid_one, gain_again[0], shift_again[0])
    grad_resid_one, grad_gain_one, grad_shift_one = norm_one_back(grad_one)
    grad_branch_one = grad_resid_one.astype(jnp.bfloat16)
    grad_self_out = times_cols(mixed_flat, grad_branch_one)
    grad_self_mixed = (
        times_rows(grad_branch_one, out_back).astype(jnp.bfloat16).reshape(heads_shape)
    )
    grad_self_q, grad_self_k, grad_self_v = attend_backward(
        self_queries, self_keys, self_values, allowed, self_lse, grad_self_mixed
    )
    grad_projected = jnp.stack(
        [
            grad_self_q.reshape(token_rows, local_width),
            grad_self_k.reshape(token_rows, local_width),
            grad_self_v.reshape(token_rows, local_width),
        ]
    )
    grad_self_qkv = jnp.einsum(
        "nd,jnc->jdc", tokens, grad_projected, preferred_element_type=jnp.float32
    )
    grad_tokens = grad_resid_one + half_sum(
        jnp.einsum("jnc,jdc->nd", grad_projected, qkv_back, preferred_element_type=jnp.float32)
    )
    grad_hidden = grad_tokens.astype(jnp.bfloat16).reshape(hidden_in.shape)
    grad_gain = jnp.stack([grad_gain_one, grad_gain_two, grad_gain_three])
    grad_shift = jnp.stack([grad_shift_one, grad_shift_two, grad_shift_three])
    shares = (
        lax.psum_scatter(grad_self_qkv, "dp", scatter_dimension=1, tiled=True),
        lax.psum_scatter(grad_self_out, "dp", scatter_dimension=1, tiled=True),
        lax.psum_scatter(grad_cross_query, "dp", scatter_dimension=0, tiled=True),
        lax.psum_scatter(grad_cross_kv, "dp", scatter_dimension=1, tiled=True),
        lax.psum_scatter(grad_cross_out, "dp", scatter_dimension=1, tiled=True),
        lax.psum_scatter(grad_up, "dp", scatter_dimension=0, tiled=True),
        lax.psum_scatter(grad_down, "dp", scatter_dimension=1, tiled=True),
        lax.psum_scatter(grad_vision, "dp", scatter_dimension=0, tiled=True),
        lax.psum_scatter(grad_text, "dp", scatter_dimension=0, tiled=True),
        lax.psum_scatter(grad_gain, "dp", scatter_dimension=1, tiled=True),
        lax.psum_scatter(grad_shift, "dp", scatter_dimension=1, tiled=True),
    )
    return (contrast_loss, block_b.reshape(hidden_in.shape), grad_hidden, grad_feats) + tuple(
        shares
    )


def solution(mesh):
    return jax.shard_map(
        shards,
        mesh=mesh,
        in_specs=(
            P("dp", None, None),
            P("dp", None, None),
            P("dp", None),
            P("dp"),
            P("dp", None, None),
            P(None, "dp", "mp"),
            P("mp", "dp"),
            P("dp", "mp"),
            P(None, "dp", "mp"),
            P("mp", "dp"),
            P("dp", "mp"),
            P("mp", "dp"),
            P("dp", None),
            P("dp", None),
            P(None, "dp"),
            P(None, "dp"),
        ),
        out_specs=(
            P(),
            P("dp", None, None),
            P("dp", None, None),
            P("dp", None, None),
            P(None, "dp", "mp"),
            P("mp", "dp"),
            P("dp", "mp"),
            P(None, "dp", "mp"),
            P("mp", "dp"),
            P("dp", "mp"),
            P("mp", "dp"),
            P("dp", None),
            P("dp", None),
            P(None, "dp"),
            P(None, "dp"),
        ),
        check_vma=False,
    )
```

profile of v0, /device:TPU:0, one launch (start us, length us, event | category | flops | bytes accessed | tf_op | source)
XLA Modules:
  0.0 1574.6 jit_solution(16052719423150312157)
XLA Ops:
  10.1 23.3 %all-gather = bf16[16,48,3]{1,2,0:T(4,128)(2,1)S(1)} all-gather(bf16[1,48,3]{1,2,0:T(4,128)(2,1)} %bitcast.198), channel_id=1, replica_groups=mesh['dp'=16,'mp'=2] {'dp'}, dimensions={0}, use_global_device_ids=true | all-gather | bytes 4896 | tf_op jit(solution)/shard_map/all_gather | solution.py:148
  65.2 22.6 %all_gather.64 = bf16[384,768]{0,1:T(8,128)(2,1)} all-gather(bf16[384,48]{0,1:T(8,128)(2,1)S(1)} %copy-done.75), channel_id=1, replica_groups=mesh['dp'=16,'mp'=2] {'dp'}, dimensions={1}, use_global_device_ids=true | all-gather | bytes 626688 | tf_op jit(solution)/shard_map/all_gather | solution.py:140
  87.8 21.4 %all_gather.68 = bf16[768,384]{1,0:T(8,128)(2,1)} all-gather(bf16[48,384]{1,0:T(8,128)(2,1)S(1)} %copy-done.76), channel_id=1, replica_groups=mesh['dp'=16,'mp'=2] {'dp'}, dimensions={0}, use_global_device_ids=true | all-gather | bytes 626688 | tf_op jit(solution)/shard_map/all_gather | solution.py:141
  109.2 21.5 %all_gather.69 = bf16[384,768]{0,1:T(8,128)(2,1)} all-gather(bf16[384,48]{0,1:T(8,128)(2,1)S(1)} %copy-done.77), channel_id=1, replica_groups=mesh['dp'=16,'mp'=2] {'dp'}, dimensions={1}, use_global_device_ids=true | all-gather | bytes 626688 | tf_op jit(solution)/shard_map/all_gather | solution.py:143
  169.7 19.2 %all-reduce.18.cloned.1.call-done = f32[512,768]{1,0:T(8,128)} async-done(((f32[512,768]{1,0:T(8,128)}), f32[512,768]{1,0:T(8,128)}) %all-reduce.18.cloned.1.call-update) | async-done | bytes 1572880 | tf_op jit(solution)/shard_map/psum | solution.py:49
  204.2 33.3 %all-reduce.20.cloned.1.call-done = f32[256,768]{1,0:T(8,128)} async-done(((f32[256,768]{1,0:T(8,128)}), f32[256,768]{1,0:T(8,128)}) %all-reduce.20.cloned.1.call-update) | async-done | bytes 786448 | tf_op jit(solution)/shard_map/psum | solution.py:49
  242.9 39.0 %all-gather.11.cloned.1.call-done = bf16[768,1536]{1,0:T(8,128)(2,1)} async-done(((bf16[48,1536]{1,0:T(8,128)(2,1)}), bf16[768,1536]{1,0:T(8,128)(2,1)}) %all-gather.11.cloned.1.call-update) | async-done | bytes 2359312 | tf_op jit(solution)/shard_map/all_gather | solution.py:144
  293.0 32.3 %all-gather.13.cloned.1.call-done = bf16[1536,768]{0,1:T(8,128)(2,1)} async-done(((bf16[1536,48]{0,1:T(8,128)(2,1)}), bf16[1536,768]{0,1:T(8,128)(2,1)}) %all-gather.13.cloned.1.call-update) | async-done | bytes 2359312 | tf_op jit(solution)/shard_map/all_gather | solution.py:145
  343.5 21.9 %all_gather.72 = bf16[768,256]{1,0:T(8,128)(2,1)} all-gather(bf16[48,256]{1,0:T(8,128)(2,1)S(1)} %copy-done.84), channel_id=1, replica_groups=mesh['dp'=16,'mp'=2] {'dp'}, dimensions={0}, use_global_device_ids=true | all-gather | bytes 417792 | tf_op jit(solution)/shard_map/all_gather | solution.py:146
  365.4 18.9 %all_gather.73 = bf16[768,256]{1,0:T(8,128)(2,1)S(1)} all-gather(bf16[48,256]{1,0:T(8,128)(2,1)} %param.29), channel_id=1, replica_groups=mesh['dp'=16,'mp'=2] {'dp'}, dimensions={0}, use_global_device_ids=true | all-gather | bytes 417792 | tf_op jit(solution)/shard_map/all_gather | solution.py:147
  392.3 18.9 %all_gather.76 = bf16[128,256]{1,0:T(8,128)(2,1)S(1)} all-gather(bf16[8,256]{1,0:T(8,128)(2,1)S(1)} %fusion.100), channel_id=1, replica_groups=mesh['dp'=16,'mp'=2] {'dp'}, dimensions={0}, use_global_device_ids=true | all-gather | bytes 69632 | tf_op jit(solution)/shard_map/all_gather | solution.py:244
  434.8 31.8 %all-reduce.7 = (f32[]{:T(128)}, f32[]{:T(128)}, f32[384]{0:T(512)}, f32[128]{0:T(128)}, f32[128]{0:T(128)}) all-reduce(f32[]{:T(128)} %subtract_reduce_fusion.1, f32[]{:T(128)} %subtract_reduce_fusion, f32[384]{0:T(512)} %copy-done.106, f32[128]{0:T(128)} %copy-done.116, f32[128]{0:T(128)} %copy-done.115), channel_id=1, replica_groups=mesh['dp'=16,'mp'=2] {'dp'}, use_global_device_ids=true, to_apply=%region_22.23 | all-reduce | flops 642 | bytes 5136 | tf_op jit(solution)/shard_map/psum | solution.py:253
  491.3 47.0 %all-reduce.24.cloned.1.call-done = f32[512,768]{1,0:T(8,128)} async-done(((f32[512,768]{1,0:T(8,128)}), f32[512,768]{1,0:T(8,128)}) %all-reduce.24.cloned.1.call-update) | async-done | bytes 1572880 | tf_op jit(solution)/shard_map/psum | solution.py:49
  684.6 33.5 %reduce-scatter.30.cloned.1.call-done = f32[48,3]{1,0:T(8,128)} async-done(((f32[768,3]{1,0:T(8,128)}), f32[48,3]{1,0:T(8,128)}) %reduce-scatter.30.cloned.1.call-update) | async-done | bytes 592
  719.5 51.4 %all-reduce.28.cloned.1.call-done = f32[512,768]{1,0:T(8,128)} async-done(((f32[512,768]{1,0:T(8,128)}), f32[512,768]{1,0:T(8,128)}) %all-reduce.28.cloned.1.call-update) | async-done | bytes 1572880 | tf_op jit(solution)/shard_map/psum | solution.py:49
  773.4 180.5 %all-reduce.32.cloned.1.call-done = (f32[3,768,384]{2,0,1:T(4,128)}, f32[2,1408,384]{2,0,1:T(2,128)}) async-done(((f32[3,768,384]{2,0,1:T(4,128)}, f32[2,1408,384]{2,0,1:T(2,128)}), (f32[3,768,384]{2,0,1:T(4,128)}, f32[2,1408,384]{2,0,1:T(2,128)})) %all-reduce.32.cloned.1.call-update) | async-done | bytes 7864336
  957.3 144.9 %all-reduce.30.cloned.1.call-done = bf16[8,257,1408]{2,1,0:T(8,128)(2,1)} async-done(((bf16[8,257,1408]{2,1,0:T(8,128)(2,1)}), bf16[8,257,1408]{2,1,0:T(8,128)(2,1)}) %all-reduce.30.cloned.1.call-update) | async-done | bytes 5789712 | tf_op jit(solution)/shard_map/psum | solution.py:375
  1108.2 55.3 %reduce-scatter.26.cloned.1.call-done = f32[48,256]{1,0:T(8,128)} async-done(((f32[768,256]{1,0:T(8,128)}), f32[48,256]{1,0:T(8,128)}) %reduce-scatter.26.cloned.1.call-update) | async-done | bytes 49168 | tf_op jit(solution)/shard_map/reduce_scatter | solution.py:414
  1163.4 59.6 %reduce-scatter.24.cloned.1.call-done = f32[48,256]{1,0:T(8,128)} async-done(((f32[768,256]{1,0:T(8,128)}), f32[48,256]{1,0:T(8,128)}) %reduce-scatter.24.cloned.1.call-update) | async-done | bytes 49168 | tf_op jit(solution)/shard_map/reduce_scatter | solution.py:413
  1223.0 61.6 %reduce-scatter.18.cloned.1.call-done = f32[384,48]{0,1:T(8,128)} async-done(((f32[384,768]{0,1:T(8,128)}), f32[384,48]{0,1:T(8,128)}) %reduce-scatter.18.cloned.1.call-update) | async-done | bytes 73744 | tf_op jit(solution)/shard_map/reduce_scatter | solution.py:410
  1284.6 61.6 %reduce-scatter.16.cloned.1.call-done = f32[48,384]{1,0:T(8,128)} async-done(((f32[768,384]{1,0:T(8,128)}), f32[48,384]{1,0:T(8,128)}) %reduce-scatter.16.cloned.1.call-update) | async-done | bytes 73744 | tf_op jit(solution)/shard_map/reduce_scatter | solution.py:408
  1346.3 61.7 %reduce-scatter.14.cloned.1.call-done = f32[384,48]{0,1:T(8,128)} async-done(((f32[384,768]{0,1:T(8,128)}), f32[384,48]{0,1:T(8,128)}) %reduce-scatter.14.cloned.1.call-update) | async-done | bytes 73744 | tf_op jit(solution)/shard_map/reduce_scatter | solution.py:407
  1408.0 79.4 %reduce-scatter.22.cloned.1.call-done = f32[1536,48]{0,1:T(8,128)} async-done(((f32[1536,768]{0,1:T(8,128)}), f32[1536,48]{0,1:T(8,128)}) %reduce-scatter.22.cloned.1.call-update) | async-done | bytes 294928 | tf_op jit(solution)/shard_map/reduce_scatter | solution.py:412
  1487.4 79.1 %reduce-scatter.20.cloned.1.call-done = f32[48,1536]{1,0:T(8,128)} async-done(((f32[768,1536]{1,0:T(8,128)}), f32[48,1536]{1,0:T(8,128)}) %reduce-scatter.20.cloned.1.call-update) | async-done | bytes 294928 | tf_op jit(solution)/shard_map/reduce_scatter | solution.py:411
  (479 shorter events, 334.0 us)
Async XLA Ops:
  7.2 123.6 %all-gather.7.cloned.1.call-start = ((), (), s32[]{:S(2)}) async-start(), calls=%async_computation.9 | async-start | bytes 1880064 | tf_op jit(solution)/shard_map/all_gather | solution.py:139
  7.9 132.5 %all-gather.9.cloned.1.call-start = ((), (), s32[]{:S(2)}) async-start(), calls=%async_computation.11 | async-start | bytes 2297856 | tf_op jit(solution)/shard_map/all_gather | solution.py:142
  8.7 180.2 %all-reduce.18.cloned.1.call-start = ((), (), s32[]{:S(2)}) async-start(), calls=%async_computation.10 | async-start | bytes 3145728 | tf_op jit(solution)/shard_map/psum | solution.py:49
  57.3 73.5 %copy-start.29 = (bf16[8,64,768]{2,1,0:T(8,128)(2,1)S(1)}, bf16[8,64,768]{2,1,0:T(8,128)(2,1)}, u32[]{:S(2)}) copy-start(bf16[8,64,768]{2,1,0:T(8,128)(2,1)} %param.16) | copy-start | bytes 2359300
  64.4 126.5 %copy-start.66 = (f32[768]{0:T(1024)}, f32[768]{0:T(1024)S(1)}, u32[]{:S(2)}) copy-start(f32[768]{0:T(1024)S(1)} %get-tuple-element.104) | copy-start | bytes 9220
  64.5 322.3 %copy-start.68 = (f32[768]{0:T(1024)}, f32[768]{0:T(1024)S(1)}, u32[]{:S(2)}) copy-start(f32[768]{0:T(1024)S(1)} %get-tuple-element.102) | copy-start | bytes 9220
  140.0 97.5 %all-reduce.20.cloned.1.call-start = ((), (), s32[]{:S(2)}) async-start(), calls=%async_computation.12 | async-start | bytes 1572864 | tf_op jit(solution)/shard_map/psum | solution.py:49
  203.0 79.0 %all-gather.11.cloned.1.call-start = ((), (), s32[]{:S(2)}) async-start(), calls=%async_computation.13 | async-start | bytes 2506752 | tf_op jit(solution)/shard_map/all_gather | solution.py:144
  203.6 121.7 %all-gather.13.cloned.1.call-start = ((), (), s32[]{:S(2)}) async-start(), calls=%async_computation.14 | async-start | bytes 2506752 | tf_op jit(solution)/shard_map/all_gather | solution.py:145
  204.2 180.1 %all-reduce.22.cloned.1.call-start = ((), (), s32[]{:S(2)}) async-start(), calls=%async_computation.15 | async-start | bytes 3145728 | tf_op jit(solution)/shard_map/psum | solution.py:49
  330.0 208.3 %all-reduce.24.cloned.1.call-start = ((), (), s32[]{:S(2)}) async-start(), calls=%async_computation.16 | async-start | bytes 3145728 | tf_op jit(solution)/shard_map/psum | solution.py:49
  489.4 100.4 %all-reduce.26.cloned.1.call-start = ((), (), s32[]{:S(2)}) async-start(), calls=%async_computation.17 | async-start | bytes 1572864 | tf_op jit(solution)/shard_map/psum | solution.py:49
  555.3 127.9 %reduce-scatter.28.cloned.1.call-start = ((), (), s32[]{:S(2)}) async-start(), calls=%async_computation.27 | async-start | bytes 417792
  604.3 113.8 %reduce-scatter.30.cloned.1.call-start = ((), (), s32[]{:S(2)}) async-start(), calls=%async_computation.28 | async-start | bytes 417792
  611.3 159.6 %all-reduce.28.cloned.1.call-start = ((), (), s32[]{:S(2)}) async-start(), calls=%async_computation.18 | async-start | bytes 3145728 | tf_op jit(solution)/shard_map/psum | solution.py:49
  615.9 338.0 %all-reduce.32.cloned.1.call-start = ((), (), s32[]{:S(2)}) async-start(), calls=%async_computation.29 | async-start | bytes 18087936
  642.2 460.0 %all-reduce.30.cloned.1.call-start = ((), (), s32[]{:S(2)}) async-start(), calls=%async_computation.19 | async-start | bytes 11894784 | tf_op jit(solution)/shard_map/psum | solution.py:375
  659.6 503.9 %reduce-scatter.26.cloned.1.call-start = ((), (), s32[]{:S(2)}) async-start(), calls=%async_computation.26 | async-start | bytes 835584 | tf_op jit(solution)/shard_map/reduce_scatter | solution.py:414
  661.5 561.5 %reduce-scatter.24.cloned.1.call-start = ((), (), s32[]{:S(2)}) async-start(), calls=%async_computation.25 | async-start | bytes 835584 | tf_op jit(solution)/shard_map/reduce_scatter | solution.py:413
  663.0 621.6 %reduce-scatter.18.cloned.1.call-start = ((), (), s32[]{:S(2)}) async-start(), calls=%async_computation.22 | async-start | bytes 1253376 | tf_op jit(solution)/shard_map/reduce_scatter | solution.py:410
  664.6 681.6 %reduce-scatter.16.cloned.1.call-start = ((), (), s32[]{:S(2)}) async-start(), calls=%async_computation.21 | async-start | bytes 1253376 | tf_op jit(solution)/shard_map/reduce_scatter | solution.py:408
  667.5 740.5 %reduce-scatter.14.cloned.1.call-start = ((), (), s32[]{:S(2)}) async-start(), calls=%async_computation.20 | async-start | bytes 1253376 | tf_op jit(solution)/shard_map/reduce_scatter | solution.py:407
  669.3 818.1 %reduce-scatter.22.cloned.1.call-start = ((), (), s32[]{:S(2)}) async-start(), calls=%async_computation.24 | async-start | bytes 5013504 | tf_op jit(solution)/shard_map/reduce_scatter | solution.py:412
  674.5 892.0 %reduce-scatter.20.cloned.1.call-start = ((), (), s32[]{:S(2)}) async-start(), calls=%async_computation.23 | async-start | bytes 5013504 | tf_op jit(solution)/shard_map/reduce_scatter | solution.py:411
  (118 other events, 640.9 us)
Sparse Core Ops, SparseCore 0:
  10.3 43.1 all-gather.6
  55.7 42.7 all-gather.8
  140.1 48.7 all-reduce.17
  203.1 34.3 all-reduce.19
  239.6 42.3 all-gather.10
  284.1 41.0 all-gather.12
  330.1 50.2 all-reduce.21
  489.5 48.7 all-reduce.23
  555.4 34.3 all-reduce.25
  604.4 55.5 reduce-scatter.27
  663.5 54.5 reduce-scatter.29
  720.4 50.4 all-reduce.27
  774.6 179.1 all-reduce.31
  956.3 145.8 all-reduce.29
  1106.6 56.7 reduce-scatter.25
  1167.4 55.5 reduce-scatter.23
  1227.5 57.0 reduce-scatter.17
  1289.1 57.0 reduce-scatter.15
  1350.9 57.0 reduce-scatter.13
  1412.8 74.5 reduce-scatter.21
  1491.8 74.5 reduce-scatter.19
where the time goes:
time: 1590 us; the launch traced here: 1570 us
  waiting for transfers between devices  1040 us (65%)
  blocking collectives  227 us (14%)
  local copies, waits for them, and re-layouts  135 us (8%)
  matrix products  113 us (7%)
  other arithmetic  33.8 us (2%)
  between operations  21.1 us (1%)
    unnamed x24, waiting for transfers between devices  217 us
    psum x6, waiting for transfers between devices, half_sum(): return lax.psum(value, 'mp')  152 us
    psum x1, waiting for transfers between devices, shards(): lax.psum(feature_part.astype(jnp.bfloat16), 'mp').reshape(image_feats.shape)  145 us
    reduce_scatter x1, waiting for transfers between devices, shards(): lax.psum_scatter(grad_down, 'dp', scatter_dimension=1, tiled=True)  79.4 us
    reduce_scatter x1, waiting for transfers between devices, shards(): lax.psum_scatter(grad_up, 'dp', scatter_dimension=0, tiled=True)  79.1 us
    reduce_scatter x1, waiting for transfers between devices, shards(): lax.psum_scatter(grad_self_out, 'dp', scatter_dimension=1, tiled=True)  61.7 us
    reduce_scatter x1, waiting for transfers between devices, shards(): lax.psum_scatter(grad_cross_query, 'dp', scatter_dimension=0, tiled=True)  61.6 us
    reduce_scatter x1, waiting for transfers between devices, shards(): lax.psum_scatter(grad_cross_out, 'dp', scatter_dimension=1, tiled=True)  61.6 us
  transfers between devices with their start and end apart: 21, of which 17 were waited for; matrix products, arithmetic and copies ran while one was open for 12% of the time, Pallas kernels for 0%

commit v1 on v0

v1 whole, which is shorter than its diff:
```python
import jax
import jax.numpy as jnp
from jax import lax
from jax.sharding import PartitionSpec as P

HEAD_DIM = 64
NQ = 32
EPS_NORM = 1e-06
EPS_UNIT = 1e-06
SIM_SCALE = 16.0
MASKED = -1000000000.0
F32 = jnp.float32
BF16 = jnp.bfloat16


def layer_norm(value, gain, shift):
    row_mean = jnp.mean(value, -1, keepdims=True)
    centered = value - row_mean
    row_var = jnp.mean(centered * centered, -1, keepdims=True)
    return centered * lax.rsqrt(row_var + EPS_NORM) * gain + shift


def unit_rows(value):
    return value * lax.rsqrt(jnp.sum(value * value, -1, keepdims=True) + EPS_UNIT)


def gelu_exact(value):
    return jax.nn.gelu(value, approximate=False)


def matmul(left, right):
    return jnp.dot(left, right, preferred_element_type=F32)


def times_rows(left, right):
    return lax.dot_general(left, right, (((1,), (1,)), ((), ())), preferred_element_type=F32)


def times_cols(left, right):
    return lax.dot_general(left, right, (((0,), (0,)), ((), ())), preferred_element_type=F32)


def segments(lengths, seq_len):
    ends = [NQ + lengths[:, 0]]
    for c in range(1, lengths.shape[1]):
        ends.append(ends[-1] + lengths[:, c])
    bounds = jnp.stack(ends, axis=1)
    places = jnp.arange(seq_len, dtype=jnp.int32)
    labels = (places >= NQ).astype(jnp.int32)[None, :] + jnp.sum(
        (places[None, None, :] >= bounds[:, :-1, None]).astype(jnp.int32), axis=1
    )
    return labels, bounds - lengths


def attend_scores(queries_b, keys_b, allowed):
    scores = jnp.einsum("gqhe,gkhe->ghqk", queries_b, keys_b, preferred_element_type=F32) * HEAD_DIM ** (-0.5)
    if allowed is not None:
        scores = jnp.where(allowed[:, None], scores, MASKED)
    return scores


def attend_forward(queries_b, keys_b, values_b, allowed):
    scores = attend_scores(queries_b, keys_b, allowed)
    row_peak = jnp.max(scores, -1, keepdims=True)
    expo = jnp.exp(scores - row_peak)
    row_total = jnp.sum(expo, -1, keepdims=True)
    attn_probs = expo / row_total
    mixed_out = jnp.einsum("ghqk,gkhe->gqhe", attn_probs.astype(BF16), values_b, preferred_element_type=F32)
    return mixed_out.astype(BF16), row_peak + jnp.log(row_total)


def attend_backward(queries_b, keys_b, values_b, allowed, row_lse, grad_mixed):
    scores = attend_scores(queries_b, keys_b, allowed)
    attn_probs = jnp.exp(scores - row_lse)
    grad_probs = jnp.einsum("gqhe,gkhe->ghqk", grad_mixed, values_b, preferred_element_type=F32)
    grad_scores = attn_probs * (grad_probs - jnp.sum(grad_probs * attn_probs, -1, keepdims=True))
    grad_scores_b = grad_scores.astype(BF16)
    scale = HEAD_DIM ** (-0.5)
    grad_queries = jnp.einsum("ghqk,gkhe->gqhe", grad_scores_b, keys_b, preferred_element_type=F32) * scale
    grad_keys = jnp.einsum("ghqk,gqhe->gkhe", grad_scores_b, queries_b, preferred_element_type=F32) * scale
    grad_values = jnp.einsum("ghqk,gqhe->gkhe", attn_probs.astype(BF16), grad_mixed, preferred_element_type=F32)
    return grad_queries.astype(BF16), grad_keys.astype(BF16), grad_values.astype(BF16)


def shards(
    n_dp, n_mp, hidden_in, image_feats, caption_lengths, pair_image, out_grad, self_qkv, self_out, cross_query,
    cross_kv, cross_out, up_weight, down_weight, vision_proj, text_proj, norm_gain, norm_bias,
):
    both = ("mp", "dp")
    me_m = lax.axis_index("mp")
    me_d = lax.axis_index("dp")
    block_items_n, seq_len, width = hidden_in.shape
    items = block_items_n // n_mp
    vis_len, vis_width = image_feats.shape[1:]
    captions = caption_lengths.shape[1]
    tokens_n, query_n, feat_n, text_n = items * seq_len, items * NQ, items * vis_len, items * captions
    lane = self_qkv.shape[2]
    rows, rows_kv = self_qkv.shape[1], cross_kv.shape[1]
    pieces = up_weight.shape[1] // lane
    heads = width // HEAD_DIM
    emb = vision_proj.shape[1]

    def mine(value):
        return lax.dynamic_slice_in_dim(value, me_m * items, items, axis=0)

    hidden = mine(hidden_in)
    feats = mine(image_feats)
    lengths = mine(caption_lengths)
    cotangent = mine(out_grad)

    def cut(value):
        return jnp.moveaxis(value.reshape(value.shape[0], -1, lane), 1, 0).reshape(-1, lane)

    half_emb = emb // n_mp
    vis_half = lax.dynamic_slice_in_dim(vision_proj, me_m * half_emb, half_emb, axis=1)
    txt_half = lax.dynamic_slice_in_dim(text_proj, me_m * half_emb, half_emb, axis=1)
    norms = jnp.concatenate([norm_gain, norm_bias], axis=0).T
    norms = jnp.pad(norms, ((0, 0), (0, lane - 2 * half_emb - norms.shape[1])))
    misc = jnp.concatenate([vis_half, txt_half, norms], axis=1)
    packed = jnp.concatenate(
        [
            self_qkv.reshape(-1, lane), cross_query, self_out.T, misc, cross_kv.reshape(-1, lane), cross_out.T,
            cut(up_weight), cut(down_weight.T),
        ],
        axis=0,
    )
    sizes = [rows] * 6 + [rows_kv] * 2 + [rows] * (1 + 2 * pieces)
    places = [0]
    for size in sizes:
        places.append(places[-1] + size)
    gathered = lax.all_gather(packed, both, axis=0, tiled=False).reshape(n_mp, n_dp, places[-1], lane)

    def part(index):
        return gathered[:, :, places[index] : places[index + 1]].reshape(n_mp, n_dp * sizes[index], lane)

    def wide(value):
        return jnp.moveaxis(value, 0, 1).reshape(value.shape[1], -1)

    w_qkv = [wide(part(j)) for j in range(3)]
    w_query = wide(part(3))
    w_out_t = wide(part(4))
    w_misc = part(5)
    w_kv = [wide(part(6)), wide(part(7))]
    w_cross_out_t = wide(part(8))
    w_up = jnp.stack([part(9 + p) for p in range(pieces)], axis=1)
    w_up = jnp.transpose(w_up, (2, 0, 1, 3)).reshape(width, -1)
    w_down_t = jnp.stack([part(9 + pieces + p) for p in range(pieces)], axis=1)
    w_down_t = jnp.transpose(w_down_t, (2, 0, 1, 3)).reshape(width, -1)
    w_vision = wide(w_misc[:, :, :half_emb])
    w_text = wide(w_misc[:, :, half_emb : 2 * half_emb])
    norm_rows = w_misc[0, :, 2 * half_emb : 2 * half_emb + 6].T.astype(F32)
    gain, shift = norm_rows[:3], norm_rows[3:]

    labels, starts = segments(lengths, seq_len)
    allowed = labels[:, :, None] == labels[:, None, :]
    tokens = hidden.reshape(tokens_n, width)
    shape4 = (items, seq_len, heads, HEAD_DIM)
    q, k, v = (matmul(tokens, w).astype(BF16).reshape(shape4) for w in w_qkv)
    mixed, self_lse = attend_forward(q, k, v, allowed)
    mixed = mixed.reshape(tokens_n, width)
    resid_one = tokens.astype(F32) + times_rows(mixed, w_out_t)
    normed_one = layer_norm(resid_one, gain[0], shift[0])
    normed_items = normed_one.reshape(items, seq_len, width)
    first_query = normed_items[:, :NQ].reshape(query_n, width)
    first_query_b = first_query.astype(BF16)
    cross_q = matmul(first_query_b, w_query).astype(BF16).reshape(items, NQ, heads, HEAD_DIM)
    feat_flat = feats.reshape(feat_n, vis_width)
    shape_vis = (items, vis_len, heads, HEAD_DIM)
    cross_k, cross_v = (matmul(feat_flat, w).astype(BF16).reshape(shape_vis) for w in w_kv)
    cross_mixed, cross_lse = attend_forward(cross_q, cross_k, cross_v, None)
    cross_flat = cross_mixed.reshape(query_n, width)
    resid_two = first_query + times_rows(cross_flat, w_cross_out_t)
    normed_query = layer_norm(resid_two, gain[1], shift[1])
    normed_two = jnp.concatenate(
        [normed_query.reshape(items, NQ, width), normed_items[:, NQ:]], axis=1
    ).reshape(tokens_n, width)
    normed_two_b = normed_two.astype(BF16)
    up_value = matmul(normed_two_b, w_up)
    activation = gelu_exact(up_value).astype(BF16)
    resid_three = normed_two + times_rows(activation, w_down_t)
    block_b = layer_norm(resid_three, gain[2], shift[2]).astype(BF16)
    block_items = block_b.reshape(items, seq_len, width)
    query_out = block_items[:, :NQ].reshape(query_n, width)
    image_raw = jnp.mean(matmul(query_out, w_vision).reshape(items, NQ, emb), axis=1)
    image_b = unit_rows(image_raw).astype(BF16)
    picker = (starts[:, :, None] == jnp.arange(seq_len, dtype=jnp.int32)[None, None, :]).astype(BF16)
    cls_rows = (
        jnp.einsum("ics,isd->icd", picker, block_items, preferred_element_type=F32).astype(BF16).reshape(text_n, width)
    )
    text_raw = matmul(cls_rows, w_text)
    text_b = unit_rows(text_raw).astype(BF16)

    all_pairs = lax.all_gather(pair_image, "dp", axis=0, tiled=True)
    embs = lax.all_gather(jnp.concatenate([image_b, text_b], axis=0), ("dp", "mp"), axis=0, tiled=False)
    all_image = embs[:, :items].reshape(-1, emb)
    all_text = embs[:, items:].reshape(-1, emb)
    image_count, text_count = all_image.shape[0], all_text.shape[0]
    sims = times_rows(all_image, all_text) * SIM_SCALE
    is_pair = all_pairs[None, :] == jnp.arange(image_count, dtype=jnp.int32)[:, None]
    col_peak = jnp.max(sims, axis=0, keepdims=True)
    col_lse = col_peak + jnp.log(jnp.sum(jnp.exp(sims - col_peak), axis=0, keepdims=True))
    row_peak = jnp.max(sims, axis=1, keepdims=True)
    row_expo = jnp.exp(sims - row_peak)
    row_lse = row_peak + jnp.log(jnp.sum(row_expo, axis=1, keepdims=True))
    pair_sims = jnp.where(is_pair, sims, MASKED)
    pos_peak = jnp.max(pair_sims, axis=1, keepdims=True)
    row_pos = pos_peak + jnp.log(jnp.sum(jnp.exp(pair_sims - pos_peak), axis=1, keepdims=True))
    col_pos = jnp.sum(jnp.where(is_pair, sims, 0.0), axis=0, keepdims=True)
    half_image, half_text = 0.5 / image_count, 0.5 / text_count
    contrast_loss = half_text * jnp.sum(col_lse - col_pos) + half_image * jnp.sum(row_lse - row_pos)
    hit = is_pair.astype(F32)
    grad_sims = (
        half_text * (jnp.exp(sims - col_lse) - hit)
        + half_image * (jnp.exp(sims - row_lse) - jnp.where(is_pair, jnp.exp(pair_sims - row_pos), 0.0))
    ).astype(BF16)
    first_image = (me_d * n_mp + me_m) * items
    own_rows = lax.dynamic_slice_in_dim(grad_sims, first_image, items, axis=0)
    own_cols = lax.dynamic_slice_in_dim(grad_sims, first_image * captions, text_n, axis=1)
    grad_image_unit = matmul(own_rows, all_text) * SIM_SCALE
    grad_text_unit = times_cols(own_cols, all_image) * SIM_SCALE
    grad_image_raw = jax.vjp(unit_rows, image_raw)[1](grad_image_unit)[0]
    grad_image_all = (
        jnp.broadcast_to((grad_image_raw / NQ)[:, None, :], (items, NQ, emb)).reshape(query_n, emb).astype(BF16)
    )
    grad_vision = times_cols(query_out, grad_image_all)
    grad_text_raw = jax.vjp(unit_rows, text_raw)[1](grad_text_unit)[0].astype(BF16)
    grad_text = times_cols(cls_rows, grad_text_raw)
    query_grad = times_rows(grad_image_all, w_vision).reshape(items, NQ, width)
    spread_text = jnp.einsum(
        "ics,ice->ise", picker, grad_text_raw.reshape(items, captions, emb), preferred_element_type=F32
    ).astype(BF16)
    spread = times_rows(spread_text.reshape(tokens_n, emb), w_text).reshape(items, seq_len, width)
    query_pad = jnp.concatenate([query_grad, jnp.zeros((items, seq_len - NQ, width), F32)], axis=1)
    grad_items = (cotangent.astype(F32) + spread + query_pad).reshape(tokens_n, width)
    grad_resid_three, grad_gain_three, grad_shift_three = jax.vjp(layer_norm, resid_three, gain[2], shift[2])[1](grad_items)
    grad_branch_three = grad_resid_three.astype(BF16)
    grad_down_t = times_cols(grad_branch_three, activation)
    grad_activation = matmul(grad_branch_three, w_down_t)
    grad_up_value = jax.vjp(gelu_exact, up_value)[1](grad_activation)[0].astype(BF16)
    grad_up = times_cols(normed_two_b, grad_up_value)
    grad_normed_two = grad_resid_three + times_rows(grad_up_value, w_up)
    grad_two_items = grad_normed_two.reshape(items, seq_len, width)
    grad_two_query = grad_two_items[:, :NQ].reshape(query_n, width)
    grad_resid_two, grad_gain_two, grad_shift_two = jax.vjp(layer_norm, resid_two, gain[1], shift[1])[1](grad_two_query)
    grad_branch_two = grad_resid_two.astype(BF16)
    grad_cross_out_t = times_cols(grad_branch_two, cross_flat)
    grad_cross_mixed = matmul(grad_branch_two, w_cross_out_t).astype(BF16).reshape(items, NQ, heads, HEAD_DIM)
    grad_cross_q, grad_cross_k, grad_cross_v = attend_backward(
        cross_q, cross_k, cross_v, None, cross_lse, grad_cross_mixed
    )
    grad_cross_q = grad_cross_q.reshape(query_n, width)
    grad_cross_query = times_cols(first_query_b, grad_cross_q)
    grad_first_query = grad_resid_two + times_rows(grad_cross_q, w_query)
    grad_cross_k = grad_cross_k.reshape(feat_n, width)
    grad_cross_v = grad_cross_v.reshape(feat_n, width)
    grad_feats = (
        (times_rows(grad_cross_k, w_kv[0]) + times_rows(grad_cross_v, w_kv[1])).astype(BF16).reshape(feats.shape)
    )
    grad_feats_far = lax.ppermute(grad_feats, "mp", [(i, i ^ 1) for i in range(n_mp)])
    grad_kv = [times_cols(feat_flat, grad_cross_k), times_cols(feat_flat, grad_cross_v)]
    grad_one = jnp.concatenate(
        [grad_first_query.reshape(items, NQ, width), grad_two_items[:, NQ:]], axis=1
    ).reshape(tokens_n, width)
    grad_resid_one, grad_gain_one, grad_shift_one = jax.vjp(layer_norm, resid_one, gain[0], shift[0])[1](grad_one)
    grad_branch_one = grad_resid_one.astype(BF16)
    grad_self_out_t = times_cols(grad_branch_one, mixed)
    grad_mixed = matmul(grad_branch_one, w_out_t).astype(BF16).reshape(shape4)
    grad_heads = attend_backward(q, k, v, allowed, self_lse, grad_mixed)
    grad_heads = [g.reshape(tokens_n, width) for g in grad_heads]
    grad_qkv = [times_cols(tokens, g) for g in grad_heads]
    grad_tokens = grad_resid_one
    for j in range(3):
        grad_tokens = grad_tokens + times_rows(grad_heads[j], w_qkv[j])
    grad_hidden = grad_tokens.astype(BF16).reshape(hidden.shape)

    def narrow(value, size):
        return jnp.transpose(value.reshape(n_dp, size, n_mp, -1, lane), (2, 0, 3, 1, 4)).reshape(n_mp, n_dp, -1, lane)

    def halves(value):
        return jnp.transpose(value.reshape(n_dp, rows, n_mp, half_emb), (2, 0, 1, 3))

    norm_grads = jnp.stack(
        [grad_gain_one, grad_gain_two, grad_gain_three, grad_shift_one, grad_shift_two, grad_shift_three], axis=1
    ).reshape(1, n_dp, rows, 6)
    norm_grads = jnp.concatenate([norm_grads] + [jnp.zeros_like(norm_grads)] * (n_mp - 1), axis=0)
    misc_grad = jnp.concatenate(
        [
            halves(grad_vision), halves(grad_text), norm_grads,
            jnp.zeros((n_mp, n_dp, rows, lane - 2 * half_emb - 6), F32),
        ],
        axis=3,
    )
    packed_grad = jnp.concatenate(
        [
            value.astype(BF16)
            for value in [narrow(g, rows) for g in grad_qkv]
            + [narrow(grad_cross_query, rows), narrow(grad_self_out_t, rows), misc_grad]
            + [narrow(g, rows_kv) for g in grad_kv]
            + [narrow(grad_cross_out_t, rows), narrow(grad_up, rows), narrow(grad_down_t, rows)]
        ],
        axis=2,
    ).reshape(n_mp * n_dp, places[-1], lane)
    summed = lax.psum_scatter(packed_grad, both, scatter_dimension=0, tiled=False).astype(F32)

    def share(first, last):
        return summed[places[first] : places[last]]

    def uncut(value):
        return jnp.moveaxis(value.reshape(pieces, rows, lane), 0, 1).reshape(rows, pieces * lane)

    misc_share = share(5, 6).astype(BF16)
    misc_far = lax.ppermute(misc_share, "mp", [(i, i ^ 1) for i in range(n_mp)])
    low = jnp.where(me_m == 0, misc_share, misc_far).astype(F32)
    high = jnp.where(me_m == 0, misc_far, misc_share).astype(F32)
    norm_share = low[:, 2 * half_emb : 2 * half_emb + 6].T

    def whole(own, far):
        low_part = jnp.where(me_m == 0, own, far)
        high_part = jnp.where(me_m == 0, far, own)
        return jnp.concatenate([low_part, high_part], axis=0)

    def exchanged(value):
        return whole(value, lax.ppermute(value, "mp", [(i, i ^ 1) for i in range(n_mp)]))

    return (
        contrast_loss,
        exchanged(block_items),
        exchanged(grad_hidden),
        whole(grad_feats, grad_feats_far),
        share(0, 3).reshape(3, rows, lane),
        share(4, 5).T,
        share(3, 4),
        share(6, 8).reshape(2, rows_kv, lane),
        share(8, 9).T,
        uncut(share(9, 9 + pieces)),
        uncut(share(9 + pieces, 9 + 2 * pieces)).T,
        jnp.concatenate([low[:, :half_emb], high[:, :half_emb]], axis=1),
        jnp.concatenate([low[:, half_emb : 2 * half_emb], high[:, half_emb : 2 * half_emb]], axis=1),
        norm_share[:3],
        norm_share[3:],
    )


def solution(mesh):
    n_dp, n_mp = mesh.shape["dp"], mesh.shape["mp"]

    def body(*args):
        return shards(n_dp, n_mp, *args)

    return jax.shard_map(
        body,
        mesh=mesh,
        in_specs=(
            P("dp", None, None),
            P("dp", None, None),
            P("dp", None),
            P("dp"),
            P("dp", None, None),
            P(None, "dp", "mp"),
            P("mp", "dp"),
            P("dp", "mp"),
            P(None, "dp", "mp"),
            P("mp", "dp"),
            P("dp", "mp"),
            P("mp", "dp"),
            P("dp", None),
            P("dp", None),
            P(None, "dp"),
            P(None, "dp"),
        ),
        out_specs=(
            P(),
            P("dp", None, None),
            P("dp", None, None),
            P("dp", None, None),
            P(None, "dp", "mp"),
            P("mp", "dp"),
            P("dp", "mp"),
            P(None, "dp", "mp"),
            P("mp", "dp"),
            P("dp", "mp"),
            P("mp", "dp"),
            P("dp", None),
            P("dp", None),
            P(None, "dp"),
            P(None, "dp"),
        ),
        check_vma=False,
    )
```

time: 1590 us -> 821 us (0.52)
  waiting for transfers between devices: 1040 us -> 300 us
  blocking collectives: 227 us -> 81.1 us
  local copies, waits for them, and re-layouts: 135 us -> 256 us
    reduce_scatter x7 -> x1, waiting for transfers between devices: 458 us -> 99.7 us  [shards(): lax.psum_scatter(packed_grad, both, scatter_dimension=0, tiled=False)]
    psum x7 -> x0, waiting for transfers between devices: 297 us -> none  [the longest x6 152 us: half_sum(): return lax.psum(value, 'mp')]
    unnamed x24 -> x2, waiting for transfers between devices: 217 us -> 0.03 us
    all_gather x9 -> x1, blocking collectives: 184 us -> 66.8 us  [shards(): lax.all_gather(jnp.concatenate([image_b, text_b], axis=0), ('dp', 'mp'),...]
    ppermute x0 -> x4, waiting for transfers between devices: none -> 91.7 us  [the longest x2 91.7 us: exchanged(): lax.ppermute(value, 'mp', [(i, i ^ 1) for i in range(n_mp)])]
    reshape x16 -> x42, local copies, waits for them, and re-layouts: 23.9 us -> 99.6 us  [the longest x4 24.1 us: shards(): matmul(feat_flat, w).astype(BF16).reshape(shape_vis)]
    convert_element_type x5 -> x21, local copies, waits for them, and re-layouts: 1.87 us -> 39.1 us  [the longest x11 23.5 us: shards(): value.astype(BF16)]
    all_gather x4 -> x1, waiting for transfers between devices: 71.3 us -> 108 us  [shards(): lax.all_gather(packed, both, axis=0, tiled=False)]
  transfers between devices with their start and end apart: 21 -> 6, of which waited for: 17 -> 4; matrix products, arithmetic and copies ran while one was open for 12% -> 7% of each run, Pallas kernels for 0% -> 0%
where the time goes in v1:
time: 821 us; the launch traced here: 814 us
  waiting for transfers between devices  300 us (37%)
  local copies, waits for them, and re-layouts  256 us (31%)
  matrix products  110 us (13%)
  blocking collectives  81.1 us (10%)
  other arithmetic  43.4 us (5%)
  between operations  19.4 us (2%)
    all_gather x1, waiting for transfers between devices, shards(): lax.all_gather(packed, both, axis=0, tiled=False)  108 us
    reduce_scatter x1, waiting for transfers between devices, shards(): lax.psum_scatter(packed_grad, both, scatter_dimension=0, tiled=False)  99.7 us
    ppermute x2, waiting for transfers between devices, exchanged(): lax.ppermute(value, 'mp', [(i, i ^ 1) for i in range(n_mp)])  91.7 us
    all_gather x1, blocking collectives, shards(): lax.all_gather(jnp.concatenate([image_b, text_b], axis=0), ('dp', 'mp'),...  66.8 us
    unnamed x353, local copies, waits for them, and re-layouts  41.2 us
    dot_general x13, matrix products, matmul(): return jnp.dot(left, right, preferred_element_type=F32)  40.1 us
    dot_general x13, matrix products, times_rows(): lax.dot_general(left, right, (((1,), (1,)), ((), ())), preferred_element_...  26.4 us
    reshape x4, local copies, waits for them, and re-layouts, shards(): matmul(feat_flat, w).astype(BF16).reshape(shape_vis)  24.1 us
  transfers between devices with their start and end apart: 6, of which 4 were waited for; matrix products, arithmetic and copies ran while one was open for 7% of the time, Pallas kernels for 0%

profile of v1, /device:TPU:0, one launch (start us, length us, event | category | flops | bytes accessed | tf_op | source)
XLA Modules:
  0.0 813.7 jit_solution(1919220970216209199)
XLA Ops:
  27.6 5.3 copy.439
  35.0 14.3 %all-reduce.3 = s32[384]{0:T(512)} all-reduce(s32[384]{0:T(512)S(1)} %dynamic-update-slice), channel_id=1, replica_groups=mesh['dp'=16,'mp'=2] {'dp'}, use_global_device_ids=true, to_apply=%add.3 | all-reduce | flops 384 | bytes 3072
  50.2 108.4 %all-gather.4.cloned.1.call-done = bf16[28672,384]{1,0:T(8,128)(2,1)} async-done(((bf16[896,384]{1,0:T(8,128)(2,1)}), bf16[28672,384]{1,0:T(8,128)(2,1)}) %all-gather.4.cloned.1.call-update) | async-done | bytes 22020112 | tf_op jit(solution)/shard_map/all_gather | solution.py:131
  158.5 12.4 %fusion.116 = (bf16[2,16,48,384]{3,2,1,0:T(8,128)(2,1)}, bf16[2,16,48,384]{3,2,1,0:T(8,128)(2,1)}, bf16[2,16,48,384]{3,2,1,0:T(8,128)(2,1)}, bf16[2,16,48,384]{3...) fusion(bf16[2,16,896,384]{3,2,1,0:T(8,128)(2,1)} %bitcast.495), kind=kLoop, calls=%fused_computation.325 | loop fusion | bytes 35389440 | tf_op jit(solution)/shard_map/slice | solution.py:134
  170.9 4.8 fusion.117
  203.7 6.5 convolution_convert_fusion.2
  210.1 6.1 reshape.764
  216.2 6.8 copy.384
  225.6 5.2 convolution_convert_fusion.1
  230.8 4.4 reshape.765
  235.2 6.8 copy.383
  282.3 9.2 %multiply_convert_fusion.1 = (bf16[256,3072]{1,0:T(8,128)(2,1)S(1)}, f32[256,3072]{1,0:T(8,128)}, f32[256,3072]{1,0:T(8,128)}) fusion(bf16[256,768]{1,0:T(8,128)(2,1)S(1)} %bitcast.608, bf16[768,3072]{0,1:T(8,128)(2,1)S(1)} %bitcast.541), kind=kOutput, calls=%fused_computation.40 | convolution fusion | flops 1259077632 | bytes 12976128 | tf_op jit(solution)/shard_map/dot_general | solution.py:32
  309.8 66.8 %all-gather.1 = bf16[512,256]{1,0:T(8,128)(2,1)S(1)} all-gather(bf16[16,256]{1,0:T(8,128)(2,1)S(1)} %pad_maximum_fusion.9), channel_id=3, replica_groups=mesh['dp'=16,'mp'=2] {'dp','mp'}, dimensions={0}, use_global_device_ids=true | all-gather | bytes 270336 | tf_op jit(solution)/shard_map/all_gather | solution.py:194
  408.3 11.2 %fusion.6 = (bf16[3072,256]{0,1:T(8,128)(2,1)}, f32[256,3072]{1,0:T(8,128)S(1)}) fusion(f32[256,3072]{1,0:T(8,128)S(1)} %copy-done.157, bf16[768,3072]{0,1:T(8,128)(2,1)} %bitcast.546, f32[256,768]{1,0:T(8,128)S(1)} %get-tuple-element.116, f32[256]{0:T(256)S(1)} %negate_multiply_fusion.2), kind=kOutput, calls=%fused_computation.17 | convolution fusion | flops 1264975872 | bytes 13370368 | tf_op jit(solution)/shard_map/dot_general | solution.py:32
  483.0 5.0 reshape.714
  491.2 4.8 reshape.715
  512.3 5.0 convert_bitcast_fusion.3
  539.4 9.8 %convert_element_type.441 = bf16[16,48,2,4,384]{4,3,2,1,0:T(4,128)(2,1)} reshape(bf16[768,3072]{1,0:T(8,128)(2,1)} %convolution_convert_fusion) | data formatting | bytes 9437184 | tf_op jit(solution)/shard_map/convert_element_type | solution.py:295
  570.6 4.3 fusion.130
  575.0 4.5 fusion
  579.4 4.5 reshape.716
  583.9 5.0 copy.420
  594.1 88.7 %collective-permute-done = bf16[4,64,768]{2,1,0:T(8,128)(2,1)S(1)} collective-permute-done((bf16[4,64,768]{2,1,0:T(8,128)(2,1)S(1)}, bf16[4,64,768]{2,1,0:T(8,128)(2,1)S(1)}, u32[]{:S(2)}, u32[]{:S(2)}) %collective-permute-start) | collective-permute-done | bytes 393248 | tf_op jit(solution)/shard_map/ppermute | solution.py:323
  695.0 99.7 %reduce-scatter.2.cloned.1.call-done = bf16[1,896,384]{2,1,0:T(8,128)(2,1)} async-done(((bf16[32,896,384]{2,1,0:T(8,128)(2,1)}), bf16[1,896,384]{2,1,0:T(8,128)(2,1)}) %reduce-scatter.2.cloned.1.call-update) | async-done | bytes 688144 | tf_op jit(solution)/shard_map/reduce_scatter | solution.py:303
  (602 shorter events, 295.0 us)
Async XLA Ops:
  7.2 19.4 %copy-start = (bf16[8,64,768]{2,1,0:T(8,128)(2,1)S(1)}, bf16[8,64,768]{2,1,0:T(8,128)(2,1)}, u32[]{:S(2)}) copy-start(bf16[8,64,768]{2,1,0:T(8,128)(2,1)} %param.16) | copy-start | bytes 2359300
  7.2 151.3 %all-gather.4.cloned.1.call-start = ((), (), s32[]{:S(2)}) async-start(), calls=%async_computation.2 | async-start | bytes 22708224 | tf_op jit(solution)/shard_map/all_gather | solution.py:131
  16.0 778.7 %reduce-scatter.2.cloned.1.call-start = ((), (), s32[]{:S(2)}) async-start(), calls=%async_computation.1 | async-start | bytes 22708224 | tf_op jit(solution)/shard_map/reduce_scatter | solution.py:303
  26.6 269.1 %copy-start.120 = (s32[4,3]{1,0:T(4,128)}, s32[4,3]{1,0:T(4,128)S(1)}, u32[]{:S(2)}) copy-start(s32[4,3]{1,0:T(4,128)S(1)} %copy.396) | copy-start | bytes 148
  197.6 58.8 %copy-start.106 = (f32[768]{0:T(1024)}, f32[768]{0:T(1024)S(1)}, u32[]{:S(2)}) copy-start(f32[768]{0:T(1024)S(1)} %get-tuple-element.108) | copy-start | bytes 9220
  197.6 97.8 %copy-start.102 = (f32[768]{0:T(1024)}, f32[768]{0:T(1024)S(1)}, u32[]{:S(2)}) copy-start(f32[768]{0:T(1024)S(1)} %get-tuple-element.105) | copy-start | bytes 9220
  197.6 97.8 %copy-start.111 = (f32[768]{0:T(1024)}, f32[768]{0:T(1024)S(1)}, u32[]{:S(2)}) copy-start(f32[768]{0:T(1024)S(1)} %get-tuple-element.106) | copy-start | bytes 9220
  282.2 9.2 %copy-start.43 = (bf16[2,4,768,384]{2,3,1,0:T(8,128)(2,1)}, bf16[2,4,768,384]{2,3,1,0:T(8,128)(2,1)S(1)}, u32[]{:S(2)}) copy-start(bf16[2,4,768,384]{2,3,1,0:T(8,128)(2,1)S(1)} %pad_maximum_fusion.1) | copy-start | bytes 14155780
  406.6 12.9 %slice-start.2 = ((s8[4718592]{0:T(1024)(128)(4,1)}), s8[4194304]{0:T(1024)(128)(4,1)S(1)}, s32[]{:S(2)}) async-start(s8[4718592]{0:T(1024)(128)(4,1)} %bitcast.542), calls=%async_computation.5 | async-start | bytes 8388608
  408.3 11.3 %copy-start.50 = (f32[256,768]{1,0:T(8,128)}, f32[256,768]{1,0:T(8,128)S(1)}, u32[]{:S(2)}) copy-start(f32[256,768]{1,0:T(8,128)S(1)} %get-tuple-element.116) | copy-start | bytes 2359300
  408.3 11.2 %copy-start.128 = (f32[256]{0:T(256)}, f32[256]{0:T(256)S(1)}, u32[]{:S(2)}) copy-start(f32[256]{0:T(256)S(1)} %negate_multiply_fusion.2) | copy-start | bytes 3076
  408.3 11.2 %slice-start.3 = ((s8[4718592]{0:T(1024)(128)(4,1)}), s8[524288]{0:T(1024)(128)(4,1)S(1)}, s32[]{:S(2)}) async-start(s8[4718592]{0:T(1024)(128)(4,1)} %bitcast.542), calls=%async_computation.6 | async-start | bytes 1048576
  408.3 11.2 %copy-start.156 = (f32[256,3072]{1,0:T(8,128)S(1)}, f32[256,3072]{1,0:T(8,128)}, u32[]{:S(2)}) copy-start(f32[256,3072]{1,0:T(8,128)} %get-tuple-element.125) | copy-start | bytes 9437188
  470.4 9.4 %copy-start.25 = (bf16[4,257,12,64]{1,3,2,0:T(8,128)(2,1)S(1)}, bf16[4,257,12,64]{1,3,2,0:T(8,128)(2,1)}, u32[]{:S(2)}) copy-start(bf16[4,257,12,64]{1,3,2,0:T(8,128)(2,1)} %fusion.29) | copy-start | bytes 4737028
  588.9 99.5 %collective-permute-start.2 = (bf16[4,257,1408]{2,0,1:T(4,128)(2,1)}, bf16[4,257,1408]{2,0,1:T(4,128)(2,1)}, u32[]{:S(2)}, u32[]{:S(2)}) collective-permute-start(bf16[4,257,1408]{2,0,1:T(4,128)(2,1)} %copy.420), channel_id=1, source_target_pairs={{0,1},{1,0},{2,3},{3,2},{4,5},{5,4},{6,7},{7,6},{8,9},{9,8},{10,11... | collective-permute-start | bytes 8684552 | tf_op jit(solution)/shard_map/ppermute | solution.py:259
  589.2 93.7 %collective-permute-start = (bf16[4,64,768]{2,1,0:T(8,128)(2,1)S(1)}, bf16[4,64,768]{2,1,0:T(8,128)(2,1)S(1)}, u32[]{:S(2)}, u32[]{:S(2)}) collective-permute-start(bf16[4,64,768]{2,1,0:T(8,128)(2,1)S(1)} %bitcast.573), channel_id=1, source_target_pairs={{0,1},{1,0},{2,3},{3,2},{4,5},{5,4},{6,7},{7,6},{8,9},{9,8},{10,11... | collective-permute-start | bytes 1179656 | tf_op jit(solution)/shard_map/ppermute | solution.py:323
  591.5 91.4 %copy-start.103 = (f32[768]{0:T(1024)S(1)}, f32[768]{0:T(1024)}, u32[]{:S(2)}) copy-start(f32[768]{0:T(1024)} %copy-done.102) | copy-start | bytes 9220
  591.5 91.4 %copy-start.110 = (f32[256]{0:T(256)S(1)}, f32[256]{0:T(256)}, u32[]{:S(2)}) copy-start(f32[256]{0:T(256)} %copy-done.109) | copy-start | bytes 3076
  591.5 91.4 %copy-start.112 = (f32[768]{0:T(1024)S(1)}, f32[768]{0:T(1024)}, u32[]{:S(2)}) copy-start(f32[768]{0:T(1024)} %copy-done.111) | copy-start | bytes 9220
  591.5 91.4 %copy-start.115 = (f32[256]{0:T(256)S(1)}, f32[256]{0:T(256)}, u32[]{:S(2)}) copy-start(f32[256]{0:T(256)} %copy-done.114) | copy-start | bytes 3076
  592.6 94.8 %collective-permute-start.1 = (bf16[4,64,768]{2,1,0:T(8,128)(2,1)S(1)}, bf16[4,64,768]{2,1,0:T(8,128)(2,1)S(1)}, u32[]{:S(2)}, u32[]{:S(2)}) collective-permute-start(bf16[4,64,768]{2,1,0:T(8,128)(2,1)S(1)} %bitcast.589), channel_id=1, source_target_pairs={{0,1},{1,0},{2,3},{3,2},{4,5},{5,4},{6,7},{7,6},{8,9},{9,8},{10,11... | collective-permute-start | bytes 1179656 | tf_op jit(solution)/shard_map/ppermute | solution.py:323
  594.1 94.3 %copy-start.4 = (bf16[4,257,1408]{2,1,0:T(8,128)(2,1)S(1)}, bf16[4,257,1408]{2,1,0:T(8,128)(2,1)}, u32[]{:S(2)}) copy-start(bf16[4,257,1408]{2,1,0:T(8,128)(2,1)} %reshape.716) | copy-start | bytes 8684548
  794.7 10.8 %copy-start.1 = (bf16[8,64,768]{2,1,0:T(8,128)(2,1)S(1)}, bf16[8,64,768]{2,1,0:T(8,128)(2,1)}, u32[]{:S(2)}) copy-start(bf16[8,64,768]{2,1,0:T(8,128)(2,1)} %param.16) | copy-start | bytes 2359300
  795.6 7.2 collective-permute-start.3
  (144 other events, 502.0 us)
Sparse Core Ops, SparseCore 0:
  16.1 142.3 all-gather.3
  569.1 225.4 reduce-scatter.1

commit v2 on v1

v2 whole, which is shorter than its diff:
```python
import functools

import jax
import jax.numpy as jnp
from jax import lax
from jax.experimental import pallas as pl
from jax.experimental.pallas import tpu as pltpu
from jax.sharding import PartitionSpec as P

HEAD_DIM = 64
NQ = 32
EPS_NORM = 1e-06
EPS_UNIT = 1e-06
SIM_SCALE = 16.0
MASKED = -1000000000.0
F32 = jnp.float32
BF16 = jnp.bfloat16


def dot(left, right):
    return jnp.dot(left, right, preferred_element_type=F32)


def dot_nt(left, right):
    return lax.dot_general(left, right, (((1,), (1,)), ((), ())), preferred_element_type=F32)


def dot_tn(left, right):
    return lax.dot_general(left, right, (((0,), (0,)), ((), ())), preferred_element_type=F32)


def iota(shape, dim):
    return lax.broadcasted_iota(jnp.int32, shape, dim)


def norm_forward(value, gain, shift):
    mean = jnp.mean(value, -1, keepdims=True)
    centered = value - mean
    scale = lax.rsqrt(jnp.mean(centered * centered, -1, keepdims=True) + EPS_NORM)
    return centered * scale * gain + shift


def norm_backward(value, grad, gain):
    mean = jnp.mean(value, -1, keepdims=True)
    centered = value - mean
    scale = lax.rsqrt(jnp.mean(centered * centered, -1, keepdims=True) + EPS_NORM)
    unit = centered * scale
    inner = grad * gain
    back = scale * (inner - jnp.mean(inner, -1, keepdims=True) - unit * jnp.mean(inner * unit, -1, keepdims=True))
    return back, jnp.sum(grad * unit, 0, keepdims=True), jnp.sum(grad, 0, keepdims=True)


def low_lanes(rows):
    return iota((rows, 2 * HEAD_DIM), 1) < HEAD_DIM


def pair_rows(value):
    low = low_lanes(value.shape[0])
    value = value.astype(F32)
    zero = jnp.zeros_like(value)
    return jnp.concatenate([jnp.where(low, value, zero), jnp.where(low, zero, value)], axis=0).astype(BF16)


def merge_rows(value):
    half = value.shape[0] // 2
    return jnp.where(low_lanes(half), value[:half], value[half:])


def probabilities(queries, keys, keep):
    scores = dot_nt(queries, keys) * HEAD_DIM ** (-0.5)
    scores = jnp.where(keep, scores, MASKED)
    expo = jnp.exp(scores - jnp.max(scores, -1, keepdims=True))
    return expo / jnp.sum(expo, -1, keepdims=True)


def attention_back(queries, keys, values, grads, keep):
    probs = probabilities(queries, keys, keep)
    grad_probs = dot_nt(grads, values)
    grad_scores = (probs * (grad_probs - jnp.sum(grad_probs * probs, -1, keepdims=True))).astype(BF16)
    scale = HEAD_DIM ** (-0.5)
    grad_q = merge_rows(dot(grad_scores, keys)) * scale
    grad_k = dot_tn(grad_scores, queries) * scale
    grad_v = dot_tn(probs.astype(BF16), grads)
    return grad_q.astype(BF16), grad_k.astype(BF16), grad_v.astype(BF16)


def same_segment(lens_ref, item, rows, keys):
    first = NQ + lens_ref[item, 0]
    second = first + lens_ref[item, 1]

    def label(place):
        return (
            (place >= NQ).astype(jnp.int32) + (place >= first).astype(jnp.int32) + (place >= second).astype(jnp.int32)
        )

    return label(iota((rows, keys), 0) & (keys - 1)) == label(iota((rows, keys), 1))


def aligned(index, step):
    return pl.ds(pl.multiple_of(index * step, step), step)


def fetch(weights, part, chunk_rows, target, sems, first):
    lane = weights.shape[3]
    copies = []
    for m in range(weights.shape[0]):
        copies.append(
            pltpu.make_async_copy(
                weights.at[m, :, pl.ds(part * chunk_rows, chunk_rows), :],
                target.at[:, :, pl.ds(m * lane, lane)],
                sems.at[first + m],
            )
        )
        copies[-1].start()
    return copies


def fetch_tile(weights, part, chunk_rows, target, lane_at, m, sem):
    lane = weights.shape[3]
    copy = pltpu.make_async_copy(
        weights.at[m, :, pl.ds(part * chunk_rows, chunk_rows), :], target.at[:, :, pl.ds(lane_at, lane)], sem
    )
    copy.start()
    return copy


def flat(ref_value):
    return ref_value.reshape(-1, ref_value.shape[-1])


def store_halves(out_ref, row_at, chunk_rows, stored, value, m_of, d_of):
    n_mp, n_chunk, _, lane = out_ref.shape
    if stored != chunk_rows:
        value = jnp.concatenate([value, jnp.zeros((stored - chunk_rows, value.shape[1]), value.dtype)], axis=0)
    for m in range(value.shape[1] // lane):
        for d in range(n_chunk):
            out_ref[m_of(m), d_of(d), pl.ds(row_at, stored), :] = value[
                d * chunk_rows : d * chunk_rows + stored, m * lane : (m + 1) * lane
            ].astype(BF16)


def self_forward(lens_ref, hid_ref, norm_ref, w_ref, qkv_ref, mixed_ref, resid_ref, normed_ref, fq_ref, cq_ref, wbuf, sems):
    items = lens_ref.shape[0]
    seq = hid_ref.shape[0] // items
    width = hid_ref.shape[1]
    rc = wbuf.shape[2]
    copies = [fetch(w_ref, p, rc, wbuf.at[p], sems, p * w_ref.shape[0]) for p in range(5)]
    x = hid_ref[...]
    for j in range(3):
        for c in copies[j]:
            c.wait()
        qkv_ref[j] = dot(x, flat(wbuf[j])).astype(BF16)

    def one(item, carry):
        rows = aligned(item, seq)
        keep = same_segment(lens_ref, item, 2 * seq, seq)
        for p in range(width // 128):
            lanes = pl.ds(p * 128, 128)
            probs = probabilities(pair_rows(qkv_ref[0, rows, lanes]), qkv_ref[1, rows, lanes], keep)
            mixed_ref[rows, lanes] = merge_rows(dot(probs.astype(BF16), qkv_ref[2, rows, lanes])).astype(BF16)
        return carry

    lax.fori_loop(0, items, one, 0)
    for p in (3, 4):
        for c in copies[p]:
            c.wait()
    resid = x.astype(F32) + dot_nt(mixed_ref[...], flat(wbuf[4]))
    resid_ref[...] = resid
    normed = norm_forward(resid, norm_ref[0:1], norm_ref[3:4])
    normed_ref[...] = normed
    query = jnp.concatenate([normed[i * seq : i * seq + NQ] for i in range(items)], axis=0).astype(BF16)
    fq_ref[...] = query
    cq_ref[...] = dot(query, flat(wbuf[3])).astype(BF16)


def cross_forward(
    vis_len, normed_ref, cq_ref, feat_ref, kvw_ref, norm_ref, w_ref, kv_ref, mixed_ref, resid_ref, two_ref, wbuf, sems
):
    items = cq_ref.shape[0] // NQ
    seq = normed_ref.shape[0] // items
    width = cq_ref.shape[1]
    vis_pad = feat_ref.shape[0] // items
    copies = fetch(w_ref, 5, wbuf.shape[1], wbuf, sems, 0)
    step = 256
    for j in range(2):

        def project(n, carry, j=j):
            lanes = aligned(n, step)
            kv_ref[j, :, lanes] = dot(feat_ref[...], kvw_ref[j, :, lanes]).astype(BF16)
            return carry

        lax.fori_loop(0, width // step, project, 0)

    def one(item, carry):
        rows, keys = aligned(item, NQ), aligned(item, vis_pad)
        keep = iota((2 * NQ, vis_pad), 1) < vis_len
        for p in range(width // 128):
            lanes = pl.ds(p * 128, 128)
            probs = probabilities(pair_rows(cq_ref[rows, lanes]), kv_ref[0, keys, lanes], keep)
            mixed_ref[rows, lanes] = merge_rows(dot(probs.astype(BF16), kv_ref[1, keys, lanes])).astype(BF16)
        return carry

    lax.fori_loop(0, items, one, 0)
    for c in copies:
        c.wait()
    first = jnp.concatenate([normed_ref[i * seq : i * seq + NQ] for i in range(items)], axis=0)
    resid = first + dot_nt(mixed_ref[...], flat(wbuf[...]))
    resid_ref[...] = resid
    normed = norm_forward(resid, norm_ref[1:2], norm_ref[4:5])
    for i in range(items):
        two_ref[i * seq : i * seq + NQ] = normed[i * NQ : (i + 1) * NQ]
        two_ref[i * seq + NQ : (i + 1) * seq] = normed_ref[i * seq + NQ : (i + 1) * seq]


def picker_of(lens_ref, rows, seq):
    items, captions = lens_ref.shape
    shape = (rows, items * seq)
    row = iota(shape, 0)
    target = jnp.full(shape, -1, jnp.int32)
    for i in range(items):
        start = i * seq + NQ
        for c in range(captions):
            target = jnp.where(row == i * captions + c, start, target)
            start = start + lens_ref[i, c]
    return (target == iota(shape, 1)).astype(F32).astype(BF16)


def unit_forward(value):
    return value * lax.rsqrt(jnp.sum(value * value, -1, keepdims=True) + EPS_UNIT)


def unit_backward(value, grad):
    scale = lax.rsqrt(jnp.sum(value * value, -1, keepdims=True) + EPS_UNIT)
    return grad * scale - value * (scale * scale * scale * jnp.sum(grad * value, -1, keepdims=True))


def ffn_fetch(w_ref, up_buf, down_buf, sems):
    n_mp, lane = w_ref.shape[0], w_ref.shape[3]
    tiles, _, rc, tile = up_buf.shape
    per = tile // lane
    pieces = tiles * per // n_mp
    ups, downs = [[] for _ in range(tiles)], [[] for _ in range(tiles)]
    for t in range(tiles):
        for s in range(per):
            piece = t * per + s
            m, p = piece // pieces, piece % pieces
            ups[t].append(fetch_tile(w_ref, 6 + p, rc, up_buf.at[t], s * lane, m, sems.at[2 * piece]))
            downs[t].append(fetch_tile(w_ref, 6 + pieces + p, rc, down_buf.at[t], s * lane, m, sems.at[2 * piece + 1]))
    return ups, downs


def misc_fetch(w_ref, part, misc_buf, sems):
    rc = misc_buf.shape[2]
    copies = []
    for m in range(w_ref.shape[0]):
        copies.append(
            pltpu.make_async_copy(w_ref.at[m, :, pl.ds(part * rc, rc), :], misc_buf.at[m], sems.at[m])
        )
        copies[-1].start()
    return copies


def ffn_forward(
    lens_ref, two_ref, norm_ref, w_ref, up_ref, act_ref, resid_ref, block_ref, cls_ref, iraw_ref, traw_ref, emb_ref,
    up_buf, down_buf, misc_buf, sems, msems,
):
    items, captions = lens_ref.shape
    seq = two_ref.shape[0] // items
    tiles = up_buf.shape[0]
    n_mp, lane = w_ref.shape[0], w_ref.shape[3]
    ups, downs = ffn_fetch(w_ref, up_buf, down_buf, sems)
    miscs = misc_fetch(w_ref, 6 + 2 * (tiles * (up_buf.shape[3] // lane) // n_mp), misc_buf, msems)
    two = two_ref[...]
    two_b = two.astype(BF16)
    resid = two
    for t in range(tiles):
        for c in ups[t]:
            c.wait()
        up = dot(two_b, flat(up_buf[t]))
        up_ref[t] = up
        act = (0.5 * up * (1.0 + lax.erf(up * (0.5**0.5)))).astype(BF16)
        act_ref[t] = act
        for c in downs[t]:
            c.wait()
        resid = resid + dot_nt(act, flat(down_buf[t]))
    resid_ref[...] = resid
    block = norm_forward(resid, norm_ref[2:3], norm_ref[5:6]).astype(BF16)
    block_ref[...] = block
    rows = iraw_ref.shape[0]
    cls = dot(picker_of(lens_ref, rows, seq), block).astype(BF16)
    cls_ref[...] = cls
    query = jnp.concatenate([block[i * seq : i * seq + NQ] for i in range(items)], axis=0)
    for c in miscs:
        c.wait()
    half = iraw_ref.shape[1] // n_mp
    row = iota((rows, half), 0)
    for m in range(n_mp):
        misc = flat(misc_buf[m])
        image = dot(query, misc[:, :half])
        raw = jnp.zeros((rows, half), F32)
        for i in range(items):
            raw = jnp.where(row == i, jnp.sum(image[i * NQ : (i + 1) * NQ], 0, keepdims=True) * (1.0 / NQ), raw)
        iraw_ref[:, m * half : (m + 1) * half] = raw
        traw_ref[:, m * half : (m + 1) * half] = dot(cls, misc[:, half : 2 * half])
    image_b = unit_forward(iraw_ref[...]).astype(BF16)
    text_b = unit_forward(traw_ref[...]).astype(BF16)
    r, c = iota((rows, rows), 0), iota((rows, rows), 1)
    put_image = ((r == c) & (r < items)).astype(F32).astype(BF16)
    put_text = ((r == c + items) & (c < items * captions)).astype(F32).astype(BF16)
    emb_ref[...] = (dot(put_image, image_b) + dot(put_text, text_b)).astype(BF16)


def device_of(place, shift, me):
    place = place >> shift
    relative = ((place >> 3) & 1) + 2 * (place >> 4) + 4 * ((place >> 2) & 1) + 8 * (place & 3)
    return relative ^ me


def contrast(items, captions, me_ref, emb_ref, pair_ref, iraw_ref, traw_ref, loss_ref, gi_ref, gt_ref):
    me = me_ref[0]
    rows = iraw_ref.shape[0]
    n_dev = emb_ref.shape[0] // rows
    shift = rows.bit_length() - 1
    images, texts = n_dev * items, n_dev * captions * items
    emb = emb_ref[...]
    r, c = iota((images, n_dev * rows), 0), iota((images, n_dev * rows), 1)
    slot = c & (rows - 1)
    pick = ((device_of(c, shift, me) * items + slot == r) & (slot < items)).astype(F32).astype(BF16)
    image = dot(pick, emb).astype(BF16)
    r, c = iota((texts, n_dev * rows), 0), iota((texts, n_dev * rows), 1)
    slot = (c & (rows - 1)) - items
    pick = ((device_of(c, shift, me) * (items * captions) + slot == r) & (slot >= 0)).astype(F32).astype(BF16)
    text = dot(pick, emb).astype(BF16)
    sims = dot_nt(image, text) * SIM_SCALE
    is_pair = pair_ref[...] == iota((images, texts), 0)
    col_peak = jnp.max(sims, 0, keepdims=True)
    col_lse = col_peak + jnp.log(jnp.sum(jnp.exp(sims - col_peak), 0, keepdims=True))
    row_peak = jnp.max(sims, 1, keepdims=True)
    row_lse = row_peak + jnp.log(jnp.sum(jnp.exp(sims - row_peak), 1, keepdims=True))
    pair_sims = jnp.where(is_pair, sims, MASKED)
    pos_peak = jnp.max(pair_sims, 1, keepdims=True)
    row_pos = pos_peak + jnp.log(jnp.sum(jnp.exp(pair_sims - pos_peak), 1, keepdims=True))
    col_pos = jnp.sum(jnp.where(is_pair, sims, 0.0), 0, keepdims=True)
    half_image, half_text = 0.5 / images, 0.5 / texts
    loss_ref[...] = half_text * jnp.sum(col_lse - col_pos, axis=1, keepdims=True) + half_image * jnp.sum(
        row_lse - row_pos, axis=0, keepdims=True
    )
    hit = jnp.where(is_pair, 1.0, 0.0)
    grad = (
        half_text * (jnp.exp(sims - col_lse) - hit)
        + half_image * (jnp.exp(sims - row_lse) - jnp.exp(pair_sims - row_pos))
    ).astype(BF16)
    r, c = iota((rows, images), 0), iota((rows, images), 1)
    own = ((c == me * items + r) & (r < items)).astype(F32).astype(BF16)
    grad_image = dot(dot(own, grad).astype(BF16), text) * SIM_SCALE
    r, c = iota((rows, texts), 0), iota((rows, texts), 1)
    own = ((c == me * (items * captions) + r) & (r < items * captions)).astype(F32).astype(BF16)
    grad_text = dot(dot_nt(own, grad).astype(BF16), image) * SIM_SCALE
    gi_ref[...] = (unit_backward(iraw_ref[...], grad_image) * (1.0 / NQ)).astype(BF16)
    gt_ref[...] = unit_backward(traw_ref[...], grad_text).astype(BF16)


def ffn_backward(
    lens_ref, me_ref, gi_ref, gt_ref, block_ref, cls_ref, og_ref, two_ref, resid_ref, up_ref, act_ref, norm_ref, w_ref,
    gtwo_ref, ng_ref, gw_ref, up_buf, down_buf, misc_buf, sems, msems,
):
    items = lens_ref.shape[0]
    seq = two_ref.shape[0] // items
    tokens = two_ref.shape[0]
    tiles, nc, rc, tile = up_buf.shape
    n_mp, lane = w_ref.shape[0], w_ref.shape[3]
    per = tile // lane
    pieces = tiles * per // n_mp
    miscs = misc_fetch(w_ref, 6 + 2 * pieces, misc_buf, msems)
    ups, downs = ffn_fetch(w_ref, up_buf, down_buf, sems)
    rows, emb = gi_ref.shape
    half = emb // n_mp
    gi, gt = gi_ref[...], gt_ref[...]
    r, c = iota((tokens, rows), 0), iota((tokens, rows), 1)
    spread = (((r // seq) == c) & ((r & (seq - 1)) < NQ)).astype(F32).astype(BF16)
    gi_rows = dot(spread, gi).astype(BF16)
    gt_rows = dot_tn(picker_of(lens_ref, rows, seq), gt).astype(BF16)
    for c in miscs:
        c.wait()
    grad = og_ref[...].astype(F32)
    block = block_ref[...]
    cls = cls_ref[...]
    zero = jnp.zeros((rc * nc, lane - 2 * half), F32)
    for m in range(n_mp):
        misc = flat(misc_buf[m])
        lanes = slice(m * half, (m + 1) * half)
        grad = grad + dot_nt(gi_rows[:, lanes], misc[:, :half]) + dot_nt(gt_rows[:, lanes], misc[:, half : 2 * half])
        share = jnp.concatenate([dot_tn(block, gi_rows[:, lanes]), dot_tn(cls, gt[:, lanes]), zero], axis=1)
        store_halves(gw_ref, 2 * pieces * rc, rc, rc, share, lambda _, m=m: m ^ me_ref[1], lambda d: d ^ me_ref[2])
    back, gain_grad, shift_grad = norm_backward(resid_ref[...], grad, norm_ref[2:3])
    ng_ref[...] = jnp.concatenate([gain_grad, shift_grad], axis=0)
    branch = back.astype(BF16)
    two_b = two_ref[...].astype(BF16)
    total = back
    for t in range(tiles):
        for c in downs[t] + ups[t]:
            c.wait()
        up = up_ref[t]
        slope = 0.5 * (1.0 + lax.erf(up * (0.5**0.5))) + up * jnp.exp(-0.5 * up * up) * 0.3989422804014327
        grad_up = (dot(branch, flat(down_buf[t])) * slope).astype(BF16)
        m, p = (t * per) // pieces, (t * per) % pieces
        for s in range(per):
            lanes = slice(s * lane, (s + 1) * lane)
            for base, left, right in ((0, two_b, grad_up), (pieces, branch, act_ref[t])):
                store_halves(
                    gw_ref, (base + p + s) * rc, rc, rc, dot_tn(left, right[:, lanes]),
                    lambda _, m=m: m ^ me_ref[1], lambda d: d ^ me_ref[2],
                )
        total = total + dot_nt(grad_up, flat(up_buf[t]))
    gtwo_ref[...] = total


def cross_backward(
    vis_len, rc, me_ref, gtwo_ref, resid_ref, mixed_ref, cq_ref, fq_ref, kv_ref, kvw_ref, norm_ref, w_ref,
    gone_ref, ng_ref, gkv_ref, gf_ref, gw_ref, wbuf, gq_buf, sems,
):
    items = cq_ref.shape[0] // NQ
    seq = gtwo_ref.shape[0] // items
    width = cq_ref.shape[1]
    vis_pad = kv_ref.shape[1] // items
    wrc = wbuf.shape[2]
    n_mp = w_ref.shape[0]
    copies = [fetch(w_ref, p, wrc, wbuf.at[i], sems, i * n_mp) for i, p in enumerate((5, 3))]
    xor_m, xor_d = (lambda m: m ^ me_ref[1]), (lambda d: d ^ me_ref[2])
    grad = jnp.concatenate([gtwo_ref[i * seq : i * seq + NQ] for i in range(items)], axis=0)
    back, gain_grad, shift_grad = norm_backward(resid_ref[...], grad, norm_ref[1:2])
    ng_ref[...] = jnp.concatenate([gain_grad, shift_grad], axis=0)
    branch = back.astype(BF16)
    for c in copies[0]:
        c.wait()
    grad_mixed = dot(branch, flat(wbuf[0])).astype(BF16)
    gq_buf[...] = grad_mixed

    def one(item, carry):
        rows, keys = aligned(item, NQ), aligned(item, vis_pad)
        keep = iota((2 * NQ, vis_pad), 1) < vis_len
        for p in range(width // 128):
            lanes = pl.ds(p * 128, 128)
            grad_q, grad_k, grad_v = attention_back(
                pair_rows(cq_ref[rows, lanes]), kv_ref[0, keys, lanes], kv_ref[1, keys, lanes],
                pair_rows(gq_buf[rows, lanes]), keep,
            )
            gq_buf[rows, lanes] = grad_q
            gkv_ref[0, keys, lanes] = grad_k
            gkv_ref[1, keys, lanes] = grad_v
        return carry

    lax.fori_loop(0, items, one, 0)
    step = 128

    def feats(n, carry):
        lanes = aligned(n, step)
        gf_ref[:, lanes] = (
            dot_nt(gkv_ref[0], kvw_ref[0, lanes, :]) + dot_nt(gkv_ref[1], kvw_ref[1, lanes, :])
        ).astype(BF16)
        return carry

    lax.fori_loop(0, gf_ref.shape[1] // step, feats, 0)
    store_halves(gw_ref, 0, rc, rc, dot_tn(branch, mixed_ref[...]), xor_m, xor_d)
    store_halves(gw_ref, rc, rc, rc, dot_tn(fq_ref[...], gq_buf[...]), xor_m, xor_d)
    for c in copies[1]:
        c.wait()
    first = back + dot_nt(gq_buf[...], flat(wbuf[1]))
    for i in range(items):
        gone_ref[i * seq : i * seq + NQ] = first[i * NQ : (i + 1) * NQ]
        gone_ref[i * seq + NQ : (i + 1) * seq] = gtwo_ref[i * seq + NQ : (i + 1) * seq]


def kv_backward(rk, stored, me_ref, feat_t_ref, gkv_ref, gw_ref):
    for j in range(2):
        store_halves(
            gw_ref, j * stored, rk, stored, dot(feat_t_ref[...], gkv_ref[j]),
            lambda m: m ^ me_ref[1], lambda d: d ^ me_ref[2],
        )


def self_backward(
    rc, lens_ref, me_ref, gone_ref, resid_ref, hid_ref, mixed_ref, qkv_ref, norm_ref, ngb_ref, ngc_ref, w_ref,
    gh_ref, gw_ref, wbuf, gm_buf, gqkv_buf, sems,
):
    items = lens_ref.shape[0]
    seq = hid_ref.shape[0] // items
    width = hid_ref.shape[1]
    n_mp = w_ref.shape[0]
    copies = [fetch(w_ref, p, wbuf.shape[2], wbuf.at[i], sems, i * n_mp) for i, p in enumerate((4, 0, 1, 2))]
    xor_m, xor_d = (lambda m: m ^ me_ref[1]), (lambda d: d ^ me_ref[2])
    back, gain_grad, shift_grad = norm_backward(resid_ref[...], gone_ref[...], norm_ref[0:1])
    branch = back.astype(BF16)
    for c in copies[0]:
        c.wait()
    gm_buf[...] = dot(branch, flat(wbuf[0])).astype(BF16)

    def one(item, carry):
        rows = aligned(item, seq)
        keep = same_segment(lens_ref, item, 2 * seq, seq)
        for p in range(width // 128):
            lanes = pl.ds(p * 128, 128)
            grads = attention_back(
                pair_rows(qkv_ref[0, rows, lanes]), qkv_ref[1, rows, lanes], qkv_ref[2, rows, lanes],
                pair_rows(gm_buf[rows, lanes]), keep,
            )
            for j in range(3):
                gqkv_buf[j, rows, lanes] = grads[j]
        return carry

    lax.fori_loop(0, items, one, 0)
    x = hid_ref[...]
    for j in range(3):
        store_halves(gw_ref, j * rc, rc, rc, dot_tn(x, gqkv_buf[j]), xor_m, xor_d)
    store_halves(gw_ref, 3 * rc, rc, rc, dot_tn(branch, mixed_ref[...]), xor_m, xor_d)
    norms = jnp.concatenate(
        [gain_grad, ngb_ref[0:1], ngc_ref[0:1], shift_grad, ngb_ref[1:2], ngc_ref[1:2], jnp.zeros((122, width), F32)],
        axis=0,
    ).T
    lane = gw_ref.shape[3]
    norms = jnp.concatenate([norms, jnp.zeros((width, lane - 128), F32)], axis=1)
    for m in range(gw_ref.shape[0]):
        store_halves(gw_ref, 4 * rc, rc, rc, norms if m == 0 else jnp.zeros_like(norms), lambda _, m=m: m ^ me_ref[1], xor_d)
    total = back
    for j in range(3):
        for c in copies[j + 1]:
            c.wait()
        total = total + dot_nt(gqkv_buf[j], flat(wbuf[j + 1]))
    gh_ref[...] = total.astype(BF16)


def run(body, outs, scratch, *ins):
    spaces = {"v": pltpu.VMEM, "s": pltpu.SMEM, "a": pl.ANY}
    return pl.pallas_call(
        body,
        out_shape=[jax.ShapeDtypeStruct(shape, dtype) for shape, dtype in outs],
        in_specs=[pl.BlockSpec(memory_space=spaces[kind]) for kind, _ in ins],
        out_specs=[pl.BlockSpec(memory_space=pltpu.VMEM) for _ in outs],
        scratch_shapes=scratch,
        compiler_params=pltpu.CompilerParams(vmem_limit_bytes=60 * 1024 * 1024),
    )(*[value for _, value in ins])


def contrast_plain(all_image, all_text, all_pairs, image_raw, text_raw, first_image):
    items, text_n = image_raw.shape[0], text_raw.shape[0]
    captions = text_n // items
    image_count, text_count = all_image.shape[0], all_text.shape[0]
    sims = dot_nt(all_image, all_text) * SIM_SCALE
    is_pair = all_pairs == jnp.arange(image_count, dtype=jnp.int32)[:, None]
    col_peak = jnp.max(sims, axis=0, keepdims=True)
    col_lse = col_peak + jnp.log(jnp.sum(jnp.exp(sims - col_peak), axis=0, keepdims=True))
    row_peak = jnp.max(sims, axis=1, keepdims=True)
    row_lse = row_peak + jnp.log(jnp.sum(jnp.exp(sims - row_peak), axis=1, keepdims=True))
    pair_sims = jnp.where(is_pair, sims, MASKED)
    pos_peak = jnp.max(pair_sims, axis=1, keepdims=True)
    row_pos = pos_peak + jnp.log(jnp.sum(jnp.exp(pair_sims - pos_peak), axis=1, keepdims=True))
    col_pos = jnp.sum(jnp.where(is_pair, sims, 0.0), axis=0, keepdims=True)
    half_image, half_text = 0.5 / image_count, 0.5 / text_count
    loss = half_text * jnp.sum(col_lse - col_pos) + half_image * jnp.sum(row_lse - row_pos)
    hit = is_pair.astype(F32)
    grad_sims = (
        half_text * (jnp.exp(sims - col_lse) - hit)
        + half_image * (jnp.exp(sims - row_lse) - jnp.exp(pair_sims - row_pos))
    ).astype(BF16)
    own_rows = lax.dynamic_slice_in_dim(grad_sims, first_image, items, axis=0)
    own_cols = lax.dynamic_slice_in_dim(grad_sims, first_image * captions, text_n, axis=1)
    grad_image = dot(own_rows, all_text) * SIM_SCALE
    grad_text = dot_tn(own_cols, all_image) * SIM_SCALE
    grad_i = (unit_backward(image_raw, grad_image) * (1.0 / NQ)).astype(BF16)
    return loss, grad_i, unit_backward(text_raw, grad_text).astype(BF16)


def shards(
    n_dp, n_mp, hidden_in, image_feats, caption_lengths, pair_image, out_grad, self_qkv, self_out, cross_query,
    cross_kv, cross_out, up_weight, down_weight, vision_proj, text_proj, norm_gain, norm_bias,
):
    me_m = lax.axis_index("mp")
    me_d = lax.axis_index("dp")
    me = me_d * n_mp + me_m
    block_items_n, seq, width = hidden_in.shape
    items = block_items_n // n_mp
    vis_len, vis_width = image_feats.shape[1:]
    captions = caption_lengths.shape[1]
    tokens_n, query_n, text_n = items * seq, items * NQ, items * captions
    rows, lane = self_qkv.shape[1:]
    rows_kv = cross_kv.shape[1]
    pieces = up_weight.shape[1] // lane
    emb = vision_proj.shape[1]
    half_emb = emb // n_mp
    emb_rows = items + text_n
    vis_pad = -(-vis_len // 16) * 16
    tile = 2 * lane
    tiles = n_mp * pieces * lane // tile
    in_chunks = rows % 16 == 0
    fast = in_chunks and n_dp == 16 and n_mp == 2

    def mine(value):
        return lax.dynamic_slice_in_dim(value, me_m * items, items, axis=0)

    lengths = mine(caption_lengths)

    def cut(value):
        return jnp.moveaxis(value.reshape(value.shape[0], -1, lane), 1, 0).reshape(-1, lane)

    vis_half = lax.dynamic_slice_in_dim(vision_proj, me_m * half_emb, half_emb, axis=1)
    txt_half = lax.dynamic_slice_in_dim(text_proj, me_m * half_emb, half_emb, axis=1)
    misc = jnp.concatenate([vis_half, txt_half, jnp.zeros((rows, lane - 2 * half_emb), BF16)], axis=1)
    packed = jnp.concatenate(
        [
            self_qkv.reshape(-1, lane), cross_query, self_out.T, cross_out.T, cut(up_weight), cut(down_weight.T), misc,
            cross_kv.reshape(-1, lane),
        ],
        axis=0,
    )
    n_parts = 7 + 2 * pieces
    gathered = lax.all_gather(packed, ("mp", "dp"), axis=0, tiled=False).reshape(n_mp, n_dp, -1, lane)
    norms = lax.all_gather(jnp.concatenate([norm_gain, norm_bias], axis=0), "dp", axis=1, tiled=True)
    norms = jnp.pad(norms.astype(F32), ((0, 2), (0, 0)))
    all_pairs = lax.all_gather(pair_image, "dp", axis=0, tiled=True)[None, :]

    hidden = mine(hidden_in).reshape(tokens_n, width)
    cotangent = mine(out_grad).reshape(tokens_n, width)
    feats = jnp.pad(mine(image_feats), ((0, 0), (0, vis_pad - vis_len), (0, 0))).reshape(items * vis_pad, vis_width)
    feats_t = feats.T
    feats, feats_t, norms, all_pairs = lax.optimization_barrier((feats, feats_t, norms, all_pairs))

    kv_w = gathered[:, :, n_parts * rows :].reshape(n_mp, n_dp, 2, rows_kv, lane)
    kv_w = jnp.transpose(kv_w, (2, 1, 3, 0, 4)).reshape(2, vis_width, width)
    if in_chunks:
        w, nc, rc = gathered, n_dp, rows
    else:
        w = gathered[:, :, : n_parts * rows].reshape(n_mp, n_dp, n_parts, rows, lane)
        w = jnp.transpose(w, (0, 2, 1, 3, 4)).reshape(n_mp, 1, n_parts * width, lane)
        nc, rc = 1, width

    def vm(*shape, dtype=BF16):
        return pltpu.VMEM(shape, dtype)

    sems = pltpu.SemaphoreType.DMA
    qkv, mixed, resid_one, normed_one, first_query, cross_q = run(
        self_forward,
        [
            ((3, tokens_n, width), BF16), ((tokens_n, width), BF16), ((tokens_n, width), F32), ((tokens_n, width), F32),
            ((query_n, width), BF16), ((query_n, width), BF16),
        ],
        [vm(5, nc, rc, width), sems((5 * n_mp,))],
        ("s", lengths), ("v", hidden), ("v", norms), ("a", w),
    )
    kv, cross_mixed, resid_two, normed_two = run(
        functools.partial(cross_forward, vis_len),
        [
            ((2, items * vis_pad, width), BF16), ((query_n, width), BF16), ((query_n, width), F32),
            ((tokens_n, width), F32),
        ],
        [vm(nc, rc, width), sems((n_mp,))],
        ("v", normed_one), ("v", cross_q), ("v", feats), ("v", kv_w), ("v", norms), ("a", w),
    )
    ffn_scratch = [
        vm(tiles, nc, rc, tile), vm(tiles, nc, rc, tile), vm(n_mp, nc, rc, lane), sems((2 * n_mp * pieces,)), sems((n_mp,)),
    ]
    up_value, act, resid_three, block, cls_rows, image_raw, text_raw, embs = run(
        ffn_forward,
        [
            ((tiles, tokens_n, tile), F32), ((tiles, tokens_n, tile), BF16), ((tokens_n, width), F32),
            ((tokens_n, width), BF16), ((emb_rows, width), BF16), ((emb_rows, emb), F32), ((emb_rows, emb), F32),
            ((emb_rows, emb), BF16),
        ],
        ffn_scratch,
        ("s", lengths), ("v", normed_two), ("v", norms), ("a", w),
    )
    if fast:
        both = ("dp", "mp")
        n_dev = n_dp * n_mp

        def spread(value, steps):
            got = [value] + [lax.ppermute(value, both, [(i, i ^ s) for i in range(n_dev)]) for s in steps]
            return jnp.concatenate(got, axis=0)

        everything = spread(spread(spread(embs, (8, 16, 24)), (4, 1, 5)), (2,))
        loss, grad_i, grad_t = run(
            functools.partial(contrast, items, captions),
            [((1, 1), F32), ((emb_rows, emb), BF16), ((emb_rows, emb), BF16)],
            [],
            ("s", jnp.stack([me])), ("v", everything), ("v", all_pairs), ("v", image_raw), ("v", text_raw),
        )
        loss = loss[0, 0]
    else:
        everything = lax.all_gather(embs, ("dp", "mp"), axis=0, tiled=False)
        all_image, all_text = everything[:, :items].reshape(-1, emb), everything[:, items:].reshape(-1, emb)
        loss, grad_i, grad_t = contrast_plain(
            all_image, all_text, all_pairs, image_raw[:items], text_raw[:text_n], me * items
        )
        grad_i = jnp.pad(grad_i, ((0, emb_rows - items), (0, 0)))
        grad_t = jnp.pad(grad_t, ((0, emb_rows - text_n), (0, 0)))

    place = jnp.zeros((3,), jnp.int32)
    stored = -(-rows_kv // 16) * 16 if in_chunks else vis_width
    rk = rows_kv if in_chunks else vis_width
    grad_two, norm_c, gw_ffn = run(
        ffn_backward,
        [((tokens_n, width), F32), ((2, width), F32), ((n_mp, nc, (1 + 2 * pieces) * rc, lane), BF16)],
        ffn_scratch,
        ("s", lengths), ("s", place), ("v", grad_i), ("v", grad_t), ("v", block), ("v", cls_rows), ("v", cotangent),
        ("v", normed_two), ("v", resid_three), ("v", up_value), ("v", act), ("v", norms), ("a", w),
    )
    grad_one, norm_b, grad_kv, grad_feats, gw_cross = run(
        functools.partial(cross_backward, vis_len, rc),
        [
            ((tokens_n, width), F32), ((2, width), F32), ((2, items * vis_pad, width), BF16),
            ((items * vis_pad, vis_width), BF16), ((n_mp, nc, 2 * rc, lane), BF16),
        ],
        [vm(2, nc, rc, width), vm(query_n, width), sems((2 * n_mp,))],
        ("s", place), ("v", grad_two), ("v", resid_two), ("v", cross_mixed), ("v", cross_q), ("v", first_query),
        ("v", kv), ("v", kv_w), ("v", norms), ("a", w),
    )
    swap = [(i, i ^ 1) for i in range(n_mp)]
    grad_feats = grad_feats.reshape(items, vis_pad, vis_width)[:, :vis_len]
    far_feats = lax.ppermute(grad_feats, "mp", swap)
    (gw_kv,) = run(
        functools.partial(kv_backward, rk, stored),
        [((n_mp, nc, 2 * stored, lane), BF16)],
        [],
        ("s", place), ("v", feats_t), ("v", grad_kv),
    )
    grad_hidden, gw_self = run(
        functools.partial(self_backward, rc),
        [((tokens_n, width), BF16), ((n_mp, nc, 5 * rc, lane), BF16)],
        [vm(4, nc, rc, width), vm(tokens_n, width), vm(3, tokens_n, width), sems((4 * n_mp,))],
        ("s", lengths), ("s", place), ("v", grad_one), ("v", resid_one), ("v", hidden), ("v", mixed), ("v", qkv),
        ("v", norms), ("v", norm_b), ("v", norm_c), ("a", w),
    )

    groups = [(gw_self, 5, rows, rows), (gw_cross, 2, rows, rows), (gw_ffn, 1 + 2 * pieces, rows, rows)]
    groups += [(gw_kv, 2, rows_kv, stored if in_chunks else rows_kv)]
    if not in_chunks:
        groups = [
            (
                jnp.transpose(g.reshape(n_mp, count, n_dp, size, lane), (0, 2, 1, 3, 4)).reshape(n_mp, n_dp, -1, lane),
                count, size, size,
            )
            for g, count, size, _ in groups
        ]
    packed_grad = jnp.concatenate([g for g, *_ in groups], axis=2).reshape(n_mp * n_dp, -1, lane)
    summed = lax.psum_scatter(packed_grad, ("mp", "dp"), scatter_dimension=0, tiled=False).astype(F32)
    parts, at = [], 0
    for _, count, size, kept in groups:
        for _ in range(count):
            parts.append(summed[at : at + size])
            at += kept
    g_qkv, g_out, g_norm, g_cross_out, g_query = parts[:3], parts[3], parts[4], parts[5], parts[6]
    g_up, g_down, g_misc = parts[7 : 7 + pieces], parts[7 + pieces : 7 + 2 * pieces], parts[7 + 2 * pieces]
    g_kv = parts[8 + 2 * pieces :]

    def whole(own, far, axis):
        first = jnp.where(me_m == 0, own, far)
        second = jnp.where(me_m == 0, far, own)
        return jnp.concatenate([first, second], axis=axis)

    def exchanged(value):
        return whole(value, lax.ppermute(value, "mp", swap), 0)

    small = jnp.concatenate([g_misc[:, : 2 * half_emb], g_norm[:, :128]], axis=1).astype(BF16)
    far = lax.ppermute(small, "mp", swap)
    low = jnp.where(me_m == 0, small, far).astype(F32)
    high = jnp.where(me_m == 0, far, small).astype(F32)
    norm_share = low[:, 2 * half_emb : 2 * half_emb + 6].T
    return (
        loss,
        exchanged(block.reshape(items, seq, width)),
        exchanged(grad_hidden.reshape(items, seq, width)),
        whole(grad_feats, far_feats, 0),
        jnp.stack(g_qkv),
        g_out.T,
        g_query,
        jnp.stack(g_kv),
        g_cross_out.T,
        jnp.concatenate(g_up, axis=1),
        jnp.concatenate(g_down, axis=1).T,
        jnp.concatenate([low[:, :half_emb], high[:, :half_emb]], axis=1),
        jnp.concatenate([low[:, half_emb : 2 * half_emb], high[:, half_emb : 2 * half_emb]], axis=1),
        norm_share[:3],
        norm_share[3:],
    )


def solution(mesh):
    n_dp, n_mp = mesh.shape["dp"], mesh.shape["mp"]

    def body(*args):
        return shards(n_dp, n_mp, *args)

    return jax.shard_map(
        body,
        mesh=mesh,
        in_specs=(
            P("dp", None, None),
            P("dp", None, None),
            P("dp", None),
            P("dp"),
            P("dp", None, None),
            P(None, "dp", "mp"),
            P("mp", "dp"),
            P("dp", "mp"),
            P(None, "dp", "mp"),
            P("mp", "dp"),
            P("dp", "mp"),
            P("mp", "dp"),
            P("dp", None),
            P("dp", None),
            P(None, "dp"),
            P(None, "dp"),
        ),
        out_specs=(
            P(),
            P("dp", None, None),
            P("dp", None, None),
            P("dp", None, None),
            P(None, "dp", "mp"),
            P("mp", "dp"),
            P("dp", "mp"),
            P(None, "dp", "mp"),
            P("mp", "dp"),
            P("dp", "mp"),
            P("mp", "dp"),
            P("dp", None),
            P("dp", None),
            P(None, "dp"),
            P(None, "dp"),
        ),
        check_vma=False,
    )
```

time: 821 us -> 598 us (0.73)
  local copies, waits for them, and re-layouts: 256 us -> 57.4 us
  Pallas kernels: 0 us -> 125 us
  matrix products: 110 us -> 0 us
  blocking collectives: 81.1 us -> 32.8 us
  waiting for transfers between devices: 300 us -> 322 us
  other arithmetic: 43.4 us -> 27.9 us
  starting transfers between devices: 3.87 us -> 12.9 us
    pallas_call x0 -> x8, Pallas kernels: none -> 125 us  [run(): pl.pallas_call(body, out_shape=[jax.ShapeDtypeStruct(shape, dtype) for sh...]
    dot_general x52 -> x0, matrix products: 110 us -> none  [the longest x13 40.1 us: matmul(): return jnp.dot(left, right, preferred_element_type=F32)]
    reshape x40 -> x2, local copies, waits for them, and re-layouts: 97.7 us -> 15.9 us  [the longest x1 10.3 us: shards(): kv_w = jnp.transpose(kv_w, (2, 1, 3, 0, 4)).reshape(2, vis_width, width)]
    all_gather x1, blocking collectives: 66.8 us -> 18.9 us  [shards(): lax.all_gather(jnp.concatenate([norm_gain, norm_bias], axis=0), 'dp', axi...]
    convert_element_type x21 -> x0, local copies, waits for them, and re-layouts: 39.1 us -> none  [the longest x11 23.5 us: shards(): value.astype(BF16)]
    reduce_scatter x1, waiting for transfers between devices: 99.7 us -> 129 us  [shards(): lax.psum_scatter(packed_grad, ('mp', 'dp'), scatter_dimension=0, tiled=Fa...]
    unnamed x353 -> x47, local copies, waits for them, and re-layouts: 41.2 us -> 12.2 us
    another operation x16 -> x1, local copies, waits for them, and re-layouts: 20.9 us -> 0.51 us  [the longest x4 9.9 us: shards(): w_up = jnp.stack([part(9 + p) for p in range(pieces)], axis=1)]
  transfers between devices with their start and end apart: 6 -> 13, of which waited for: 4 -> 10; matrix products, arithmetic and copies ran while one was open for 7% -> 6% of each run, Pallas kernels for 0% -> 0%
where the time goes in v2:
time: 598 us; the launch traced here: 593 us
  waiting for transfers between devices  322 us (54%)
  Pallas kernels  125 us (21%)
  local copies, waits for them, and re-layouts  57.4 us (10%)
  blocking collectives  32.8 us (5%)
  other arithmetic  27.9 us (5%)
  between operations  15.2 us (3%)
  starting transfers between devices  12.9 us (2%)
    reduce_scatter x1, waiting for transfers between devices, shards(): lax.psum_scatter(packed_grad, ('mp', 'dp'), scatter_dimension=0, tiled=Fa...  129 us
    pallas_call x8, Pallas kernels, run(): pl.pallas_call(body, out_shape=[jax.ShapeDtypeStruct(shape, dtype) for sh...  125 us
    all_gather x1, waiting for transfers between devices, shards(): lax.all_gather(packed, ('mp', 'dp'), axis=0, tiled=False)  93.6 us
    ppermute x2, waiting for transfers between devices, exchanged(): return whole(value, lax.ppermute(value, 'mp', swap), 0)  92 us
    all_gather x1, blocking collectives, shards(): lax.all_gather(jnp.concatenate([norm_gain, norm_bias], axis=0), 'dp', axi...  18.9 us
    concatenate x1, other arithmetic, shards(): jnp.concatenate([g for g, *_ in groups], axis=2)  15.8 us
    unnamed x1, blocking collectives  13.9 us
    unnamed x47, local copies, waits for them, and re-layouts  12.2 us
  transfers between devices with their start and end apart: 13, of which 10 were waited for; matrix products, arithmetic and copies ran while one was open for 6% of the time, Pallas kernels for 0%

profile of v2, /device:TPU:0, one launch (start us, length us, event | category | flops | bytes accessed | tf_op | source)
XLA Modules:
  0.0 593.5 jit_solution(8438847468291845500)
XLA Ops:
  15.2 4.1 constant_dynamic-slice_fusion.3
  21.6 5.5 copy.60
  28.7 13.9 %all-reduce.2 = s32[384]{0:T(512)S(1)} all-reduce(s32[384]{0:T(512)S(1)} %dynamic-update-slice), channel_id=1, replica_groups=mesh['dp'=16,'mp'=2] {'dp'}, use_global_device_ids=true, to_apply=%add.2 | all-reduce | flops 384 | bytes 3072
  43.2 18.9 %all-gather.1 = bf16[16,48,6]{1,2,0:T(8,128)(2,1)S(1)} all-gather(bf16[1,48,6]{1,2,0:T(8,128)(2,1)S(1)} %maximum_bitcast_fusion.1), channel_id=1, replica_groups=mesh['dp'=16,'mp'=2] {'dp'}, dimensions={0}, use_global_device_ids=true | all-gather | bytes 9792 | tf_op jit(solution)/shard_map/all_gather | solution.py:617
  64.3 93.6 %all-gather.4.cloned.1.call-done = bf16[28672,384]{1,0:T(8,128)(2,1)} async-done(((bf16[896,384]{1,0:T(8,128)(2,1)}), bf16[28672,384]{1,0:T(8,128)(2,1)}) %all-gather.4.cloned.1.call-update) | async-done | bytes 22020112 | tf_op jit(solution)/shard_map/all_gather | solution.py:616
  157.9 2.7 slice.163
  160.6 6.5 %copy.64 = bf16[2,16,88,2,384]{4,3,2,1,0:T(2,128)(2,1)} copy(bf16[2,16,88,2,384]{4,2,0,1,3:T(8,128)(2,1)S(1)} %bitcast.74) | data formatting | bytes 8650752 | tf_op jit(solution)/shard_map/transpose | solution.py:628
  167.1 10.3 %reshape.110.kvw_ref = bf16[2,1408,768]{2,1,0:T(8,128)(2,1)} reshape(bf16[2,16,88,2,384]{4,3,2,1,0:T(2,128)(2,1)} %copy.64) | data formatting | bytes 8650752 | tf_op jit(solution)/shard_map/reshape | solution.py:628
  177.4 9.1 %shard_map.271 = (bf16[3,256,768]{2,1,0:T(8,128)(2,1)}, bf16[256,768]{1,0:T(8,128)(2,1)}, f32[256,768]{1,0:T(8,128)}, f32[256,768]{1,0:T(8,128)}, bf16[128,768]{1,0:T(8,128)(2,1)}, /*index=5*/bf16[128,768]{1,0:T(8,128)(2,1)}) custom-call(s32[4,3]{1,0:T(4,128)} %copy.68.lens_ref, bf16[256,768]{1,0:T(8,128)(2,1)} %bitcast.78, ...), custom_call_target="tpu_custom_call" | custom-call | tf_op jit(solution)/shard_map/pallas_call | solution.py:534
  186.6 20.5 %shard_map.272 = (bf16[2,1088,768]{2,1,0:T(8,128)(2,1)}, bf16[128,768]{1,0:T(8,128)(2,1)}, f32[128,768]{1,0:T(8,128)}, f32[256,768]{1,0:T(8,128)}) custom-call(f32[256,768]{1,0:T(8,128)} %get-tuple-element.51.normed_ref, bf16[128,768]{1,0:T(8,128)(2,1)} %get-tuple-element.52.cq_ref, bf16[1088,1408]{1,0:T(8,128)(2,1)} %bitcast.73, ...), custom_call_target="tpu_custom_call" | custom-call | tf_op jit(solution)/shard_map/pallas_call | solution.py:534
  207.1 10.1 %shard_map.273 = (f32[4,256,768]{2,1,0:T(8,128)}, bf16[4,256,768]{2,1,0:T(8,128)(2,1)}, f32[256,768]{1,0:T(8,128)}, bf16[256,768]{1,0:T(8,128)(2,1)}, bf16[16,76...) custom-call(s32[4,3]{1,0:T(4,128)} %copy.68.lens_ref, ...), custom_call_target="tpu_custom_call" | custom-call | tf_op jit(solution)/shard_map/pallas_call | solution.py:534
  222.8 2.8 collective-permute-done.2
  234.5 2.7 shard_map.274
  237.8 17.0 %shard_map.275 = (f32[256,768]{1,0:T(8,128)}, f32[2,768]{1,0:T(2,128)}, bf16[2,16,432,384]{3,2,1,0:T(8,128)(2,1)}) custom-call(s32[4,3]{1,0:T(4,128)} %copy.68.lens_ref, s32[3]{0:T(128)} %broadcast_1_me_ref.2.me_ref, bf16[16,256]{1,0:T(8,128)(2,1)} %get-tuple-element.61.gi_ref, bf16[16,256]{1,0:T(8,128)(2,1)} %get-tuple-element.62.gt_ref, ...), custom_call_target="tpu_custom_call" | custom-call | tf_op jit(solution)/shard_map/pallas_call | solution.py:534
  254.8 34.4 %shard_map.276 = (f32[256,768]{1,0:T(8,128)}, f32[2,768]{1,0:T(2,128)}, bf16[2,1088,768]{2,1,0:T(8,128)(2,1)}, bf16[1088,1408]{1,0:T(8,128)(2,1)}, bf16[2,16,96,384]{3,2,1,0:T(8,128)(2,1)}) custom-call(s32[3]{0:T(128)} %broadcast_1_me_ref.2.me_ref, f32[256,768]{1,0:T(8,128)} %get-tuple-element.67.gtwo_ref, f32[128,768]{1,0:T(8,128)} %get-tuple-element.68.resid_ref, ...), custom_call_target="tpu_custom_call" | custom-call | tf_op jit(solution)/shard_map/pallas_call | solution.py:534
  289.2 11.0 %shard_map.278 = bf16[2,16,192,384]{3,2,1,0:T(8,128)(2,1)} custom-call(s32[3]{0:T(128)} %broadcast_1_me_ref.2.me_ref, bf16[1408,1088]{1,0:T(8,128)(2,1)} %bitcast.75, bf16[2,1088,768]{2,1,0:T(8,128)(2,1)} %get-tuple-element.84.gkv_ref), custom_call_target="tpu_custom_call" | custom-call | tf_op jit(solution)/shard_map/pallas_call | solution.py:534
  300.2 20.6 %shard_map.277 = (bf16[256,768]{1,0:T(8,128)(2,1)}, bf16[2,16,240,384]{3,2,1,0:T(8,128)(2,1)}) custom-call(s32[4,3]{1,0:T(4,128)} %copy.68.lens_ref, s32[3]{0:T(128)} %broadcast_1_me_ref.2.me_ref, f32[256,768]{1,0:T(8,128)} %get-tuple-element.72.gone_ref, f32[256,768]{1,0:T(8,128)} %get-tuple-element.73.resid_ref, bf16[256,768]{1,0:T(8,128)(2,1)} %bitcast.79, ...), custom_call_target="tpu_custom_call" | custom-call | tf_op jit(solution)/shard_map/pallas_call | solution.py:534
  320.8 15.8 %pad_maximum_fusion = bf16[2,16,960,384]{3,2,1,0:T(8,128)(2,1)} fusion(bf16[2,16,192,384]{3,2,1,0:T(8,128)(2,1)} %shard_map.278, bf16[2,16,432,384]{3,2,1,0:T(8,128)(2,1)} %get-tuple-element.82, bf16[2,16,96,384]{3,2,1,0:T(8,128)(2,1)S(1)} %copy-done.2, bf16[2,16,240,384]{3,2,1,0:T(8,128)(2,1)} %get-tuple-element.80), kind=kLoop, calls=%fused_computation | loop fusion | flops 94371840 | bytes 47185920 | tf_op jit(solution)/shard_map/concatenate | solution.py:743
  336.7 3.7 slice.164
  343.9 83.0 %collective-permute-done.7 = bf16[4,64,768]{2,1,0:T(8,128)(2,1)S(1)} collective-permute-done((bf16[4,64,768]{2,1,0:T(8,128)(2,1)S(1)}, bf16[4,64,768]{2,1,0:T(8,128)(2,1)S(1)}, u32[]{:S(2)}, u32[]{:S(2)}) %collective-permute-start.7) | collective-permute-done | bytes 393248 | tf_op jit(solution)/shard_map/ppermute | solution.py:760
  427.9 9.0 %collective-permute-done.8 = bf16[4,64,768]{2,1,0:T(8,128)(2,1)S(1)} collective-permute-done((bf16[4,64,768]{2,1,0:T(8,128)(2,1)S(1)}, bf16[4,64,768]{2,1,0:T(8,128)(2,1)S(1)}, u32[]{:S(2)}, u32[]{:S(2)}) %collective-permute-start.8) | collective-permute-done | bytes 393248 | tf_op jit(solution)/shard_map/ppermute | solution.py:760
  437.9 3.5 broadcast_select_fusion.1
  442.0 3.3 copy.65
  445.2 129.0 %reduce-scatter.2.cloned.1.call-done = bf16[1,960,384]{2,1,0:T(8,128)(2,1)} async-done(((bf16[32,960,384]{2,1,0:T(8,128)(2,1)}), bf16[1,960,384]{2,1,0:T(8,128)(2,1)}) %reduce-scatter.2.cloned.1.call-update) | async-done | bytes 737296 | tf_op jit(solution)/shard_map/reduce_scatter | solution.py:744
  (112 shorter events, 47.1 us)
Async XLA Ops:
  7.2 56.4 %copy-start = (bf16[8,64,768]{2,1,0:T(8,128)(2,1)S(1)}, bf16[8,64,768]{2,1,0:T(8,128)(2,1)}, u32[]{:S(2)}) copy-start(bf16[8,64,768]{2,1,0:T(8,128)(2,1)} %param.16) | copy-start | bytes 2359300
  7.2 150.7 %all-gather.4.cloned.1.call-start = ((), (), s32[]{:S(2)}) async-start(), calls=%async_computation.2 | async-start | bytes 22708224 | tf_op jit(solution)/shard_map/all_gather | solution.py:616
  15.2 559.1 %reduce-scatter.2.cloned.1.call-start = ((), (), s32[]{:S(2)}) async-start(), calls=%async_computation.1 | async-start | bytes 24330240 | tf_op jit(solution)/shard_map/reduce_scatter | solution.py:744
  21.6 5.5 copy-start.12
  21.6 6.8 %copy-start.11 = (s32[24]{0:T(128)S(1)}, s32[24]{0:T(128)}, u32[]{:S(2)}) copy-start(s32[24]{0:T(128)} %param.19) | copy-start | bytes 292
  21.6 21.5 %copy-start.9 = (bf16[3,48]{1,0:T(4,128)(2,1)S(1)}, bf16[3,48]{1,0:T(4,128)(2,1)}, u32[]{:S(2)}) copy-start(bf16[3,48]{1,0:T(4,128)(2,1)} %param.31) | copy-start | bytes 868
  21.6 21.5 %copy-start.10 = (bf16[3,48]{1,0:T(4,128)(2,1)S(1)}, bf16[3,48]{1,0:T(4,128)(2,1)}, u32[]{:S(2)}) copy-start(bf16[3,48]{1,0:T(4,128)(2,1)} %param.30) | copy-start | bytes 868
  21.6 41.2 %copy-start.8 = (s32[8,3]{0,1:T(4,128)S(1)}, s32[8,3]{0,1:T(4,128)}, u32[]{:S(2)}) copy-start(s32[8,3]{0,1:T(4,128)} %param.18) | copy-start | bytes 292
  207.1 25.4 %copy-start.7 = (bf16[8,64,768]{2,1,0:T(8,128)(2,1)S(1)}, bf16[8,64,768]{2,1,0:T(8,128)(2,1)}, u32[]{:S(2)}) copy-start(bf16[8,64,768]{2,1,0:T(8,128)(2,1)} %param.20) | copy-start | bytes 2359300
  217.2 5.2 collective-permute-start
  218.0 4.8 collective-permute-start.1
  219.9 5.7 collective-permute-start.2
  225.6 4.2 collective-permute-start.3
  227.0 3.9 collective-permute-start.4
  227.7 4.8 collective-permute-start.5
  232.5 1.3 collective-permute-start.6
  300.2 20.6 %copy-start.2 = (bf16[2,16,96,384]{3,2,1,0:T(8,128)(2,1)S(1)}, bf16[2,16,96,384]{3,2,1,0:T(8,128)(2,1)}, u32[]{:S(2)}) copy-start(bf16[2,16,96,384]{3,2,1,0:T(8,128)(2,1)} %get-tuple-element.81) | copy-start | bytes 7077892
  336.7 5.2 copy-start.3
  336.7 5.8 copy-start.5
  340.5 97.4 %collective-permute-start.9 = (bf16[4,257,1408]{2,1,0:T(8,128)(2,1)}, bf16[4,257,1408]{2,1,0:T(8,128)(2,1)}, u32[]{:S(2)}, u32[]{:S(2)}) collective-permute-start(bf16[4,257,1408]{2,1,0:T(8,128)(2,1)} %slice.164), channel_id=1, source_target_pairs={{0,1},{1,0},{2,3},{3,2},{4,5},{5,4},{6,7},{7,6},{8,9},{9,8},{10,11... | collective-permute-start | bytes 8684552 | tf_op jit(solution)/shard_map/ppermute | solution.py:718
  341.9 85.0 %collective-permute-start.7 = (bf16[4,64,768]{2,1,0:T(8,128)(2,1)S(1)}, bf16[4,64,768]{2,1,0:T(8,128)(2,1)S(1)}, u32[]{:S(2)}, u32[]{:S(2)}) collective-permute-start(bf16[4,64,768]{2,1,0:T(8,128)(2,1)S(1)} %bitcast.82), channel_id=1, source_target_pairs={{0,1},{1,0},{2,3},{3,2},{4,5},{5,4},{6,7},{7,6},{8,9},{9,8},{10,11... | collective-permute-start | bytes 1179656 | tf_op jit(solution)/shard_map/ppermute | solution.py:760
  342.5 94.4 %collective-permute-start.8 = (bf16[4,64,768]{2,1,0:T(8,128)(2,1)S(1)}, bf16[4,64,768]{2,1,0:T(8,128)(2,1)S(1)}, u32[]{:S(2)}, u32[]{:S(2)}) collective-permute-start(bf16[4,64,768]{2,1,0:T(8,128)(2,1)S(1)} %bitcast.89), channel_id=1, source_target_pairs={{0,1},{1,0},{2,3},{3,2},{4,5},{5,4},{6,7},{7,6},{8,9},{9,8},{10,11... | collective-permute-start | bytes 1179656 | tf_op jit(solution)/shard_map/ppermute | solution.py:760
  442.0 144.5 %copy-start.1 = (bf16[8,64,768]{2,1,0:T(8,128)(2,1)S(1)}, bf16[8,64,768]{2,1,0:T(8,128)(2,1)}, u32[]{:S(2)}) copy-start(bf16[8,64,768]{2,1,0:T(8,128)(2,1)} %param.16) | copy-start | bytes 2359300
  575.7 8.1 %collective-permute-start.10 = (bf16[48,384]{1,0:T(8,128)(2,1)S(1)}, bf16[48,384]{1,0:T(8,128)(2,1)S(1)}, u32[]{:S(2)}, u32[]{:S(2)}) collective-permute-start(bf16[48,384]{1,0:T(8,128)(2,1)S(1)} %pad_maximum_fusion.9), channel_id=1, source_target_pairs={{0,1},{1,0},{2,3},{3,2},{4,5},{5,4},{6,7},{7,6},{8,9},{9,8},{10,11... | collective-permute-start | bytes 110600 | tf_op jit(solution)/shard_map/ppermute | solution.py:763
  (2 other events, 1.6 us)
Sparse Core Ops, SparseCore 0:
  15.3 142.5 all-gather.3
  336.8 237.3 reduce-scatter.1

commit v3 on v2

--- a/solution.py
+++ b/solution.py
@@ -128,15 +128,21 @@
     return ref_value.reshape(-1, ref_value.shape[-1])
 
 
-def store_halves(out_ref, row_at, chunk_rows, stored, value, m_of, d_of):
-    n_mp, n_chunk, _, lane = out_ref.shape
-    if stored != chunk_rows:
-        value = jnp.concatenate([value, jnp.zeros((stored - chunk_rows, value.shape[1]), value.dtype)], axis=0)
+def share(outs, me_ref, order, row_at, stored, tile_ref, m, lanes, chunk_rows):
+    if len(outs) == 1:
+        outs[0][m, 0, pl.ds(row_at, stored), :] = tile_ref[pl.ds(0, stored), lanes].astype(BF16)
+        return
+    for r in range(16):
+        rows = pl.ds(pl.multiple_of((me_ref[2] ^ r) * chunk_rows, 8), stored)
+        at = {"x": (r >> 1) & 1, "y": me_ref[1] ^ m, "v": (r >> 2) & 1, "u": (r >> 3) & 1}
+        i, j, k, n = (at[axis] for axis in order)
+        outs[r & 1][i, j, k, n, pl.ds(row_at, stored), :] = tile_ref[rows, lanes].astype(BF16)
+
+
+def share_halves(outs, me_ref, order, row_at, stored, tile_ref, value, chunk_rows, lane):
+    tile_ref[pl.ds(0, value.shape[0]), :] = value
     for m in range(value.shape[1] // lane):
-        for d in range(n_chunk):
-            out_ref[m_of(m), d_of(d), pl.ds(row_at, stored), :] = value[
-                d * chunk_rows : d * chunk_rows + stored, m * lane : (m + 1) * lane
-            ].astype(BF16)
+        share(outs, me_ref, order, row_at, stored, tile_ref, m, slice(m * lane, (m + 1) * lane), chunk_rows)
 
 
 def self_forward(lens_ref, hid_ref, norm_ref, w_ref, qkv_ref, mixed_ref, resid_ref, normed_ref, fq_ref, cq_ref, wbuf, sems):
@@ -361,9 +367,11 @@
 
 
 def ffn_backward(
-    lens_ref, me_ref, gi_ref, gt_ref, block_ref, cls_ref, og_ref, two_ref, resid_ref, up_ref, act_ref, norm_ref, w_ref,
-    gtwo_ref, ng_ref, gw_ref, up_buf, down_buf, misc_buf, sems, msems,
+    orders, lens_ref, me_ref, gi_ref, gt_ref, block_ref, cls_ref, og_ref, two_ref, resid_ref, up_ref, act_ref, norm_ref, w_ref,
+    gtwo_ref, ng_ref, *refs,
 ):
+    outs, (up_buf, down_buf, misc_buf, sems, msems, tile_ref) = refs[:-6], refs[-6:]
+    downs_out, ups_out = outs[: len(outs) // 2], outs[len(outs) // 2 :]
     items = lens_ref.shape[0]
     seq = two_ref.shape[0] // items
     tokens = two_ref.shape[0]
@@ -390,8 +398,8 @@
         misc = flat(misc_buf[m])
         lanes = slice(m * half, (m + 1) * half)
         grad = grad + dot_nt(gi_rows[:, lanes], misc[:, :half]) + dot_nt(gt_rows[:, lanes], misc[:, half : 2 * half])
-        share = jnp.concatenate([dot_tn(block, gi_rows[:, lanes]), dot_tn(cls, gt[:, lanes]), zero], axis=1)
-        store_halves(gw_ref, 2 * pieces * rc, rc, rc, share, lambda _, m=m: m ^ me_ref[1], lambda d: d ^ me_ref[2])
+        tile_ref[:, :lane] = jnp.concatenate([dot_tn(block, gi_rows[:, lanes]), dot_tn(cls, gt[:, lanes]), zero], axis=1)
+        share(ups_out, me_ref, orders[1], pieces * rc, rc, tile_ref, m, slice(0, lane), rc)
     back, gain_grad, shift_grad = norm_backward(resid_ref[...], grad, norm_ref[2:3])
     ng_ref[...] = jnp.concatenate([gain_grad, shift_grad], axis=0)
     branch = back.astype(BF16)
@@ -404,37 +412,33 @@
         slope = 0.5 * (1.0 + lax.erf(up * (0.5**0.5))) + up * jnp.exp(-0.5 * up * up) * 0.3989422804014327
         grad_up = (dot(branch, flat(down_buf[t])) * slope).astype(BF16)
         m, p = (t * per) // pieces, (t * per) % pieces
-        for s in range(per):
-            lanes = slice(s * lane, (s + 1) * lane)
-            for base, left, right in ((0, two_b, grad_up), (pieces, branch, act_ref[t])):
-                store_halves(
-                    gw_ref, (base + p + s) * rc, rc, rc, dot_tn(left, right[:, lanes]),
-                    lambda _, m=m: m ^ me_ref[1], lambda d: d ^ me_ref[2],
-                )
+        for outs, order, left, right in (
+            (ups_out, orders[1], two_b, grad_up), (downs_out, orders[0], branch, act_ref[t])
+        ):
+            tile_ref[...] = dot_tn(left, right)
+            for s in range(per):
+                share(outs, me_ref, order, (p + s) * rc, rc, tile_ref, m, slice(s * lane, (s + 1) * lane), rc)
         total = total + dot_nt(grad_up, flat(up_buf[t]))
     gtwo_ref[...] = total
 
 
 def cross_backward(
-    vis_len, rc, me_ref, gtwo_ref, resid_ref, mixed_ref, cq_ref, fq_ref, kv_ref, kvw_ref, norm_ref, w_ref,
-    gone_ref, ng_ref, gkv_ref, gf_ref, gw_ref, wbuf, gq_buf, sems,
+    vis_len, gtwo_ref, resid_ref, cq_ref, kv_ref, norm_ref, w_ref, gone_ref, ng_ref, gkv_ref, gq_ref, branch_ref, wbuf, sems,
 ):
     items = cq_ref.shape[0] // NQ
     seq = gtwo_ref.shape[0] // items
     width = cq_ref.shape[1]
     vis_pad = kv_ref.shape[1] // items
-    wrc = wbuf.shape[2]
     n_mp = w_ref.shape[0]
-    copies = [fetch(w_ref, p, wrc, wbuf.at[i], sems, i * n_mp) for i, p in enumerate((5, 3))]
-    xor_m, xor_d = (lambda m: m ^ me_ref[1]), (lambda d: d ^ me_ref[2])
+    copies = [fetch(w_ref, p, wbuf.shape[2], wbuf.at[i], sems, i * n_mp) for i, p in enumerate((5, 3))]
     grad = jnp.concatenate([gtwo_ref[i * seq : i * seq + NQ] for i in range(items)], axis=0)
     back, gain_grad, shift_grad = norm_backward(resid_ref[...], grad, norm_ref[1:2])
     ng_ref[...] = jnp.concatenate([gain_grad, shift_grad], axis=0)
     branch = back.astype(BF16)
+    branch_ref[...] = branch
     for c in copies[0]:
         c.wait()
-    grad_mixed = dot(branch, flat(wbuf[0])).astype(BF16)
-    gq_buf[...] = grad_mixed
+    gq_ref[...] = dot(branch, flat(wbuf[0])).astype(BF16)
 
     def one(item, carry):
         rows, keys = aligned(item, NQ), aligned(item, vis_pad)
@@ -443,57 +447,58 @@
             lanes = pl.ds(p * 128, 128)
             grad_q, grad_k, grad_v = attention_back(
                 pair_rows(cq_ref[rows, lanes]), kv_ref[0, keys, lanes], kv_ref[1, keys, lanes],
-                pair_rows(gq_buf[rows, lanes]), keep,
+                pair_rows(gq_ref[rows, lanes]), keep,
             )
-            gq_buf[rows, lanes] = grad_q
+            gq_ref[rows, lanes] = grad_q
             gkv_ref[0, keys, lanes] = grad_k
             gkv_ref[1, keys, lanes] = grad_v
         return carry
 
     lax.fori_loop(0, items, one, 0)
-    step = 128
-
-    def feats(n, carry):
-        lanes = aligned(n, step)
-        gf_ref[:, lanes] = (
-            dot_nt(gkv_ref[0], kvw_ref[0, lanes, :]) + dot_nt(gkv_ref[1], kvw_ref[1, lanes, :])
-        ).astype(BF16)
-        return carry
-
-    lax.fori_loop(0, gf_ref.shape[1] // step, feats, 0)
-    store_halves(gw_ref, 0, rc, rc, dot_tn(branch, mixed_ref[...]), xor_m, xor_d)
-    store_halves(gw_ref, rc, rc, rc, dot_tn(fq_ref[...], gq_buf[...]), xor_m, xor_d)
     for c in copies[1]:
         c.wait()
-    first = back + dot_nt(gq_buf[...], flat(wbuf[1]))
+    first = back + dot_nt(gq_ref[...], flat(wbuf[1]))
     for i in range(items):
         gone_ref[i * seq : i * seq + NQ] = first[i * NQ : (i + 1) * NQ]
         gone_ref[i * seq + NQ : (i + 1) * seq] = gtwo_ref[i * seq + NQ : (i + 1) * seq]
 
 
-def kv_backward(rk, stored, me_ref, feat_t_ref, gkv_ref, gw_ref):
+def feats_backward(gkv_ref, kvw_ref, gf_ref):
+    step = 128
+
+    def feats(n, carry):
+        lanes = aligned(n, step)
+        total = dot_nt(gkv_ref[0], kvw_ref[0, lanes, :]) + dot_nt(gkv_ref[1], kvw_ref[1, lanes, :])
+        gf_ref[:, lanes] = total.astype(BF16)
+        return carry
+
+    lax.fori_loop(0, gf_ref.shape[1] // step, feats, 0)
+
+
+def cross_weights_backward(
+    rc, rk, stored, lane, order, me_ref, feat_t_ref, gkv_ref, branch_ref, mixed_ref, fq_ref, gq_ref, *refs,
+):
+    outs, tile_ref = refs[:-1], refs[-1]
+    share_halves(outs, me_ref, order, 0, rc, tile_ref, dot_tn(branch_ref[...], mixed_ref[...]), rc, lane)
+    share_halves(outs, me_ref, order, rc, rc, tile_ref, dot_tn(fq_ref[...], gq_ref[...]), rc, lane)
     for j in range(2):
-        store_halves(
-            gw_ref, j * stored, rk, stored, dot(feat_t_ref[...], gkv_ref[j]),
-            lambda m: m ^ me_ref[1], lambda d: d ^ me_ref[2],
-        )
-
-
-def self_backward(
-    rc, lens_ref, me_ref, gone_ref, resid_ref, hid_ref, mixed_ref, qkv_ref, norm_ref, ngb_ref, ngc_ref, w_ref,
-    gh_ref, gw_ref, wbuf, gm_buf, gqkv_buf, sems,
+        grad = dot(feat_t_ref[...], gkv_ref[j])
+        share_halves(outs, me_ref, order, 2 * rc + j * stored, stored, tile_ref, grad, rk, lane)
+
+
+def self_attention_backward(
+    lens_ref, gone_ref, resid_ref, qkv_ref, norm_ref, w_ref, back_ref, ng_ref, gqkv_ref, wbuf, gm_buf, sems,
 ):
     items = lens_ref.shape[0]
-    seq = hid_ref.shape[0] // items
-    width = hid_ref.shape[1]
-    n_mp = w_ref.shape[0]
-    copies = [fetch(w_ref, p, wbuf.shape[2], wbuf.at[i], sems, i * n_mp) for i, p in enumerate((4, 0, 1, 2))]
-    xor_m, xor_d = (lambda m: m ^ me_ref[1]), (lambda d: d ^ me_ref[2])
+    seq = gone_ref.shape[0] // items
+    width = gone_ref.shape[1]
+    copies = fetch(w_ref, 4, wbuf.shape[1], wbuf, sems, 0)
     back, gain_grad, shift_grad = norm_backward(resid_ref[...], gone_ref[...], norm_ref[0:1])
-    branch = back.astype(BF16)
-    for c in copies[0]:
+    back_ref[...] = back
+    ng_ref[...] = jnp.concatenate([gain_grad, shift_grad], axis=0)
+    for c in copies:
         c.wait()
-    gm_buf[...] = dot(branch, flat(wbuf[0])).astype(BF16)
+    gm_buf[...] = dot(back.astype(BF16), flat(wbuf[...])).astype(BF16)
 
     def one(item, carry):
         rows = aligned(item, seq)
@@ -505,40 +510,136 @@
                 pair_rows(gm_buf[rows, lanes]), keep,
             )
             for j in range(3):
-                gqkv_buf[j, rows, lanes] = grads[j]
+                gqkv_ref[j, rows, lanes] = grads[j]
         return carry
 
     lax.fori_loop(0, items, one, 0)
+
+
+def self_weights_backward(
+    rc, order, me_ref, back_ref, hid_ref, mixed_ref, gqkv_ref, nga_ref, ngb_ref, ngc_ref, w_ref, gh_ref, *refs,
+):
+    outs, (wbuf, sems, tile_ref) = refs[:-3], refs[-3:]
+    width = hid_ref.shape[1]
+    n_mp, lane = w_ref.shape[0], w_ref.shape[3]
+    copies = [fetch(w_ref, p, wbuf.shape[2], wbuf.at[p], sems, p * n_mp) for p in range(3)]
     x = hid_ref[...]
     for j in range(3):
-        store_halves(gw_ref, j * rc, rc, rc, dot_tn(x, gqkv_buf[j]), xor_m, xor_d)
-    store_halves(gw_ref, 3 * rc, rc, rc, dot_tn(branch, mixed_ref[...]), xor_m, xor_d)
+        share_halves(outs, me_ref, order, j * rc, rc, tile_ref, dot_tn(x, gqkv_ref[j]), rc, lane)
+    branch = back_ref[...].astype(BF16)
+    share_halves(outs, me_ref, order, 3 * rc, rc, tile_ref, dot_tn(branch, mixed_ref[...]), rc, lane)
     norms = jnp.concatenate(
-        [gain_grad, ngb_ref[0:1], ngc_ref[0:1], shift_grad, ngb_ref[1:2], ngc_ref[1:2], jnp.zeros((122, width), F32)],
+        [r[0:1] for r in (nga_ref, ngb_ref, ngc_ref)] + [r[1:2] for r in (nga_ref, ngb_ref, ngc_ref)]
+        + [jnp.zeros((122, width), F32)],
         axis=0,
     ).T
-    lane = gw_ref.shape[3]
-    norms = jnp.concatenate([norms, jnp.zeros((width, lane - 128), F32)], axis=1)
-    for m in range(gw_ref.shape[0]):
-        store_halves(gw_ref, 4 * rc, rc, rc, norms if m == 0 else jnp.zeros_like(norms), lambda _, m=m: m ^ me_ref[1], xor_d)
-    total = back
+    tile_ref[:, :lane] = jnp.concatenate([norms, jnp.zeros((width, lane - 128), F32)], axis=1)
+    for m in range(n_mp):
+        share(outs, me_ref, order, 4 * rc, rc, tile_ref, m, slice(0, lane), rc)
+    total = back_ref[...]
     for j in range(3):
-        for c in copies[j + 1]:
+        for c in copies[j]:
             c.wait()
-        total = total + dot_nt(gqkv_buf[j], flat(wbuf[j + 1]))
+        total = total + dot_nt(gqkv_ref[j], flat(wbuf[j]))
     gh_ref[...] = total.astype(BF16)
 
 
-def run(body, outs, scratch, *ins):
+def run(body, outs, scratch, *ins, after=()):
     spaces = {"v": pltpu.VMEM, "s": pltpu.SMEM, "a": pl.ANY}
+
+    def kernel(*refs):
+        body(*refs[: len(ins)], *refs[len(ins) + len(after) :])
+
+    def spec(kind, value):
+        if kind == "f":
+            return pl.BlockSpec((1, *value.shape[1:]), lambda i: (0, 0, 0))
+        return pl.BlockSpec(memory_space=spaces[kind])
+
+    grid = {"grid": (1,)} if any(kind == "f" for kind, _ in ins) else {}
     return pl.pallas_call(
-        body,
+        kernel,
+        **grid,
         out_shape=[jax.ShapeDtypeStruct(shape, dtype) for shape, dtype in outs],
-        in_specs=[pl.BlockSpec(memory_space=spaces[kind]) for kind, _ in ins],
+        in_specs=[spec(kind, value) for kind, value in ins] + [pl.BlockSpec(memory_space=pl.ANY)] * len(after),
         out_specs=[pl.BlockSpec(memory_space=pltpu.VMEM) for _ in outs],
         scratch_shapes=scratch,
+        cost_estimate=pl.CostEstimate(flops=3 * 10**10, bytes_accessed=10**8, transcendentals=0),
         compiler_params=pltpu.CompilerParams(vmem_limit_bytes=60 * 1024 * 1024),
-    )(*[value for _, value in ins])
+    )(*[value for _, value in ins], *after)
+
+
+def combine(terms, after):
+    left = min(t.ndim for t in terms) - 2
+    places = 2 ** (left - 1)
+    rows, lane = terms[0].shape[-2:]
+    terms = [t.reshape(-1, 2, places, rows, lane) for t in terms]
+
+    def kernel(*refs):
+        total = refs[0][0, 0, 0].astype(F32)
+        for ref in refs[1 : len(terms)]:
+            total = total + ref[0, 0, 0].astype(F32)
+        refs[-1][0] = total.astype(BF16)
+
+    return pl.pallas_call(
+        kernel,
+        grid=(places,),
+        out_shape=jax.ShapeDtypeStruct((places, rows, lane), BF16),
+        in_specs=[pl.BlockSpec((1, 1, 1, rows, lane), lambda i: (0, 1, i, 0, 0))] * len(terms)
+        + [pl.BlockSpec(memory_space=pl.ANY)] * len(after),
+        out_specs=pl.BlockSpec((1, rows, lane), lambda i: (i, 0, 0)),
+        cost_estimate=pl.CostEstimate(flops=3 * 10**10, bytes_accessed=10**8, transcendentals=0),
+        compiler_params=pltpu.CompilerParams(vmem_limit_bytes=60 * 1024 * 1024),
+    )(*terms, *after).reshape(*(2,) * (left - 1), rows, lane)
+
+
+def add_terms(refs):
+    total = refs[0][0].astype(F32)
+    for ref in refs[1:]:
+        total = total + ref[0].astype(F32)
+    return total
+
+
+def finish_up(pieces, me_ref, *refs):
+    total = add_terms(refs[:-3])
+    up_ref, misc_ref, half_ref = refs[-3:]
+    half_ref[...] = jnp.full(half_ref.shape, me_ref[1], jnp.int32)
+    rows, lane = misc_ref.shape[0], up_ref.shape[1] // pieces
+    for p in range(pieces):
+        up_ref[:, p * lane : (p + 1) * lane] = total[p * rows : (p + 1) * rows]
+    misc_ref[...] = total[pieces * rows :, : misc_ref.shape[1]].astype(BF16)
+
+
+def finish_rest(pieces, counts, stored, me_ref, misc_ref, far_ref, *refs):
+    terms, at = [], 0
+    for count in counts:
+        terms.append(add_terms(refs[at : at + count]))
+        at += count
+    down, cross, own = terms
+    (
+        down_ref, cross_out_ref, query_ref, kv_ref, qkv_ref, out_ref, vision_ref, text_ref, gain_ref, bias_ref,
+    ) = refs[at:]
+    rows, lane = query_ref.shape
+    for p in range(pieces):
+        down_ref[:, p * lane : (p + 1) * lane] = down[p * rows : (p + 1) * rows]
+    cross_out_ref[...] = cross[:rows]
+    query_ref[...] = cross[rows : 2 * rows]
+    for j in range(2):
+        at = 2 * rows + j * stored
+        kv_ref[j] = cross[at : at + kv_ref.shape[1]]
+    for j in range(3):
+        qkv_ref[j] = own[j * rows : (j + 1) * rows]
+    out_ref[...] = own[3 * rows : 4 * rows]
+    norms = jnp.concatenate([own[4 * rows : 5 * rows, :128], jnp.zeros((128 - rows, 128), F32)], axis=0).T
+    gain_ref[...] = norms[0:3, :rows]
+    bias_ref[...] = norms[3:6, :rows]
+    half = misc_ref.shape[1] // 2
+    near, far = misc_ref[...].astype(F32), far_ref[...].astype(F32)
+    first = jnp.full(near.shape, me_ref[1], jnp.int32) == 0
+    low, high = jnp.where(first, near, far), jnp.where(first, far, near)
+    vision_ref[:, :half] = low[:, :half]
+    vision_ref[:, half:] = high[:, :half]
+    text_ref[:, :half] = low[:, half:]
+    text_ref[:, half:] = high[:, half:]
 
 
 def contrast_plain(all_image, all_text, all_pairs, image_raw, text_raw, first_image):
@@ -693,93 +794,174 @@
         grad_i = jnp.pad(grad_i, ((0, emb_rows - items), (0, 0)))
         grad_t = jnp.pad(grad_t, ((0, emb_rows - text_n), (0, 0)))
 
-    place = jnp.zeros((3,), jnp.int32)
+    place = jnp.stack([me, me_m, me_d])
     stored = -(-rows_kv // 16) * 16 if in_chunks else vis_width
     rk = rows_kv if in_chunks else vis_width
-    grad_two, norm_c, gw_ffn = run(
-        ffn_backward,
-        [((tokens_n, width), F32), ((2, width), F32), ((n_mp, nc, (1 + 2 * pieces) * rc, lane), BF16)],
-        ffn_scratch,
+    swap = [(i, i ^ 1) for i in range(n_mp)]
+
+    def shared(rows_n):
+        if fast:
+            return [((2, 2, 2, 2, rows_n, lane), BF16)] * 2
+        return [((n_mp, 1, rows_n, lane), BF16)]
+
+    def along_dp(value, step):
+        return lax.ppermute(value, "dp", [(i, i ^ step) for i in range(n_dp)])
+
+    class Sum:
+        def __init__(self, order, arrays):
+            self.order = order
+            if fast:
+                keep, send = arrays
+                self.terms = [keep, along_dp(send, 1)]
+
+        def step(self, after):
+            axis, self.order = self.order[0], self.order[1:]
+            sent = combine(self.terms, after)
+            if axis == "y":
+                self.terms.append(lax.ppermute(sent, "mp", swap))
+            else:
+                self.terms.append(along_dp(sent, {"x": 2, "v": 4, "u": 8}[axis]))
+            return [sent]
+
+        def parts(self):
+            return [("f", t.reshape(-1, *t.shape[-2:])) for t in self.terms]
+
+    order_up, order_down, order_cross, order_self = "xvyu", "vxyu", "xvyu", "vxyu"
+    grad_two, norm_c, *out_ffn = run(
+        functools.partial(ffn_backward, (order_down, order_up)),
+        [((tokens_n, width), F32), ((2, width), F32)] + shared(pieces * rc) + shared((pieces + 1) * rc),
+        ffn_scratch + [vm(width, tile, dtype=F32)],
         ("s", lengths), ("s", place), ("v", grad_i), ("v", grad_t), ("v", block), ("v", cls_rows), ("v", cotangent),
         ("v", normed_two), ("v", resid_three), ("v", up_value), ("v", act), ("v", norms), ("a", w),
     )
-    grad_one, norm_b, grad_kv, grad_feats, gw_cross = run(
-        functools.partial(cross_backward, vis_len, rc),
+    half_ffn = len(out_ffn) // 2
+    out_down, out_up = out_ffn[:half_ffn], out_ffn[half_ffn:]
+    sum_down, sum_up = Sum(order_down, out_down), Sum(order_up, out_up)
+    far_block = lax.ppermute(block, "mp", swap)
+    last = [out_up[0]]
+
+    def steps(*sums):
+        nonlocal last
+        if fast:
+            for each in sums:
+                last = each.step(last)
+
+    grad_one, norm_b, grad_kv, grad_cq, branch_two = run(
+        functools.partial(cross_backward, vis_len),
         [
-            ((tokens_n, width), F32), ((2, width), F32), ((2, items * vis_pad, width), BF16),
-            ((items * vis_pad, vis_width), BF16), ((n_mp, nc, 2 * rc, lane), BF16),
+            ((tokens_n, width), F32), ((2, width), F32), ((2, items * vis_pad, width), BF16), ((query_n, width), BF16),
+            ((query_n, width), BF16),
         ],
-        [vm(2, nc, rc, width), vm(query_n, width), sems((2 * n_mp,))],
-        ("s", place), ("v", grad_two), ("v", resid_two), ("v", cross_mixed), ("v", cross_q), ("v", first_query),
-        ("v", kv), ("v", kv_w), ("v", norms), ("a", w),
-    )
-    swap = [(i, i ^ 1) for i in range(n_mp)]
-    grad_feats = grad_feats.reshape(items, vis_pad, vis_width)[:, :vis_len]
+        [vm(2, nc, rc, width), sems((2 * n_mp,))],
+        ("v", grad_two), ("v", resid_two), ("v", cross_q), ("v", kv), ("v", norms), ("a", w), after=last + [far_block],
+    )
+    last = [branch_two]
+    steps(sum_down, sum_up)
+    (grad_feats,) = run(
+        feats_backward, [((items * vis_pad, vis_width), BF16)], [], ("v", grad_kv), ("v", kv_w), after=last
+    )
+    last = [grad_feats]
     far_feats = lax.ppermute(grad_feats, "mp", swap)
-    (gw_kv,) = run(
-        functools.partial(kv_backward, rk, stored),
-        [((n_mp, nc, 2 * stored, lane), BF16)],
-        [],
-        ("s", place), ("v", feats_t), ("v", grad_kv),
-    )
-    grad_hidden, gw_self = run(
-        functools.partial(self_backward, rc),
-        [((tokens_n, width), BF16), ((n_mp, nc, 5 * rc, lane), BF16)],
-        [vm(4, nc, rc, width), vm(tokens_n, width), vm(3, tokens_n, width), sems((4 * n_mp,))],
-        ("s", lengths), ("s", place), ("v", grad_one), ("v", resid_one), ("v", hidden), ("v", mixed), ("v", qkv),
-        ("v", norms), ("v", norm_b), ("v", norm_c), ("a", w),
-    )
-
-    groups = [(gw_self, 5, rows, rows), (gw_cross, 2, rows, rows), (gw_ffn, 1 + 2 * pieces, rows, rows)]
-    groups += [(gw_kv, 2, rows_kv, stored if in_chunks else rows_kv)]
-    if not in_chunks:
-        groups = [
-            (
-                jnp.transpose(g.reshape(n_mp, count, n_dp, size, lane), (0, 2, 1, 3, 4)).reshape(n_mp, n_dp, -1, lane),
-                count, size, size,
-            )
-            for g, count, size, _ in groups
-        ]
-    packed_grad = jnp.concatenate([g for g, *_ in groups], axis=2).reshape(n_mp * n_dp, -1, lane)
-    summed = lax.psum_scatter(packed_grad, ("mp", "dp"), scatter_dimension=0, tiled=False).astype(F32)
-    parts, at = [], 0
-    for _, count, size, kept in groups:
-        for _ in range(count):
-            parts.append(summed[at : at + size])
-            at += kept
-    g_qkv, g_out, g_norm, g_cross_out, g_query = parts[:3], parts[3], parts[4], parts[5], parts[6]
-    g_up, g_down, g_misc = parts[7 : 7 + pieces], parts[7 + pieces : 7 + 2 * pieces], parts[7 + 2 * pieces]
-    g_kv = parts[8 + 2 * pieces :]
-
-    def whole(own, far, axis):
-        first = jnp.where(me_m == 0, own, far)
-        second = jnp.where(me_m == 0, far, own)
-        return jnp.concatenate([first, second], axis=axis)
-
-    def exchanged(value):
-        return whole(value, lax.ppermute(value, "mp", swap), 0)
-
-    small = jnp.concatenate([g_misc[:, : 2 * half_emb], g_norm[:, :128]], axis=1).astype(BF16)
-    far = lax.ppermute(small, "mp", swap)
-    low = jnp.where(me_m == 0, small, far).astype(F32)
-    high = jnp.where(me_m == 0, far, small).astype(F32)
-    norm_share = low[:, 2 * half_emb : 2 * half_emb + 6].T
+    out_cross = run(
+        functools.partial(cross_weights_backward, rc, rk, stored, lane, order_cross),
+        shared(2 * rc + 2 * stored),
+        [vm(vis_width + stored - rk, width, dtype=F32)],
+        ("s", place), ("v", feats_t), ("v", grad_kv), ("v", branch_two), ("v", cross_mixed), ("v", first_query),
+        ("v", grad_cq), after=last,
+    )
+    last = [out_cross[0]]
+    sum_cross = Sum(order_cross, out_cross)
+    steps(sum_down, sum_up)
+    grad_resid_one, norm_a, grad_qkv = run(
+        self_attention_backward,
+        [((tokens_n, width), F32), ((2, width), F32), ((3, tokens_n, width), BF16)],
+        [vm(nc, rc, width), vm(tokens_n, width), sems((n_mp,))],
+        ("s", lengths), ("v", grad_one), ("v", resid_one), ("v", qkv), ("v", norms), ("a", w), after=last,
+    )
+    last = [grad_qkv]
+    steps(sum_cross)
+    grad_hidden, *out_self = run(
+        functools.partial(self_weights_backward, rc, order_self),
+        [((tokens_n, width), BF16)] + shared(5 * rc),
+        [vm(3, nc, rc, width), sems((3 * n_mp,)), vm(width, width, dtype=F32)],
+        ("s", place), ("v", grad_resid_one), ("v", hidden), ("v", mixed), ("v", grad_qkv), ("v", norm_a),
+        ("v", norm_b), ("v", norm_c), ("a", w), after=last,
+    )
+    last = [out_self[0]]
+    sum_self = Sum(order_self, out_self)
+    far_hidden = lax.ppermute(grad_hidden, "mp", swap)
+    steps(sum_down, sum_up, sum_self, sum_down, sum_up, sum_cross, sum_self)
+    groups = [(out_up, pieces + 1, rows), (out_down, pieces, rows), (out_cross, 2, rows), (out_cross, 2, rows_kv)]
+    groups += [(out_self, 5, rows)]
+
+    def whole(own, far, half):
+        return jnp.concatenate([jnp.where(half == 0, own, far), jnp.where(half == 0, far, own)], axis=0)
+
+
+    if fast:
+        up_grad, misc, half_late = run(
+            functools.partial(finish_up, pieces),
+            [((rows, pieces * lane), F32), ((rows, 2 * half_emb), BF16), ((1, 1), jnp.int32)], [],
+            ("s", place), *sum_up.parts(), after=last,
+        )
+        half_late = half_late[0, 0]
+        last = [misc]
+        far_misc = lax.ppermute(misc, "mp", swap)
+        steps(sum_cross, sum_self, sum_cross, sum_self)
+        others = [sum_down, sum_cross, sum_self]
+        down_grad, cross_out_grad, query_grad, kv_grad, qkv_grad, out_grad_t, vision_grad, text_grad, gain, bias = run(
+            functools.partial(finish_rest, pieces, [len(s.terms) for s in others], stored),
+            [
+                ((rows, pieces * lane), F32), ((rows, lane), F32), ((rows, lane), F32), ((2, rows_kv, lane), F32),
+                ((3, rows, lane), F32), ((rows, lane), F32), ((rows, emb), F32), ((rows, emb), F32), ((3, rows), F32),
+                ((3, rows), F32),
+            ],
+            [],
+            ("s", place), ("v", misc), ("v", far_misc), *[p for s in others for p in s.parts()],
+        )
+    else:
+        half_late = me_m
+        shares, at = [], {}
+        for g, count, size in groups:
+            start = at.get(id(g), 0)
+            at[id(g)] = start + count * n_dp * size
+            value = g[0][:, :, start : at[id(g)]].reshape(n_mp, count, n_dp, size, lane)
+            shares.append(jnp.transpose(value, (0, 2, 1, 3, 4)).reshape(n_mp * n_dp, -1, lane))
+        packed_grad = jnp.concatenate(shares, axis=1)
+        got, at = lax.psum_scatter(packed_grad, ("mp", "dp"), scatter_dimension=0, tiled=False).astype(F32), 0
+        parts = []
+        for _, count, size in groups:
+            for _ in range(count):
+                parts.append(got[at : at + size])
+                at += size
+        up_grad = jnp.concatenate(parts[:pieces], axis=1)
+        down_grad = jnp.concatenate(parts[pieces + 1 : 2 * pieces + 1], axis=1)
+        cross_out_grad, query_grad, *kv_grad = parts[2 * pieces + 1 : 2 * pieces + 5]
+        kv_grad, qkv_grad = jnp.stack(kv_grad), jnp.stack(parts[2 * pieces + 5 : 2 * pieces + 8])
+        out_grad_t, norm_grad = parts[2 * pieces + 8][:, :], parts[2 * pieces + 9][:, :6].T
+        gain, bias = norm_grad[:3], norm_grad[3:]
+        misc = parts[pieces][:, : 2 * half_emb].astype(BF16)
+        far = lax.ppermute(misc, "mp", swap)
+        low = jnp.where(me_m == 0, misc, far).astype(F32)
+        high = jnp.where(me_m == 0, far, misc).astype(F32)
+        vision_grad = jnp.concatenate([low[:, :half_emb], high[:, :half_emb]], axis=1)
+        text_grad = jnp.concatenate([low[:, half_emb:], high[:, half_emb:]], axis=1)
     return (
         loss,
-        exchanged(block.reshape(items, seq, width)),
-        exchanged(grad_hidden.reshape(items, seq, width)),
-        whole(grad_feats, far_feats, 0),
-        jnp.stack(g_qkv),
-        g_out.T,
-        g_query,
-        jnp.stack(g_kv),
-        g_cross_out.T,
-        jnp.concatenate(g_up, axis=1),
-        jnp.concatenate(g_down, axis=1).T,
-        jnp.concatenate([low[:, :half_emb], high[:, :half_emb]], axis=1),
-        jnp.concatenate([low[:, half_emb : 2 * half_emb], high[:, half_emb : 2 * half_emb]], axis=1),
-        norm_share[:3],
-        norm_share[3:],
+        whole(block.reshape(items, seq, width), far_block.reshape(items, seq, width), half_late),
+        whole(grad_hidden.reshape(items, seq, width), far_hidden.reshape(items, seq, width), half_late),
+        whole(grad_feats, far_feats, half_late).reshape(-1, vis_pad, vis_width)[:, :vis_len],
+        qkv_grad,
+        out_grad_t.T,
+        query_grad,
+        kv_grad,
+        cross_out_grad.T,
+        up_grad,
+        down_grad.T,
+        vision_grad,
+        text_grad,
+        gain,
+        bias,
     )
 
 

time: 598 us -> 494 us (0.83)
  waiting for transfers between devices: 322 us -> 143 us
  Pallas kernels: 125 us -> 192 us
  starting transfers between devices: 12.9 us -> 34.8 us
  other arithmetic: 27.9 us -> 9.86 us
    reduce_scatter x1 -> x0, waiting for transfers between devices: 129 us -> none  [shards(): lax.psum_scatter(packed_grad, ('mp', 'dp'), scatter_dimension=0, tiled=Fa...]
    pallas_call x8 -> x28, Pallas kernels: 125 us -> 192 us  [the longest x12 137 us: run(): pl.pallas_call(kernel, **grid, out_shape=[jax.ShapeDtypeStruct(shape, dty...]
    ppermute x3 -> x23, waiting for transfers between devices: 92 us -> 42 us  [the longest x16 32.8 us: along_dp(): return lax.ppermute(value, 'dp', [(i, i ^ step) for i in range(n_dp)])]
    ppermute x3 -> x23, starting transfers between devices: 3.5 us -> 25.3 us  [the longest x16 17.8 us: along_dp(): return lax.ppermute(value, 'dp', [(i, i ^ step) for i in range(n_dp)])]
    concatenate x8 -> x3, other arithmetic: 20.3 us -> 4.93 us  [whole(): jnp.concatenate([jnp.where(half == 0, own, far), jnp.where(half == 0, far...]
    unnamed x47 -> x77, local copies, waits for them, and re-layouts: 12.2 us -> 20.5 us
  transfers between devices with their start and end apart: 13 -> 32, of which waited for: 10 -> 12; matrix products, arithmetic and copies ran while one was open for 6% -> 7% of each run, Pallas kernels for 0% -> 31%
where the time goes in v3:
time: 494 us; the launch traced here: 489 us
  Pallas kernels  192 us (39%)
  waiting for transfers between devices  143 us (29%)
  local copies, waits for them, and re-layouts  60.7 us (12%)
  starting transfers between devices  34.8 us (7%)
  blocking collectives  31.7 us (6%)
  between operations  16.4 us (3%)
  other arithmetic  9.86 us (2%)
    pallas_call x12, Pallas kernels, run(): pl.pallas_call(kernel, **grid, out_shape=[jax.ShapeDtypeStruct(shape, dty...  137 us
    all_gather x1, waiting for transfers between devices, shards(): lax.all_gather(packed, ('mp', 'dp'), axis=0, tiled=False)  94.5 us
    pallas_call x16, Pallas kernels, combine(): pl.pallas_call(kernel, grid=(places,), out_shape=jax.ShapeDtypeStruct((pl...  55.3 us
    ppermute x16, waiting for transfers between devices, along_dp(): return lax.ppermute(value, 'dp', [(i, i ^ step) for i in range(n_dp)])  32.8 us
    all_gather x1, blocking collectives, shards(): lax.all_gather(jnp.concatenate([norm_gain, norm_bias], axis=0), 'dp', axi...  23.2 us
    unnamed x77, local copies, waits for them, and re-layouts  20.5 us
    ppermute x16, starting transfers between devices, along_dp(): return lax.ppermute(value, 'dp', [(i, i ^ step) for i in range(n_dp)])  17.8 us
    reshape x1, local copies, waits for them, and re-layouts, shards(): kv_w = jnp.transpose(kv_w, (2, 1, 3, 0, 4)).reshape(2, vis_width, width)  10.4 us
  transfers between devices with their start and end apart: 32, of which 12 were waited for; matrix products, arithmetic and copies ran while one was open for 7% of the time, Pallas kernels for 31%

profile of v3, /device:TPU:0, one launch (start us, length us, event | category | flops | bytes accessed | tf_op | source)
XLA Modules:
  0.0 488.8 jit_solution(12037360131807021489)
XLA Ops:
  15.9 4.1 constant_dynamic-slice_fusion.3
  22.4 5.6 %copy.57 = bf16[1088,1408]{0,1:T(8,128)(2,1)} copy(bf16[1088,1408]{1,0:T(8,128)(2,1)} %bitcast.134) | data formatting | bytes 6127616 | tf_op jit(solution)/shard_map/reshape | solution.py:724
  28.0 23.2 %all-gather.1 = bf16[16,48,6]{1,2,0:T(8,128)(2,1)S(1)} all-gather(bf16[1,48,6]{1,2,0:T(8,128)(2,1)S(1)} %maximum_bitcast_fusion), channel_id=1, replica_groups=mesh['dp'=16,'mp'=2] {'dp'}, dimensions={0}, use_global_device_ids=true | all-gather | bytes 9792 | tf_op jit(solution)/shard_map/all_gather | solution.py:718
  52.8 8.6 %all-reduce.2 = s32[384]{0:T(512)S(1)} all-reduce(s32[384]{0:T(512)S(1)} %dynamic-update-slice), channel_id=1, replica_groups=mesh['dp'=16,'mp'=2] {'dp'}, use_global_device_ids=true, to_apply=%add.2 | all-reduce | flops 384 | bytes 3072
  63.3 94.5 %all-gather.4.cloned.1.call-done = bf16[28672,384]{1,0:T(8,128)(2,1)} async-done(((bf16[896,384]{1,0:T(8,128)(2,1)}), bf16[28672,384]{1,0:T(8,128)(2,1)}) %all-gather.4.cloned.1.call-update) | async-done | bytes 22020112 | tf_op jit(solution)/shard_map/all_gather | solution.py:717
  160.6 6.5 %copy.61 = bf16[2,16,88,2,384]{4,3,2,1,0:T(2,128)(2,1)} copy(bf16[2,16,88,2,384]{4,2,0,1,3:T(8,128)(2,1)S(1)} %bitcast.133) | data formatting | bytes 8650752 | tf_op jit(solution)/shard_map/transpose | solution.py:729
  167.1 10.4 %reshape.345.refs_3_.refs_1_ = bf16[2,1408,768]{2,1,0:T(8,128)(2,1)} reshape(bf16[2,16,88,2,384]{4,3,2,1,0:T(2,128)(2,1)} %copy.61) | data formatting | bytes 8650752 | tf_op jit(solution)/shard_map/reshape | solution.py:729
  177.4 9.1 %shard_map.271 = (bf16[3,256,768]{2,1,0:T(8,128)(2,1)}, bf16[256,768]{1,0:T(8,128)(2,1)}, f32[256,768]{1,0:T(8,128)}, f32[256,768]{1,0:T(8,128)}, bf16[128,768]{1,0:T(8,128)(2,1)}, /*index=5*/bf16[128,768]{1,0:T(8,128)(2,1)}) custom-call(s32[4,3]{1,0:T(4,128)} %copy.67.refs_0_, bf16[256,768]{1,0:T(8,128)(2,1)} %bitcast.153, ...), custom_call_target="tpu_custom_call" | custom-call | flops 30000001024 | bytes 100000000 | tf_op jit(solution)/shard_map/pallas_call | solution.py:559
  186.6 20.4 %shard_map.272 = (bf16[2,1088,768]{2,1,0:T(8,128)(2,1)}, bf16[128,768]{1,0:T(8,128)(2,1)}, f32[128,768]{1,0:T(8,128)}, f32[256,768]{1,0:T(8,128)}) custom-call(f32[256,768]{1,0:T(8,128)} %get-tuple-element.73.refs_0_, bf16[128,768]{1,0:T(8,128)(2,1)} %get-tuple-element.74.refs_1_.refs_2_, bf16[1088,1408]{1,0:T(8,128)(2,1)} %bitcast.135, ...), custom_call_target="tpu_custom_call" | custom-call | flops 30000001024 | bytes 100000000 | tf_op jit(solution)/shard_map/pallas_call | solution.py:559
  207.0 10.1 %shard_map.273 = (f32[4,256,768]{2,1,0:T(8,128)}, bf16[4,256,768]{2,1,0:T(8,128)(2,1)}, f32[256,768]{1,0:T(8,128)}, bf16[256,768]{1,0:T(8,128)(2,1)}, bf16[16,76...) custom-call(s32[4,3]{1,0:T(4,128)} %copy.67.refs_0_, ...), custom_call_target="tpu_custom_call" | custom-call | flops 30000001024 | bytes 100000000 | tf_op jit(solution)/shard_map/pallas_call | solution.py:559
  238.7 16.9 %shard_map.275 = (f32[256,768]{1,0:T(8,128)}, f32[2,768]{1,0:T(2,128)}, bf16[2,2,2,2,192,384]{5,4,3,2,1,0:T(8,128)(2,1)}, bf16[2,2,2,2,192,384]{5,4,3,2,1,0:T(8,...) custom-call(s32[4,3]{1,0:T(4,128)} %copy.67.refs_0_, ...), custom_call_target="tpu_custom_call" | custom-call | flops 30000001024 | bytes 100000000 | tf_op jit(solution)/shard_map/pallas_call | solution.py:559
  257.0 19.0 %shard_map.276 = (f32[256,768]{1,0:T(8,128)}, f32[2,768]{1,0:T(2,128)}, bf16[2,1088,768]{2,1,0:T(8,128)(2,1)}, bf16[128,768]{1,0:T(8,128)(2,1)}, bf16[128,768]{1,0:T(8,128)(2,1)}) custom-call(f32[256,768]{1,0:T(8,128)} %get-tuple-element.93.refs_0_, f32[128,768]{1,0:T(8,128)} %get-tuple-element.94.refs_1_, ...), custom_call_target="tpu_custom_call" | custom-call | flops 30000001024 | bytes 100000000 | tf_op jit(solution)/shard_map/pallas_call | solution.py:559
  276.0 5.7 %shard_map.277 = bf16[8,192,384]{2,1,0:T(8,128)(2,1)} custom-call(bf16[1,2,8,192,384]{4,3,2,1,0:T(8,128)(2,1)} %bitcast.230, bf16[1,2,8,192,384]{4,3,2,1,0:T(8,128)(2,1)} %bitcast.29.refs_1_, bf16[128,768]{1,0:T(8,128)(2,1)} %get-tuple-element.96.refs_2_.refs_3_), custom_call_target="tpu_custom_call" | custom-call | flops 30000001024 | bytes 100000000 | tf_op jit(solution)/shard_map/pallas_call | solution.py:583
  283.3 5.9 %shard_map.278 = bf16[8,240,384]{2,1,0:T(8,128)(2,1)} custom-call(bf16[1,2,8,240,384]{4,3,2,1,0:T(8,128)(2,1)} %bitcast.225, bf16[1,2,8,240,384]{4,3,2,1,0:T(8,128)(2,1)} %bitcast.165, bf16[2,2,2,192,384]{4,3,2,1,0:T(8,128)(2,1)} %bitcast.183), custom_call_target="tpu_custom_call" | custom-call | flops 30000001024 | bytes 100000000 | tf_op jit(solution)/shard_map/pallas_call | solution.py:583
  289.7 16.3 %shard_map.279.refs_7_ = bf16[1088,1408]{1,0:T(8,128)(2,1)} custom-call(bf16[2,1088,768]{2,1,0:T(8,128)(2,1)} %get-tuple-element.98.refs_0_.refs_2_, bf16[2,1408,768]{2,1,0:T(8,128)(2,1)} %reshape.345.refs_3_.refs_1_, bf16[2,2,2,240,384]{4,3,2,1,0:T(8,128)(2,1)} %bitcast.179), custom_call_target="tpu_custom_call" | custom-call | flops 30000001024 | bytes 100000000 | tf_op jit(solution)/shard_map/pallas_call | solution.py:559
  307.5 13.1 %shard_map.280 = (bf16[2,2,2,2,288,384]{5,4,3,2,1,0:T(8,128)(2,1)}, bf16[2,2,2,2,288,384]{5,4,3,2,1,0:T(8,128)(2,1)}) custom-call(s32[3]{0:T(128)} %pad_add_fusion.refs_1_.refs_0_, bf16[1408,1088]{1,0:T(8,128)(2,1)} %bitcast.136, bf16[2,1088,768]{2,1,0:T(8,128)(2,1)} %get-tuple-element.98.refs_0_.refs_2_, ...), custom_call_target="tpu_custom_call" | custom-call | flops 30000001024 | bytes 100000000 | tf_op jit(solution)/shard_map/pallas_call | solution.py:559
  331.5 15.7 %shard_map.283 = (f32[256,768]{1,0:T(8,128)}, f32[2,768]{1,0:T(2,128)}, bf16[3,256,768]{2,1,0:T(8,128)(2,1)}) custom-call(s32[4,3]{1,0:T(4,128)} %copy.67.refs_0_, f32[256,768]{1,0:T(8,128)} %get-tuple-element.103.refs_1_, f32[256,768]{1,0:T(8,128)} %get-tuple-element.104.refs_2_, bf16[3,256,768]{2,1,0:T(8,128)(2,1)} %get-tuple-element.105.refs_3_, ...), custom_call_target="tpu_custom_call" | custom-call | flops 30000001024 | bytes 100000000 | tf_op jit(solution)/shard_map/pallas_call | solution.py:559
  347.3 6.1 %shard_map.284 = bf16[8,288,384]{2,1,0:T(8,128)(2,1)} custom-call(bf16[1,2,8,288,384]{4,3,2,1,0:T(8,128)(2,1)} %bitcast.215, bf16[1,2,8,288,384]{4,3,2,1,0:T(8,128)(2,1)} %bitcast.49.refs_1_, bf16[3,256,768]{2,1,0:T(8,128)(2,1)} %get-tuple-element.108.refs_2_.refs_4_), custom_call_target="tpu_custom_call" | custom-call | flops 30000001024 | bytes 100000000 | tf_op jit(solution)/shard_map/pallas_call | solution.py:583
  354.8 8.1 %shard_map.285 = (bf16[256,768]{1,0:T(8,128)(2,1)}, bf16[2,2,2,2,240,384]{5,4,3,2,1,0:T(8,128)(2,1)}, bf16[2,2,2,2,240,384]{5,4,3,2,1,0:T(8,128)(2,1)}) custom-call(s32[3]{0:T(128)} %pad_add_fusion.refs_1_.refs_0_, f32[256,768]{1,0:T(8,128)} %get-tuple-element.106.refs_1_, bf16[256,768]{1,0:T(8,128)(2,1)} %bitcast.154, ...), custom_call_target="tpu_custom_call" | custom-call | flops 30000001024 | bytes 100000000 | tf_op jit(solution)/shard_map/pallas_call | solution.py:559
  371.9 5.9 %shard_map.288 = bf16[8,240,384]{2,1,0:T(8,128)(2,1)} custom-call(bf16[1,2,8,240,384]{4,3,2,1,0:T(8,128)(2,1)} %bitcast.220, bf16[1,2,8,240,384]{4,3,2,1,0:T(8,128)(2,1)} %bitcast.160, bf16[2,240,384]{2,1,0:T(8,128)(2,1)} %shard_map.287.refs_2_), custom_call_target="tpu_custom_call" | custom-call | flops 30000001024 | bytes 100000000 | tf_op jit(solution)/shard_map/pallas_call | solution.py:583
  377.8 4.0 collective-permute-done.16.refs_7_
  385.7 3.9 collective-permute-done.15.refs_5_
  399.3 22.2 %collective-permute-done.19.refs_2_ = bf16[2,2,2,240,384]{4,3,2,1,0:T(8,128)(2,1)S(1)} collective-permute-done((bf16[2,2,2,240,384]{4,3,2,1,0:T(8,128)(2,1)}, bf16[2,2,2,240,384]{4,3,2,1,0:T(8,128)(2,1)S(1)}, u32[]{:S(2)}, u32[]{:S(2)}) %collective-permute-start.19) | collective-permute-done | bytes 1474592 | tf_op jit(solution)/shard_map/ppermute | solution.py:808
  429.8 10.6 %collective-permute-done.25 = bf16[2,2,288,384]{3,2,1,0:T(8,128)(2,1)S(1)} collective-permute-done((bf16[2,2,288,384]{3,2,1,0:T(8,128)(2,1)}, bf16[2,2,288,384]{3,2,1,0:T(8,128)(2,1)S(1)}, u32[]{:S(2)}, u32[]{:S(2)}) %collective-permute-start.25) | collective-permute-done | bytes 884768 | tf_op jit(solution)/shard_map/ppermute | solution.py:808
  (180 shorter events, 126.8 us)
Async XLA Ops:
  7.2 150.7 %all-gather.4.cloned.1.call-start = ((), (), s32[]{:S(2)}) async-start(), calls=%async_computation | async-start | bytes 22708224 | tf_op jit(solution)/shard_map/all_gather | solution.py:717
  233.8 22.4 %collective-permute-start.9 = (bf16[256,768]{1,0:T(8,128)(2,1)}, bf16[256,768]{1,0:T(8,128)(2,1)S(1)}, u32[]{:S(2)}, u32[]{:S(2)}) collective-permute-start(bf16[256,768]{1,0:T(8,128)(2,1)} %get-tuple-element.84.refs_4_), channel_id=1, source_target_pairs={{0,1},{1,0},{2,3},{3,2},{4,5},{5,4},{6,7},{7,6},{8,9},{9,8},{10,11... | collective-permute-start | bytes 1179656 | tf_op jit(solution)/shard_map/ppermute | solution.py:840
  255.7 26.0 %collective-permute-start.7 = (bf16[2,2,2,2,240,384]{5,4,3,2,1,0:T(8,128)(2,1)}, bf16[2,2,2,2,240,384]{5,4,3,2,1,0:T(8,128)(2,1)S(1)}, u32[]{:S(2)}, u32[]{:S(2)}) collective-permute-start(bf16[2,2,2,2,240,384]{5,4,3,2,1,0:T(8,128)(2,1)} %get-tuple-element.90), channel_id=1, source_target_pairs={{0,2},{2,0},{4,6},{6,4},{8,10},{10,8},{12,14},{14,12},{16,18},{18,... | collective-permute-start | bytes 8847368 | tf_op jit(solution)/shard_map/ppermute | solution.py:808
  256.0 20.0 %collective-permute-start.8 = (bf16[2,2,2,2,192,384]{5,4,3,2,1,0:T(8,128)(2,1)}, bf16[2,2,2,2,192,384]{5,4,3,2,1,0:T(8,128)(2,1)}, u32[]{:S(2)}, u32[]{:S(2)}) collective-permute-start(bf16[2,2,2,2,192,384]{5,4,3,2,1,0:T(8,128)(2,1)} %get-tuple-element.92), channel_id=1, source_target_pairs={{0,2},{2,0},{4,6},{6,4},{8,10},{10,8},{12,14},{14,12},{16,18},{18,... | collective-permute-start | bytes 7077896 | tf_op jit(solution)/shard_map/ppermute | solution.py:808
  281.7 38.9 %collective-permute-start.11 = (bf16[2,2,2,192,384]{4,3,2,1,0:T(8,128)(2,1)}, bf16[2,2,2,192,384]{4,3,2,1,0:T(8,128)(2,1)}, u32[]{:S(2)}, u32[]{:S(2)}) collective-permute-start(bf16[2,2,2,192,384]{4,3,2,1,0:T(8,128)(2,1)} %bitcast.182), channel_id=1, source_target_pairs={{0,8},{2,10},{4,12},{6,14},{8,0},{10,2},{12,4},{14,6},{16,24},{18,... | collective-permute-start | bytes 3538952 | tf_op jit(solution)/shard_map/ppermute | solution.py:808
  289.1 35.6 %collective-permute-start.10 = (bf16[2,2,2,240,384]{4,3,2,1,0:T(8,128)(2,1)}, bf16[2,2,2,240,384]{4,3,2,1,0:T(8,128)(2,1)S(1)}, u32[]{:S(2)}, u32[]{:S(2)}) collective-permute-start(bf16[2,2,2,240,384]{4,3,2,1,0:T(8,128)(2,1)} %bitcast.178), channel_id=1, source_target_pairs={{0,4},{2,6},{4,0},{6,2},{8,12},{10,14},{12,8},{14,10},{16,20},{18,... | collective-permute-start | bytes 4423688 | tf_op jit(solution)/shard_map/ppermute | solution.py:808
  306.0 141.4 %collective-permute-start.22 = (bf16[1088,1408]{1,0:T(8,128)(2,1)}, bf16[1088,1408]{1,0:T(8,128)(2,1)}, u32[]{:S(2)}, u32[]{:S(2)}) collective-permute-start(bf16[1088,1408]{1,0:T(8,128)(2,1)} %shard_map.279.refs_7_), channel_id=1, source_target_pairs={{0,1},{1,0},{2,3},{3,2},{4,5},{5,4},{6,7},{7,6},{8,9},{9,8},{10,11... | collective-permute-start | bytes 9191432 | tf_op jit(solution)/shard_map/ppermute | solution.py:864
  320.6 26.7 %collective-permute-start.14 = (bf16[2,2,2,2,288,384]{5,4,3,2,1,0:T(8,128)(2,1)}, bf16[2,2,2,2,288,384]{5,4,3,2,1,0:T(8,128)(2,1)}, u32[]{:S(2)}, u32[]{:S(2)}) collective-permute-start(bf16[2,2,2,2,288,384]{5,4,3,2,1,0:T(8,128)(2,1)} %get-tuple-element.112), channel_id=1, source_target_pairs={{0,2},{2,0},{4,6},{6,4},{8,10},{10,8},{12,14},{14,12},{16,18},{18,... | collective-permute-start | bytes 10616840 | tf_op jit(solution)/shard_map/ppermute | solution.py:808
  324.2 38.9 %collective-permute-start.13 = (bf16[2,2,192,384]{3,2,1,0:T(8,128)(2,1)}, bf16[2,2,192,384]{3,2,1,0:T(8,128)(2,1)}, u32[]{:S(2)}, u32[]{:S(2)}) collective-permute-start(bf16[2,2,192,384]{3,2,1,0:T(8,128)(2,1)} %bitcast.199), channel_id=1, source_target_pairs={{0,4},{2,6},{4,0},{6,2},{8,12},{10,14},{12,8},{14,10},{16,20},{18,... | collective-permute-start | bytes 1769480 | tf_op jit(solution)/shard_map/ppermute | solution.py:808
  329.5 36.2 %collective-permute-start.12 = (bf16[2,2,240,384]{3,2,1,0:T(8,128)(2,1)}, bf16[2,2,240,384]{3,2,1,0:T(8,128)(2,1)S(1)}, u32[]{:S(2)}, u32[]{:S(2)}) collective-permute-start(bf16[2,2,240,384]{3,2,1,0:T(8,128)(2,1)} %bitcast.197), channel_id=1, source_target_pairs={{0,8},{2,10},{4,12},{6,14},{8,0},{10,2},{12,4},{14,6},{16,24},{18,... | collective-permute-start | bytes 2211848 | tf_op jit(solution)/shard_map/ppermute | solution.py:808
  353.4 41.3 %collective-permute-start.20 = (bf16[2,2,2,288,384]{4,3,2,1,0:T(8,128)(2,1)}, bf16[2,2,2,288,384]{4,3,2,1,0:T(8,128)(2,1)}, u32[]{:S(2)}, u32[]{:S(2)}) collective-permute-start(bf16[2,2,2,288,384]{4,3,2,1,0:T(8,128)(2,1)} %bitcast.170), channel_id=1, source_target_pairs={{0,4},{2,6},{4,0},{6,2},{8,12},{10,14},{12,8},{14,10},{16,20},{18,... | collective-permute-start | bytes 5308424 | tf_op jit(solution)/shard_map/ppermute | solution.py:808
  365.1 16.6 %collective-permute-start.16 = (bf16[2,192,384]{2,1,0:T(8,128)(2,1)}, bf16[2,192,384]{2,1,0:T(8,128)(2,1)S(1)}, u32[]{:S(2)}, u32[]{:S(2)}) collective-permute-start(bf16[2,192,384]{2,1,0:T(8,128)(2,1)} %shard_map.286.refs_4_), channel_id=1, source_target_pairs={{0,1},{1,0},{2,3},{3,2},{4,5},{5,4},{6,7},{7,6},{8,9},{9,8},{10,11... | collective-permute-start | bytes 884744 | tf_op jit(solution)/shard_map/ppermute | solution.py:821
  368.7 20.9 %collective-permute-start.15 = (bf16[2,240,384]{2,1,0:T(8,128)(2,1)}, bf16[2,240,384]{2,1,0:T(8,128)(2,1)S(1)}, u32[]{:S(2)}, u32[]{:S(2)}) collective-permute-start(bf16[2,240,384]{2,1,0:T(8,128)(2,1)} %shard_map.287.refs_2_), channel_id=1, source_target_pairs={{0,1},{1,0},{2,3},{3,2},{4,5},{5,4},{6,7},{7,6},{8,9},{9,8},{10,11... | collective-permute-start | bytes 1105928 | tf_op jit(solution)/shard_map/ppermute | solution.py:821
  370.2 74.9 %collective-permute-start.21 = (bf16[256,768]{1,0:T(8,128)(2,1)}, bf16[256,768]{1,0:T(8,128)(2,1)}, u32[]{:S(2)}, u32[]{:S(2)}) collective-permute-start(bf16[256,768]{1,0:T(8,128)(2,1)} %get-tuple-element.116), channel_id=1, source_target_pairs={{0,1},{1,0},{2,3},{3,2},{4,5},{5,4},{6,7},{7,6},{8,9},{9,8},{10,11... | collective-permute-start | bytes 1179656 | tf_op jit(solution)/shard_map/ppermute | solution.py:892
  381.7 39.7 %collective-permute-start.19 = (bf16[2,2,2,240,384]{4,3,2,1,0:T(8,128)(2,1)}, bf16[2,2,2,240,384]{4,3,2,1,0:T(8,128)(2,1)S(1)}, u32[]{:S(2)}, u32[]{:S(2)}) collective-permute-start(bf16[2,2,2,240,384]{4,3,2,1,0:T(8,128)(2,1)} %bitcast.180), channel_id=1, source_target_pairs={{0,8},{2,10},{4,12},{6,14},{8,0},{10,2},{12,4},{14,6},{16,24},{18,... | collective-permute-start | bytes 4423688 | tf_op jit(solution)/shard_map/ppermute | solution.py:808
  389.6 87.8 %collective-permute-start.24 = (bf16[192,384]{1,0:T(8,128)(2,1)}, bf16[192,384]{1,0:T(8,128)(2,1)}, u32[]{:S(2)}, u32[]{:S(2)}) collective-permute-start(bf16[192,384]{1,0:T(8,128)(2,1)} %bitcast.213), channel_id=1, source_target_pairs={{0,16},{2,18},{4,20},{6,22},{8,24},{10,26},{12,28},{14,30},{16,0},... | collective-permute-start | bytes 442376 | tf_op jit(solution)/shard_map/ppermute | solution.py:808
  394.7 31.5 %collective-permute-start.18 = (bf16[240,384]{1,0:T(8,128)(2,1)}, bf16[240,384]{1,0:T(8,128)(2,1)S(1)}, u32[]{:S(2)}, u32[]{:S(2)}) collective-permute-start(bf16[240,384]{1,0:T(8,128)(2,1)} %bitcast.211), channel_id=1, source_target_pairs={{0,16},{2,18},{4,20},{6,22},{8,24},{10,26},{12,28},{14,30},{16,0},... | collective-permute-start | bytes 552968 | tf_op jit(solution)/shard_map/ppermute | solution.py:808
  421.4 19.0 %collective-permute-start.25 = (bf16[2,2,288,384]{3,2,1,0:T(8,128)(2,1)}, bf16[2,2,288,384]{3,2,1,0:T(8,128)(2,1)S(1)}, u32[]{:S(2)}, u32[]{:S(2)}) collective-permute-start(bf16[2,2,288,384]{3,2,1,0:T(8,128)(2,1)} %bitcast.187), channel_id=1, source_target_pairs={{0,8},{2,10},{4,12},{6,14},{8,0},{10,2},{12,4},{14,6},{16,24},{18,... | collective-permute-start | bytes 2654216 | tf_op jit(solution)/shard_map/ppermute | solution.py:808
  426.2 26.6 %collective-permute-start.27 = (bf16[2,2,240,384]{3,2,1,0:T(8,128)(2,1)}, bf16[2,2,240,384]{3,2,1,0:T(8,128)(2,1)S(1)}, u32[]{:S(2)}, u32[]{:S(2)}) collective-permute-start(bf16[2,2,240,384]{3,2,1,0:T(8,128)(2,1)} %bitcast.195), channel_id=1, source_target_pairs={{0,4},{2,6},{4,0},{6,2},{8,12},{10,14},{12,8},{14,10},{16,20},{18,... | collective-permute-start | bytes 2211848 | tf_op jit(solution)/shard_map/ppermute | solution.py:808
  440.4 37.1 %collective-permute-start.23 = (bf16[48,256]{1,0:T(8,128)(2,1)}, bf16[48,256]{1,0:T(8,128)(2,1)S(1)}, u32[]{:S(2)}, u32[]{:S(2)}) collective-permute-start(bf16[48,256]{1,0:T(8,128)(2,1)} %get-tuple-element.117.refs_4_.refs_1_), channel_id=1, source_target_pairs={{0,1},{1,0},{2,3},{3,2},{4,5},{5,4},{6,7},{7,6},{8,9},{9,8},{10,11... | collective-permute-start | bytes 73736 | tf_op jit(solution)/shard_map/ppermute | solution.py:909
  445.1 11.8 %collective-permute-start.26 = (bf16[2,288,384]{2,1,0:T(8,128)(2,1)}, bf16[2,288,384]{2,1,0:T(8,128)(2,1)S(1)}, u32[]{:S(2)}, u32[]{:S(2)}) collective-permute-start(bf16[2,288,384]{2,1,0:T(8,128)(2,1)} %shard_map.294.refs_4_), channel_id=1, source_target_pairs={{0,1},{1,0},{2,3},{3,2},{4,5},{5,4},{6,7},{7,6},{8,9},{9,8},{10,11... | collective-permute-start | bytes 1327112 | tf_op jit(solution)/shard_map/ppermute | solution.py:821
  455.9 7.7 %collective-permute-start.29 = (bf16[2,240,384]{2,1,0:T(8,128)(2,1)}, bf16[2,240,384]{2,1,0:T(8,128)(2,1)S(1)}, u32[]{:S(2)}, u32[]{:S(2)}) collective-permute-start(bf16[2,240,384]{2,1,0:T(8,128)(2,1)} %shard_map.295.refs_5_), channel_id=1, source_target_pairs={{0,1},{1,0},{2,3},{3,2},{4,5},{5,4},{6,7},{7,6},{8,9},{9,8},{10,11... | collective-permute-start | bytes 1105928 | tf_op jit(solution)/shard_map/ppermute | solution.py:821
  459.9 17.6 %collective-permute-start.28 = (bf16[288,384]{1,0:T(8,128)(2,1)}, bf16[288,384]{1,0:T(8,128)(2,1)S(1)}, u32[]{:S(2)}, u32[]{:S(2)}) collective-permute-start(bf16[288,384]{1,0:T(8,128)(2,1)} %bitcast.206), channel_id=1, source_target_pairs={{0,16},{2,18},{4,20},{6,22},{8,24},{10,26},{12,28},{14,30},{16,0},... | collective-permute-start | bytes 663560 | tf_op jit(solution)/shard_map/ppermute | solution.py:808
  466.4 11.2 %collective-permute-start.30 = (bf16[240,384]{1,0:T(8,128)(2,1)}, bf16[240,384]{1,0:T(8,128)(2,1)S(1)}, u32[]{:S(2)}, u32[]{:S(2)}) collective-permute-start(bf16[240,384]{1,0:T(8,128)(2,1)} %bitcast.210), channel_id=1, source_target_pairs={{0,16},{2,18},{4,20},{6,22},{8,24},{10,26},{12,28},{14,30},{16,0},... | collective-permute-start | bytes 552968 | tf_op jit(solution)/shard_map/ppermute | solution.py:808
  (37 other events, 232.1 us)
Sparse Core Ops, SparseCore 0:
  15.3 142.5 all-gather.3
